TPU v7x, 32 devices: a whole 2x2x4 slice. The times are simulated.
32 devices in a mesh: dp: 8 (over z, y), mp: 4 (over x, core).
Axes of the slice: x: 2, y: 2, z: 4, core: 2. Of those that a mesh axis runs over, the one named last changes fastest.
Arguments:
- tokens: bfloat16 [16384, 1024], P('dp', 'mp'), may hold values from -6 to 6
- gain_one: float32 [1024], replicated, may hold values from 0.5 to 1.5
- gain_two: float32 [1024], replicated, may hold values from 0.5 to 1.5
- w_in: bfloat16 [1024, 1024], P(None, 'mp'), may hold values from -0.1875 to 0.1875
- w_query: bfloat16 [1024, 1024], P(None, 'mp'), may hold values from -0.1875 to 0.1875
- w_out: bfloat16 [1024, 1024], P('mp'), may hold values from -3 to 3
- w_up: bfloat16 [1024, 4096], P(None, 'mp'), may hold values from -0.1875 to 0.1875
- w_down: bfloat16 [4096, 1024], P('mp'), may hold values from -0.09375 to 0.09375
- decay_rate: float32 [1024, 16], P('mp'), may hold values from 4.8828124e-06 to 0.03
- b_in: float32 [1024, 16], P('mp'), may hold values from -4 to 4
- c_key: float32 [1024, 16], P('mp'), may hold values from -3 to 3
- c_val: float32 [1024, 16], P('mp'), may hold values from -3 to 3
- short_lengths: int32 [8, 2], P('dp'), may hold values from 1 to 1024, 1536 in all within a row
- cotangent: bfloat16 [16384, 1024], P('dp', 'mp'), may hold values from -6 to 6
Outputs:
- result: bfloat16 [16384, 1024], P('dp', 'mp')
- grad_tokens: bfloat16 [16384, 1024], P('dp', 'mp')
- grad_gain_one: float32 [1024], replicated
- grad_gain_two: float32 [1024], replicated
- grad_w_in: float32 [1024, 1024], P(None, 'mp')
- grad_w_query: float32 [1024, 1024], P(None, 'mp')
- grad_w_out: float32 [1024, 1024], P('mp')
- grad_w_up: float32 [1024, 4096], P(None, 'mp')
- grad_w_down: float32 [4096, 1024], P('mp')
- grad_decay_rate: float32 [1024, 16], P('mp')
- grad_b_in: float32 [1024, 16], P('mp')
- grad_c_key: float32 [1024, 16], P('mp')
- grad_c_val: float32 [1024, 16], P('mp')
Inputs may be any that keep to these rules, and one draw needn't show every extreme that they name: `short_lengths`: each device's short documents fill its last 1536 rows in order.
All inputs are finite; a program needn't handle non-finite values.
Results may differ from a plain program's by a relative error of at most 0.02.
Values may be sent and summed in bfloat16 or wider, within the bound.
A program may use at most 256 MiB of HBM per device.

v0:
```python
from functools import partial

import jax
import jax.numpy as jnp
from jax import lax
from jax.sharding import PartitionSpec as P

HEAD = 128
BLOCK = 512
CTX = 128
SCAN_BLOCK = 32
LONG_DEV = 512


EPS = 1e-05
HIGH = lax.Precision.HIGHEST


def from_behind(value, axis, steps):
    count = lax.axis_size(axis)
    initial, last = (max(0, -steps), min(count, count - steps))
    return lax.ppermute(value, axis, [(source, source + steps) for source in range(initial, last)])


def gather_features(values_in):
    return lax.all_gather(values_in, "mp", axis=1, tiled=True)


def reduce_features(values_in):
    return lax.psum_scatter(
        values_in.astype(jnp.bfloat16), "mp", scatter_dimension=1, tiled=True
    ).astype(jnp.float32)


def norm_forward(values_in, gain_vec):
    row_mean = jnp.mean(values_in, axis=1, keepdims=True)
    centred = values_in - row_mean
    row_var = jnp.mean(centred * centred, axis=1, keepdims=True)
    inverse = lax.rsqrt(row_var + EPS)
    normed = centred * inverse
    return (normed, inverse, normed * gain_vec)


def norm_backward(upstream, normed, inverse, gain_vec):
    gain_grad = jnp.sum(upstream * normed, axis=0)
    scaled = upstream * gain_vec
    plain_mean = jnp.mean(scaled, axis=1, keepdims=True)
    cross_mean = jnp.mean(scaled * normed, axis=1, keepdims=True)
    return (inverse * (scaled - plain_mean - normed * cross_mean), gain_grad)


def row_layout(lengths, device, row_count):
    positions = jnp.arange(row_count, dtype=jnp.int32)
    doc_ends = jnp.cumsum(lengths)
    shifted = positions - LONG_DEV
    passed = (shifted[:, None] >= doc_ends[None, :]).astype(jnp.int32)
    short_ids = 1 + jnp.sum(passed, axis=1)
    short_places = shifted - jnp.sum(passed * lengths[None, :], axis=1)
    in_long = positions < LONG_DEV
    doc_ids = jnp.where(in_long, 0, short_ids)
    places = jnp.where(in_long, device * LONG_DEV + positions, short_places)
    return (doc_ids, places)


def key_layout(doc_ids, places, device):
    ctx_places = device * LONG_DEV - CTX + jnp.arange(CTX, dtype=jnp.int32)
    key_docs = jnp.concatenate(
        [jnp.full((BLOCK,), -2, jnp.int32), jnp.zeros((CTX,), jnp.int32), doc_ids]
    )
    key_places = jnp.concatenate([jnp.full((BLOCK,), -1, jnp.int32), ctx_places, places])
    return (key_docs, key_places)


def block_mask(row_start, doc_ids, places, key_docs, key_places):
    key_span = 2 * BLOCK + CTX
    query_docs = lax.dynamic_slice_in_dim(doc_ids, row_start, BLOCK, 0)
    query_places = lax.dynamic_slice_in_dim(places, row_start, BLOCK, 0)
    span_docs = lax.dynamic_slice_in_dim(key_docs, row_start, key_span, 0)
    span_places = lax.dynamic_slice_in_dim(key_places, row_start, key_span, 0)
    first_place = query_places // BLOCK * BLOCK - CTX
    same_doc = query_docs[:, None] == span_docs[None, :]
    return (
        same_doc
        & (span_places[None, :] >= 0)
        & (span_places[None, :] >= first_place[:, None])
        & (span_places[None, :] <= query_places[:, None])
    )


def gelu_exact(values_in):
    return jax.nn.gelu(values_in, approximate=False)


def ssm_drive(decay_rate, b_in):
    return jnp.sqrt(-jnp.expm1(-2.0 * decay_rate)) * b_in


def long_state(state_in, ssm_long, decay_rate, drive_gain):
    lag_steps = (LONG_DEV - 1 - jnp.arange(LONG_DEV)).astype(jnp.float32)
    powers = jnp.exp(-decay_rate[None] * lag_steps[:, None, None])
    weighted = jnp.einsum("jcn,jc->cn", powers, ssm_long, precision=HIGH)
    return jnp.exp(-decay_rate * LONG_DEV) * state_in + drive_gain * weighted


def ssm_outputs(ssm_input, doc_ids, state_in, decay_rate, drive_gain, c_key, c_val):
    row_count, local_width = ssm_input.shape
    offsets = jnp.arange(SCAN_BLOCK)
    powers = jnp.exp(-decay_rate[None] * offsets.astype(jnp.float32)[:, None, None])
    lead_powers = powers * jnp.exp(-decay_rate)[None]
    tail_powers = powers[::-1]
    kernels = jnp.stack(
        [
            jnp.einsum("mcn,cn->mc", powers, drive_gain * c_key, precision=HIGH),
            jnp.einsum("mcn,cn->mc", powers, drive_gain * c_val, precision=HIGH),
        ]
    )
    causal = (offsets[:, None] >= offsets[None, :]).astype(jnp.float32)
    toeplitz = (
        kernels[:, jnp.maximum(offsets[:, None] - offsets[None, :], 0)] * causal[None, :, :, None]
    )
    readout = jnp.stack([c_key, c_val])
    decay_block = jnp.exp(-decay_rate * SCAN_BLOCK)

    def one_block(carry, inputs):
        ssm_state, last_doc = carry
        block_values, block_docs = inputs
        same_doc = (block_docs[:, None] == block_docs[None, :]).astype(jnp.float32)
        inner_part = jnp.einsum("ktjc,tj,jc->ktc", toeplitz, same_doc, block_values, precision=HIGH)
        keep_start = (block_docs == last_doc).astype(jnp.float32)
        start_part = jnp.einsum(
            "tcn,kcn->ktc", lead_powers, readout * ssm_state[None], precision=HIGH
        )
        outputs = inner_part + keep_start[None, :, None] * start_part
        tail_keep = (block_docs == block_docs[-1]).astype(jnp.float32)
        fresh_part = jnp.einsum(
            "jcn,jc->cn", tail_powers, block_values * tail_keep[:, None], precision=HIGH
        )
        ssm_state = keep_start[-1] * decay_block * ssm_state + drive_gain * fresh_part
        return ((ssm_state, block_docs[-1]), outputs)

    block_count = row_count // SCAN_BLOCK
    _, outputs = lax.scan(
        jax.checkpoint(one_block),
        (state_in, jnp.zeros((), jnp.int32)),
        (
            ssm_input.reshape(block_count, SCAN_BLOCK, local_width),
            doc_ids.reshape(block_count, SCAN_BLOCK),
        ),
    )
    outputs = outputs.transpose(1, 0, 2, 3).reshape(2, row_count, local_width)
    return (outputs[0], outputs[1])


def ssm_all(ssm_input, decay_rate, b_in, c_key, c_val, state_in, doc_ids):
    drive_gain = ssm_drive(decay_rate, b_in)
    keys, values = ssm_outputs(ssm_input, doc_ids, state_in, decay_rate, drive_gain, c_key, c_val)
    return (keys, values, long_state(state_in, ssm_input[:LONG_DEV], decay_rate, drive_gain))


def fold_pieces(pieces, decay_rate, gap_count):
    live_rows = gap_count >= 0
    weights = jnp.exp(
        -decay_rate[None]
        * (LONG_DEV * jnp.maximum(gap_count, 0)).astype(jnp.float32)[:, None, None]
    )
    return jnp.sum(jnp.where(live_rows[:, None, None], weights * pieces, 0.0), axis=0)


def attention_forward(queries, keys_ext, values_ext, doc_ids, places, key_docs, key_places):
    row_count, local_width = queries.shape
    head_count = local_width // HEAD
    key_span = 2 * BLOCK + CTX
    score_scale = HEAD ** (-0.5)

    def one_block(block_index):
        row_start = block_index * BLOCK
        query_block = lax.dynamic_slice_in_dim(queries, row_start, BLOCK, 0).reshape(
            BLOCK, head_count, HEAD
        )
        key_block = lax.dynamic_slice_in_dim(keys_ext, row_start, key_span, 0).reshape(
            key_span, head_count, HEAD
        )
        value_block = lax.dynamic_slice_in_dim(values_ext, row_start, key_span, 0).reshape(
            key_span, head_count, HEAD
        )
        allowed = block_mask(row_start, doc_ids, places, key_docs, key_places)
        scores = (
            jnp.einsum("qhd,khd->hqk", query_block, key_block, preferred_element_type=jnp.float32)
            * score_scale
        )
        scores = jnp.where(allowed[None], scores, -1e30)
        row_top = jnp.max(scores, axis=2, keepdims=True)
        exponents = jnp.exp(scores - row_top)
        row_total = jnp.sum(exponents, axis=2, keepdims=True)
        weights = (exponents / row_total).astype(jnp.bfloat16)
        mixed = jnp.einsum("hqk,khd->qhd", weights, value_block, preferred_element_type=jnp.float32)
        return (mixed.reshape(BLOCK, local_width), (row_top + jnp.log(row_total))[:, :, 0])

    mixed, log_totals = lax.map(one_block, jnp.arange(row_count // BLOCK, dtype=jnp.int32))
    return (mixed.reshape(row_count, local_width), log_totals)


def attention_backward(
    queries, keys_ext, values_ext, grad_attended, log_totals, doc_ids, places, key_docs, key_places
):
    row_count, local_width = queries.shape
    head_count = local_width // HEAD
    key_span = 2 * BLOCK + CTX
    score_scale = HEAD ** (-0.5)

    def one_block(block_index, totals):
        grad_queries, grad_keys, grad_values = totals
        row_start = block_index * BLOCK
        query_block = lax.dynamic_slice_in_dim(queries, row_start, BLOCK, 0).reshape(
            BLOCK, head_count, HEAD
        )
        key_block = lax.dynamic_slice_in_dim(keys_ext, row_start, key_span, 0).reshape(
            key_span, head_count, HEAD
        )
        value_block = lax.dynamic_slice_in_dim(values_ext, row_start, key_span, 0).reshape(
            key_span, head_count, HEAD
        )
        grad_block = lax.dynamic_slice_in_dim(grad_attended, row_start, BLOCK, 0).reshape(
            BLOCK, head_count, HEAD
        )
        allowed = block_mask(row_start, doc_ids, places, key_docs, key_places)
        scores = (
            jnp.einsum("qhd,khd->hqk", query_block, key_block, preferred_element_type=jnp.float32)
            * score_scale
        )
        scores = jnp.where(allowed[None], scores, -1e30)
        probabilities = jnp.exp(scores - log_totals[block_index][:, :, None])
        probs_low = probabilities.astype(jnp.bfloat16)
        grad_probs = jnp.einsum(
            "qhd,khd->hqk", grad_block, value_block, preferred_element_type=jnp.float32
        )
        value_part = jnp.einsum(
            "hqk,qhd->khd", probs_low, grad_block, preferred_element_type=jnp.float32
        )
        row_delta = jnp.sum(probabilities * grad_probs, axis=2, keepdims=True)
        grad_scores = (probabilities * (grad_probs - row_delta)).astype(jnp.bfloat16)
        query_part = (
            jnp.einsum("hqk,khd->qhd", grad_scores, key_block, preferred_element_type=jnp.float32)
            * score_scale
        )
        key_part = (
            jnp.einsum("hqk,qhd->khd", grad_scores, query_block, preferred_element_type=jnp.float32)
            * score_scale
        )
        grad_queries = lax.dynamic_update_slice_in_dim(
            grad_queries, query_part.reshape(BLOCK, local_width), row_start, 0
        )
        grad_keys = lax.dynamic_update_slice_in_dim(
            grad_keys,
            lax.dynamic_slice_in_dim(grad_keys, row_start, key_span, 0)
            + key_part.reshape(key_span, local_width),
            row_start,
            0,
        )
        grad_values = lax.dynamic_update_slice_in_dim(
            grad_values,
            lax.dynamic_slice_in_dim(grad_values, row_start, key_span, 0)
            + value_part.reshape(key_span, local_width),
            row_start,
            0,
        )
        return (grad_queries, grad_keys, grad_values)

    initial = (
        jnp.zeros((row_count, local_width), jnp.float32),
        jnp.zeros(keys_ext.shape, jnp.float32),
        jnp.zeros(values_ext.shape, jnp.float32),
    )
    return lax.fori_loop(0, row_count // BLOCK, one_block, initial)


def on_device(
    tokens,
    gain_one,
    gain_two,
    w_in,
    w_query,
    w_out,
    w_up,
    w_down,
    decay_rate,
    b_in,
    c_key,
    c_val,
    short_lengths,
    cotangent,
):
    row_count = tokens.shape[0]
    local_width = w_in.shape[1]
    device = lax.axis_index("dp")
    doc_ids, places = row_layout(short_lengths[0], device, row_count)
    key_docs, key_places = key_layout(doc_ids, places, device)
    tokens_full = gather_features(tokens).astype(jnp.float32)
    normed_one, inverse_one, hidden_one = norm_forward(tokens_full, gain_one)
    normed_one_low = hidden_one.astype(jnp.bfloat16)
    ssm_input = jnp.dot(normed_one_low, w_in, preferred_element_type=jnp.float32)
    queries = jnp.dot(normed_one_low, w_query, preferred_element_type=jnp.float32).astype(
        jnp.bfloat16
    )
    drive_gain = ssm_drive(decay_rate, b_in)
    local_end = long_state(jnp.zeros_like(decay_rate), ssm_input[:LONG_DEV], decay_rate, drive_gain)
    pieces = lax.all_gather(local_end[None], "dp", axis=0, tiled=True)
    others = jnp.arange(pieces.shape[0], dtype=jnp.int32)
    state_in = fold_pieces(pieces, decay_rate, device - 1 - others)
    (keys_raw, values_raw, _), ssm_pull = jax.vjp(
        partial(ssm_all, doc_ids=doc_ids), ssm_input, decay_rate, b_in, c_key, c_val, state_in
    )
    keys_low = keys_raw.astype(jnp.bfloat16)
    values_low = values_raw.astype(jnp.bfloat16)
    ctx_keys, ctx_values = from_behind(
        (keys_low[LONG_DEV - CTX : LONG_DEV], values_low[LONG_DEV - CTX : LONG_DEV]), "dp", 1
    )
    padding = jnp.zeros((BLOCK, local_width), jnp.bfloat16)
    keys_ext = jnp.concatenate([padding, ctx_keys, keys_low])
    values_ext = jnp.concatenate([padding, ctx_values, values_low])
    attended, log_totals = attention_forward(
        queries, keys_ext, values_ext, doc_ids, places, key_docs, key_places
    )
    attended_low = attended.astype(jnp.bfloat16)
    middle = tokens.astype(jnp.float32) + reduce_features(
        jnp.dot(attended_low, w_out, preferred_element_type=jnp.float32)
    )
    middle_full = gather_features(middle.astype(jnp.bfloat16)).astype(jnp.float32)
    normed_two, inverse_two, hidden_two = norm_forward(middle_full, gain_two)
    normed_two_low = hidden_two.astype(jnp.bfloat16)
    pre_act = jnp.dot(normed_two_low, w_up, preferred_element_type=jnp.float32)
    act_value, act_pull = jax.vjp(gelu_exact, pre_act)
    act_low = act_value.astype(jnp.bfloat16)
    result = (
        middle + reduce_features(jnp.dot(act_low, w_down, preferred_element_type=jnp.float32))
    ).astype(jnp.bfloat16)
    cotangent_full = gather_features(cotangent)
    grad_w_down = jnp.einsum(
        "ri,rd->id", act_low, cotangent_full, preferred_element_type=jnp.float32
    )
    grad_act = jnp.einsum("rd,id->ri", cotangent_full, w_down, preferred_element_type=jnp.float32)
    grad_pre = act_pull(grad_act)[0].astype(jnp.bfloat16)
    grad_w_up = jnp.einsum(
        "rd,ri->di", normed_two_low, grad_pre, preferred_element_type=jnp.float32
    )
    grad_hidden_two = jnp.einsum("ri,di->rd", grad_pre, w_up, preferred_element_type=jnp.float32)
    middle_part, grad_gain_two = norm_backward(grad_hidden_two, normed_two, inverse_two, gain_two)
    grad_middle = cotangent.astype(jnp.float32) + reduce_features(middle_part)
    grad_mid_full = gather_features(grad_middle.astype(jnp.bfloat16))
    grad_w_out = jnp.einsum(
        "ri,rd->id", attended_low, grad_mid_full, preferred_element_type=jnp.float32
    )
    grad_attended = jnp.einsum(
        "rd,id->ri", grad_mid_full, w_out, preferred_element_type=jnp.float32
    ).astype(jnp.bfloat16)
    grad_queries, grad_keys_ext, grad_values_ext = attention_backward(
        queries,
        keys_ext,
        values_ext,
        grad_attended,
        log_totals,
        doc_ids,
        places,
        key_docs,
        key_places,
    )
    back_keys, back_values = (
        from_behind(grad_keys_ext[BLOCK : BLOCK + CTX].astype(jnp.bfloat16), "dp", -1).astype(
            jnp.float32
        ),
        from_behind(grad_values_ext[BLOCK : BLOCK + CTX].astype(jnp.bfloat16), "dp", -1).astype(
            jnp.float32
        ),
    )
    grad_keys = grad_keys_ext[BLOCK + CTX :].at[LONG_DEV - CTX : LONG_DEV].add(back_keys)
    grad_values = grad_values_ext[BLOCK + CTX :].at[LONG_DEV - CTX : LONG_DEV].add(back_values)
    lead_long = jnp.exp(
        -decay_rate[None] * (jnp.arange(LONG_DEV) + 1).astype(jnp.float32)[:, None, None]
    )
    local_in = c_key * jnp.einsum("tcn,tc->cn", lead_long, grad_keys[:LONG_DEV], precision=HIGH)
    local_in = local_in + c_val * jnp.einsum(
        "tcn,tc->cn", lead_long, grad_values[:LONG_DEV], precision=HIGH
    )
    grad_pieces = lax.all_gather(local_in[None], "dp", axis=0, tiled=True)
    others_back = jnp.arange(grad_pieces.shape[0], dtype=jnp.int32)
    grad_end = fold_pieces(grad_pieces, decay_rate, others_back - device - 1)
    grad_ssm, grad_rate, grad_b, grad_ck, grad_cv, _ = ssm_pull((grad_keys, grad_values, grad_end))
    grad_ssm_low = grad_ssm.astype(jnp.bfloat16)
    grad_queries_low = grad_queries.astype(jnp.bfloat16)
    grad_w_in = jnp.einsum(
        "rd,ri->di", normed_one_low, grad_ssm_low, preferred_element_type=jnp.float32
    )
    grad_w_query = jnp.einsum(
        "rd,ri->di", normed_one_low, grad_queries_low, preferred_element_type=jnp.float32
    )
    grad_hidden_one = jnp.einsum(
        "ri,di->rd", grad_ssm_low, w_in, preferred_element_type=jnp.float32
    )
    grad_hidden_one = grad_hidden_one + jnp.einsum(
        "ri,di->rd", grad_queries_low, w_query, preferred_element_type=jnp.float32
    )
    token_part, grad_gain_one = norm_backward(grad_hidden_one, normed_one, inverse_one, gain_one)
    grad_tokens = (grad_middle + reduce_features(token_part)).astype(jnp.bfloat16)
    (
        grad_w_in,
        grad_w_query,
        grad_w_out,
        grad_w_up,
        grad_w_down,
        grad_rate,
        grad_b,
        grad_ck,
        grad_cv,
    ) = lax.psum(
        (
            grad_w_in,
            grad_w_query,
            grad_w_out,
            grad_w_up,
            grad_w_down,
            grad_rate,
            grad_b,
            grad_ck,
            grad_cv,
        ),
        "dp",
    )
    grad_gain_one, grad_gain_two = lax.psum((grad_gain_one, grad_gain_two), ("dp", "mp"))
    return (
        result,
        grad_tokens,
        grad_gain_one,
        grad_gain_two,
        grad_w_in,
        grad_w_query,
        grad_w_out,
        grad_w_up,
        grad_w_down,
        grad_rate,
        grad_b,
        grad_ck,
        grad_cv,
    )


def solution(mesh):
    placed = (
        P("dp", "mp"),
        P(),
        P(),
        P(None, "mp"),
        P(None, "mp"),
        P("mp", None),
        P(None, "mp"),
        P("mp", None),
        P("mp", None),
        P("mp", None),
        P("mp", None),
        P("mp", None),
        P("dp", None),
        P("dp", "mp"),
    )
    return jax.shard_map(
        on_device,
        mesh=mesh,
        in_specs=placed,
        out_specs=(
            P("dp", "mp"),
            P("dp", "mp"),
            P(),
            P(),
            P(None, "mp"),
            P(None, "mp"),
            P("mp", None),
            P(None, "mp"),
            P("mp", None),
            P("mp", None),
            P("mp", None),
            P("mp", None),
            P("mp", None),
        ),
        check_vma=False,
    )
```

profile of v0, /device:TPU:0, one launch (start us, length us, event | category | flops | bytes accessed | tf_op | source)
XLA Modules:
  0.0 4905.6 jit_solution(7559663918686179794)
XLA Ops:
  15.8 31.6 all-gather.7.cloned.1.call-done
  60.1 30.6 all-gather
  93.3 8.8 gather_fusion
  105.3 1070.9 %while.85 = (s32[]{:T(128)}, f32[256,16]{1,0:T(8,128)S(1)}, s32[]{:T(128)}, bf16[64,2,32,256]{3,2,0,1:T(8,128)(2,1)}, f32[64,256,16]{2,1,0:T(8,128)}, /*index=5*...) while((s32[]{:T(128)}, f32[256,16]{1,0:T(8,128)S(1)}, ...), condition=%wide.region_6.7_spmd.clone, body=%wide.region_5.6_spmd.clone.sunk | while | flops 5044354 | bytes 16164217 | solution.py:142
  1196.9 52.4 %while.83 = (s32[]{:T(128)}, bf16[4,512,256]{2,1,0:T(8,128)(2,1)}, f32[4,2,512]{2,1,0:T(2,128)}, s32[4]{0:T(128)S(1)}, bf16[2688,256]{0,1:T(8,128)(2,1)}, /*inde...) while((s32[]{:T(128)}, bf16[4,512,256]{2,1,0:T(8,128)(2,1)}, ...), condition=%wide.region_11.12_spmd, body=%wide.region_8.11_spmd.sunk | while | flops 616964736 | bytes 21050896 | solution.py:199
  1254.0 45.1 reduce-scatter.5.cloned.1.call-done
  1302.5 34.6 all-gather.9.cloned.1.call-done
  1341.9 6.8 fusion.115
  1348.7 24.9 all-gather.11.cloned.1.call-done
  1373.6 34.6 add_convert_fusion
  1408.2 7.2 fusion.70
  1419.5 44.6 reduce-scatter.9.cloned.1.call-done
  1468.7 10.6 multiply_convert_fusion.1
  1479.3 22.8 all-gather.13.cloned.1.call-done
  1511.2 168.3 %while.84 = (s32[]{:T(128)}, bf16[2048,256]{0,1:T(8,128)(2,1)}, f32[2688,256]{1,0:T(8,128)}, f32[2688,256]{1,0:T(8,128)}, bf16[2688,256]{0,1:T(8,128)(2,1)S(1)},...) while((s32[]{:T(128)}, bf16[2048,256]{0,1:T(8,128)(2,1)}, ...), condition=%wide.region_21.22_spmd, body=%wide.region_19.21_spmd.sunk | while | flops 1525260928 | bytes 99018720 | solution.py:274
  1681.7 8.3 convolution_convert_fusion.1
  1704.0 2566.2 %while.86 = (s32[]{:T(128)}, f32[2,32,32,256]{3,2,1,0:T(8,128)}, f32[2,256,16]{2,0,1:T(2,128)}, f32[32,256,16]{0,2,1:T(8,128)}, f32[32,256,16]{1,2,0:T(8,128)}, ...) while((s32[]{:T(128)}, f32[2,32,32,256]{3,2,1,0:T(8,128)}, ...), condition=%wide.region_25.26_spmd.clone, body=%wide.region_23.25_spmd.clone.sunk | while | flops 13641860 | bytes 29315576 | solution.py:142
  1754.4 5.7 multiply_reduce_fusion.28
  1794.5 5.7 multiply_reduce_fusion.28
  1874.8 5.7 multiply_reduce_fusion.28
  1914.9 5.7 multiply_reduce_fusion.28
  1955.0 5.7 multiply_reduce_fusion.28
  1995.2 5.7 multiply_reduce_fusion.28
  2035.3 5.7 multiply_reduce_fusion.28
  2075.4 5.7 multiply_reduce_fusion.28
  2155.7 5.7 multiply_reduce_fusion.28
  2276.2 5.7 multiply_reduce_fusion.28
  2316.3 5.7 multiply_reduce_fusion.28
  2356.5 5.7 multiply_reduce_fusion.28
  2396.6 5.7 multiply_reduce_fusion.28
  2476.9 5.7 multiply_reduce_fusion.28
  2557.1 5.7 multiply_reduce_fusion.28
  2717.7 5.7 multiply_reduce_fusion.28
  2798.0 5.7 multiply_reduce_fusion.28
  2838.1 5.7 multiply_reduce_fusion.28
  2918.4 5.7 multiply_reduce_fusion.28
  2958.6 5.7 multiply_reduce_fusion.28
  2998.7 5.7 multiply_reduce_fusion.28
  3038.8 5.7 multiply_reduce_fusion.28
  3119.1 5.7 multiply_reduce_fusion.28
  3159.2 5.7 multiply_reduce_fusion.28
  4276.1 31.8 all-gather.1
  4313.0 72.1 %scatter_fusion = f32[2,32,256]{2,0,1:T(2,128)S(1)} fusion(f32[2,32,256]{2,0,1:T(2,128)S(1)} %broadcast_in_dim.257, s32[1024]{0:T(1024)S(1)} %copy-done.67, f32[1024,2,256]{2,1,0:T(2,128)} %copy.291), kind=kCustom, calls=%fused_computation.1 | custom fusion | flops 524288 | bytes 6295552 | tf_op jit(solution)/shard_map/transpose(jvp())/scatter-add | solution.py:119
  4401.3 10.1 fusion.129
  4411.5 7.3 fusion.113
  4439.8 38.2 all-reduce.3
  4481.3 37.1 all-reduce.9.cloned.1.call-done
  4518.4 364.8 %all-reduce.11.cloned.1.call-done = (f32[1024,256]{1,0:T(8,128)}, f32[1024,256]{1,0:T(8,128)}, f32[256,1024]{1,0:T(8,128)}, f32[1024,1024]{1,0:T(8,128)}, f32[1024,1024]{1,0:T(8,128)}) async-done(((f32[1024,256]{1,0:T(8,128)}, f32[1024,256]{1,0:T(8,128)}, f32[256,1024]{1,0:T(8,128)}, f32[1024,1024]{1,0:T(8,128)}, f32[1024,1024]{1,0:T(8,128)}), (f32[1024,256]{1,0:T(8,128)}, f32[1024,256]{1,0:T(8,128)}, ...) | async-done | bytes 11534352 | tf_op jit(solution)/shard_map/psum | solution.py:414
  (5085 shorter events, 3820.7 us)
Async XLA Ops:
  7.2 1366.4 %copy-start = (bf16[1024,1024]{1,0:T(8,128)(2,1)S(1)}, bf16[1024,1024]{1,0:T(8,128)(2,1)}, u32[]{:S(2)}) copy-start(bf16[1024,1024]{1,0:T(8,128)(2,1)} %param.33) | copy-start | bytes 6291460
  7.2 40.1 all-gather.7.cloned.1.call-start
  7.9 1291.1 %reduce-scatter.5.cloned.1.call-start = ((), (), s32[]{:S(2)}) async-start(), calls=%async_computation.5 | async-start | bytes 5242880 | tf_op jit(solution)/shard_map/reduce_scatter | solution.py:30
  8.9 43.2 copy-start.66
  10.6 48.5 copy-start.60
  10.6 49.2 %copy-start.84 = (f32[256,16]{0,1:T(8,128)}, f32[256,16]{0,1:T(8,128)S(1)}, u32[]{:S(2)}) copy-start(f32[256,16]{0,1:T(8,128)S(1)} %get-tuple-element.1633) | copy-start | bytes 49156
  10.6 81.8 %copy-start.48 = (f32[256,16]{0,1:T(8,128)}, f32[256,16]{0,1:T(8,128)S(1)}, u32[]{:S(2)}) copy-start(f32[256,16]{0,1:T(8,128)S(1)} %get-tuple-element.1668) | copy-start | bytes 49156
  15.0 42.4 copy-start.106
  15.0 87.0 %copy-start.68 = (f32[32,32]{1,0:T(8,128)}, f32[32,32]{1,0:T(8,128)S(1)}, u32[]{:S(2)}) copy-start(f32[32,32]{1,0:T(8,128)S(1)} %fusion.109) | copy-start | bytes 12292
  15.8 36.4 copy-start.97
  57.3 33.4 copy-start.54
  57.4 33.4 copy-start.52
  59.1 46.1 copy-start.89
  59.8 45.5 copy-start.70
  59.8 45.5 copy-start.86
  1176.2 16.3 copy-start.3
  1176.2 16.3 copy-start.19
  1176.2 16.3 copy-start.22
  1176.2 16.3 copy-start.24
  1176.2 16.3 copy-start.93
  1176.2 12.0 copy-start.96
  1177.3 10.9 collective-permute-start
  1180.7 7.5 collective-permute-start.1
  1253.9 83.1 %all-gather.9.cloned.1.call-start = ((), (), s32[]{:S(2)}) async-start(), calls=%async_computation.6 | async-start | bytes 5242880 | tf_op jit(solution)/shard_map/all_gather | solution.py:26
  1301.9 71.7 %all-gather.11.cloned.1.call-start = ((), (), s32[]{:S(2)}) async-start(), calls=%async_computation.8 | async-start | bytes 5242880 | tf_op jit(solution)/shard_map/all_gather | solution.py:26
  1302.4 39.5 copy-start.103
  1302.4 161.7 %reduce-scatter.9.cloned.1.call-start = ((), (), s32[]{:S(2)}) async-start(), calls=%async_computation.9 | async-start | bytes 5242880 | tf_op jit(solution)/shard_map/reduce_scatter | solution.py:30
  1340.5 74.9 %copy-start.80 = (f32[2048]{0:T(1024)}, f32[2048]{0:T(1024)S(1)}, u32[]{:S(2)}) copy-start(f32[2048]{0:T(1024)S(1)} %broadcast_multiply_fusion.5) | copy-start | bytes 24580
  1341.9 73.5 %copy-start.91 = (f32[2048]{0:T(1024)}, f32[2048]{0:T(1024)S(1)}, u32[]{:S(2)}) copy-start(f32[2048]{0:T(1024)S(1)} %add_rsqrt_fusion) | copy-start | bytes 24580
  1373.6 34.6 copy-start.17
  1373.6 34.6 copy-start.112
  1419.5 82.7 %all-gather.13.cloned.1.call-start = ((), (), s32[]{:S(2)}) async-start(), calls=%async_computation.10 | async-start | bytes 5242880 | tf_op jit(solution)/shard_map/all_gather | solution.py:26
  1466.9 2968.8 %reduce-scatter.7.cloned.1.call-start = ((), (), s32[]{:S(2)}) async-start(), calls=%async_computation.7 | async-start | bytes 5242880 | tf_op jit(solution)/shard_map/reduce_scatter | solution.py:30
  1680.4 13.5 collective-permute-start.3
  1690.0 2788.0 %reduce-scatter.11.cloned.1.call-start = ((), (), s32[]{:S(2)}) async-start(), calls=%async_computation.11 | async-start | bytes 5242880 | tf_op jit(solution)/shard_map/reduce_scatter | solution.py:30
  1692.6 6.8 collective-permute-start.2
  4270.2 37.7 copy-start.35
  4270.2 37.8 copy-start.29
  4270.2 37.9 copy-start.69
  4312.9 72.3 %copy-start.49 = (f32[256,16]{0,1:T(8,128)S(1)}, f32[256,16]{0,1:T(8,128)}, u32[]{:S(2)}) copy-start(f32[256,16]{0,1:T(8,128)} %copy-done.48) | copy-start | bytes 49156
  4312.9 72.3 %copy-start.108 = (f32[8]{0:T(128)S(1)}, f32[8]{0:T(128)}, u32[]{:S(2)}) copy-start(f32[8]{0:T(128)} %multiply_convert_fusion.2) | copy-start | bytes 100
  4312.9 72.3 %copy-start.109 = (pred[8]{0:T(512)(128)(4,1)S(1)}, pred[8]{0:T(512)(128)(4,1)}, u32[]{:S(2)}) copy-start(pred[8]{0:T(512)(128)(4,1)} %fusion.112) | copy-start | bytes 28
  4312.9 72.6 %copy-start.59 = (f32[256,16]{0,1:T(8,128)S(1)}, f32[256,16]{0,1:T(8,128)}, u32[]{:S(2)}) copy-start(f32[256,16]{0,1:T(8,128)} %param.34) | copy-start | bytes 49156
  4312.9 72.6 %copy-start.61 = (f32[256,16]{0,1:T(8,128)S(1)}, f32[256,16]{0,1:T(8,128)}, u32[]{:S(2)}) copy-start(f32[256,16]{0,1:T(8,128)} %copy-done.60) | copy-start | bytes 49156
  4312.9 72.6 %copy-start.90 = (f32[256,16]{0,1:T(8,128)S(1)}, f32[256,16]{0,1:T(8,128)}, u32[]{:S(2)}) copy-start(f32[256,16]{0,1:T(8,128)} %copy-done.89) | copy-start | bytes 49156
  4312.9 73.3 %copy-start.107 = (f32[512]{0:T(512)S(1)}, f32[512]{0:T(512)}, u32[]{:S(2)}) copy-start(f32[512]{0:T(512)} %copy-done.106) | copy-start | bytes 6148
  4401.0 117.4 %all-reduce.9.cloned.1.call-start = ((), (), s32[]{:S(2)}) async-start(), calls=%async_computation.12 | async-start | bytes 131072 | tf_op jit(solution)/shard_map/psum | solution.py:414
  4431.2 452.0 %all-reduce.11.cloned.1.call-start = ((), (), s32[]{:S(2)}) async-start(), calls=%async_computation.13 | async-start | bytes 23068672 | tf_op jit(solution)/shard_map/psum | solution.py:414
  (884 other events, 4163.4 us)
Sparse Core Ops, SparseCore 0:
  9.6 37.7 all-gather.6
  1254.0 44.9 reduce-scatter.4
  1302.0 35.0 all-gather.8
  1338.5 35.0 all-gather.10
  1419.6 44.5 reduce-scatter.8
  1467.1 35.0 all-gather.12
  1690.1 45.6 reduce-scatter.6
  4401.1 43.1 reduce-scatter.10
  4448.7 69.6 all-reduce.8
  4524.4 358.7 all-reduce.10
where the time goes:
time: 4970 us; the launch traced here: 4910 us
  other arithmetic  1500 us (30%)
  local copies, waits for them, and re-layouts  1430 us (29%)
  matrix products  1170 us (24%)
  waiting for transfers between devices  611 us (12%)
  blocking collectives  101 us (2%)
  loops' own time  59.2 us (1%)
    dot_general x192, matrix products, one_block(): jnp.einsum('tcn,kcn->ktc', lead_powers, readout * ssm_state[None], precis...  964 us
    psum x2, waiting for transfers between devices, on_device(): lax.psum((grad_w_in, grad_w_query, grad_w_out, grad_w_up, grad_w_down, gr...  402 us
    add_any x128, other arithmetic, ssm_outputs(): lax.scan(jax.checkpoint(one_block), (state_in, jnp.zeros((), jnp.int32)),...  360 us
    dynamic_slice x192, local copies, waits for them, and re-layouts, ssm_outputs(): lax.scan(jax.checkpoint(one_block), (state_in, jnp.zeros((), jnp.int32)),...  233 us
    dynamic_update_slice x256, local copies, waits for them, and re-layouts, ssm_outputs(): lax.scan(jax.checkpoint(one_block), (state_in, jnp.zeros((), jnp.int32)),...  223 us
    squeeze x192, local copies, waits for them, and re-layouts, ssm_outputs(): lax.scan(jax.checkpoint(one_block), (state_in, jnp.zeros((), jnp.int32)),...  190 us
    while x1720, local copies, waits for them, and re-layouts  169 us
    add_any x64, other arithmetic, one_block(): ssm_state[None]  165 us

commit v1 on v0

v1 whole, which is shorter than its diff:
```python
import functools

import jax
import jax.numpy as jnp
from jax import lax
from jax.experimental import pallas as pl
from jax.experimental.pallas import tpu as pltpu
from jax.sharding import PartitionSpec as P

HEAD = 128
BLOCK = 512
CTX = 128
LONG_DEV = 512
EPS = 1e-05
SEG = 8
GROUP = 8
STATES = 16
LANES = 128
VMEM = pl.BlockSpec(memory_space=pltpu.VMEM)
SMEM = pl.BlockSpec(memory_space=pltpu.SMEM)


def seg_scan_params(par_ref, wide_ref):
    for p in range(par_ref.shape[0]):
        for n in range(STATES):
            for lt in range(par_ref.shape[2] // LANES):
                row = par_ref[p, n : n + 1, lt * LANES : (lt + 1) * LANES]
                wide_ref[p, n, lt] = jnp.broadcast_to(row, (SEG, LANES))


def keep_mask(bounds_ref, span, step):
    rows = lax.broadcasted_iota(jnp.int32, (SEG, LANES), 0) * span + step
    keep = jnp.ones((SEG, LANES), jnp.float32)
    for k in range(bounds_ref.shape[0]):
        keep = jnp.where(rows == bounds_ref[k], 0.0, keep)
    return keep


def has_bound(bounds_ref, span, group):
    found = False
    for k in range(bounds_ref.shape[0]):
        b = bounds_ref[k]
        inside = lax.rem(b, span) // GROUP == group
        found = jnp.logical_or(found, jnp.logical_and(b >= 0, inside))
    return found


def steps_of(ref, lt, group, span):
    return [ref[lt, pl.ds(group * GROUP + j, SEG, stride=span), :] for j in range(GROUP)]


def split_lanes(src_ref, dst_ref):
    for lt in range(dst_ref.shape[0]):
        dst_ref[lt] = src_ref[:, lt * LANES : (lt + 1) * LANES].astype(jnp.float32)


def with_masks(bounds_ref, span, group, body):
    flag = has_bound(bounds_ref, span, group)

    @pl.when(flag)
    def _():
        body([keep_mask(bounds_ref, span, group * GROUP + j) for j in range(GROUP)])

    @pl.when(jnp.logical_not(flag))
    def _():
        body(None)


def forward_ends(bounds_ref, u_ref, wide_ref, state_ref, span, tiles):
    state_ref[...] = jnp.zeros_like(state_ref)

    @pl.loop(0, span // GROUP)
    def _(group):
        def body(keep):
            for lt in range(tiles):
                u = steps_of(u_ref, lt, group, span)
                for n in range(STATES):
                    a = wide_ref[0, n, lt]
                    s = state_ref[lt, n * SEG : (n + 1) * SEG, :]
                    for j in range(GROUP):
                        s = a * s
                        if keep is not None:
                            s = s * keep[j]
                        s = s + u[j]
                    state_ref[lt, n * SEG : (n + 1) * SEG, :] = s

        with_masks(bounds_ref, span, group, body)


def no_bound_in_seg(bounds_ref, span, seg):
    ok = jnp.float32(1.0)
    for k in range(bounds_ref.shape[0]):
        b = bounds_ref[k]
        inside = jnp.logical_and(b >= seg * span, b < (seg + 1) * span)
        ok = jnp.where(inside, jnp.float32(0.0), ok)
    return ok


def chain_forward(bounds_ref, state_ref, first, far_ref, span, tiles):
    for lt in range(tiles):
        lanes = slice(lt * LANES, (lt + 1) * LANES)
        start = first[:, lanes]
        far = far_ref[:, lanes]
        for seg in range(SEG):
            rows = pl.ds(seg, STATES, stride=SEG)
            end = state_ref[lt, rows, :]
            state_ref[lt, rows, :] = start
            start = end + far * start * no_bound_in_seg(bounds_ref, span, seg)


def chain_backward(bounds_ref, adj_ref, last, far_ref, span, tiles):
    for lt in range(tiles):
        lanes = slice(lt * LANES, (lt + 1) * LANES)
        start = last[:, lanes]
        far = far_ref[:, lanes]
        for seg in reversed(range(SEG)):
            rows = pl.ds(seg, STATES, stride=SEG)
            end = adj_ref[lt, rows, :]
            adj_ref[lt, rows, :] = start
            start = end + far * start * no_bound_in_seg(bounds_ref, span, seg)
        yield start


def ends_kernel(span, tiles, bounds_ref, u_in, par_ref, far_ref, out_ref, u_ref, wide_ref, state_ref):
    split_lanes(u_in, u_ref)
    seg_scan_params(par_ref, wide_ref)
    forward_ends(bounds_ref, u_ref, wide_ref, state_ref, span, tiles)
    for lt in range(tiles):
        lanes = slice(lt * LANES, (lt + 1) * LANES)
        start = jnp.zeros((STATES, LANES), jnp.float32)
        for seg in range(SEG):
            end = state_ref[lt, pl.ds(seg, STATES, stride=SEG), :]
            start = end + far_ref[:, lanes] * start * no_bound_in_seg(bounds_ref, span, seg)
        out_ref[:, lanes] = start


def forward_kernel(span, tiles, bounds_ref, u_in, par_ref, far_ref, first_ref, k_out, v_out, ckpt_ref,
                   u_ref, k_ref, v_ref, wide_ref, state_ref):
    split_lanes(u_in, u_ref)
    seg_scan_params(par_ref, wide_ref)
    forward_ends(bounds_ref, u_ref, wide_ref, state_ref, span, tiles)
    chain_forward(bounds_ref, state_ref, first_ref[...], far_ref, span, tiles)

    @pl.loop(0, span // GROUP)
    def _(group):
        def body(keep):
            for lt in range(tiles):
                u = steps_of(u_ref, lt, group, span)
                ks = [jnp.zeros((SEG, LANES), jnp.float32)] * GROUP
                vs = [jnp.zeros((SEG, LANES), jnp.float32)] * GROUP
                for n in range(STATES):
                    a, ck, cv = wide_ref[0, n, lt], wide_ref[1, n, lt], wide_ref[2, n, lt]
                    s = state_ref[lt, n * SEG : (n + 1) * SEG, :]
                    ckpt_ref[group, lt, n * SEG : (n + 1) * SEG, :] = s
                    for j in range(GROUP):
                        s = a * s
                        if keep is not None:
                            s = s * keep[j]
                        s = s + u[j]
                        ks[j] = ks[j] + ck * s
                        vs[j] = vs[j] + cv * s
                    state_ref[lt, n * SEG : (n + 1) * SEG, :] = s
                for j in range(GROUP):
                    rows = pl.ds(group * GROUP + j, SEG, stride=span)
                    k_ref[lt, rows, :] = ks[j]
                    v_ref[lt, rows, :] = vs[j]

        with_masks(bounds_ref, span, group, body)

    for lt in range(tiles):
        k_out[:, lt * LANES : (lt + 1) * LANES] = k_ref[lt].astype(k_out.dtype)
        v_out[:, lt * LANES : (lt + 1) * LANES] = v_ref[lt].astype(v_out.dtype)


def adjoint_ends(bounds_ref, gk_ref, gv_ref, wide_ref, adj_ref, span, tiles):
    adj_ref[...] = jnp.zeros_like(adj_ref)
    groups = span // GROUP

    @pl.loop(0, groups)
    def _(step):
        group = groups - 1 - step

        def body(keep):
            for lt in range(tiles):
                gk = steps_of(gk_ref, lt, group, span)
                gv = steps_of(gv_ref, lt, group, span)
                for n in range(STATES):
                    a, ck, cv = wide_ref[0, n, lt], wide_ref[1, n, lt], wide_ref[2, n, lt]
                    m = adj_ref[lt, n * SEG : (n + 1) * SEG, :]
                    for j in reversed(range(GROUP)):
                        m = a * (m + (ck * gk[j] + cv * gv[j]))
                        if keep is not None:
                            m = m * keep[j]
                    adj_ref[lt, n * SEG : (n + 1) * SEG, :] = m

        with_masks(bounds_ref, span, group, body)


def adjoint_ends_kernel(span, tiles, bounds_ref, gk_in, gv_in, par_ref, far_ref, out_ref, gk_ref, gv_ref, wide_ref, adj_ref):
    split_lanes(gk_in, gk_ref)
    split_lanes(gv_in, gv_ref)
    seg_scan_params(par_ref, wide_ref)
    adjoint_ends(bounds_ref, gk_ref, gv_ref, wide_ref, adj_ref, span, tiles)
    for lt in range(tiles):
        lanes = slice(lt * LANES, (lt + 1) * LANES)
        start = jnp.zeros((STATES, LANES), jnp.float32)
        for seg in reversed(range(SEG)):
            end = adj_ref[lt, pl.ds(seg, STATES, stride=SEG), :]
            start = end + far_ref[:, lanes] * start * no_bound_in_seg(bounds_ref, span, seg)
        out_ref[:, lanes] = start


def backward_kernel(span, tiles, bounds_ref, u_in, gk_in, gv_in, par_ref, far_ref, last_ref, ckpt_ref,
                    gu_out, sums_out, u_ref, gk_ref, gv_ref, gu_ref, wide_ref, adj_ref, acc_ref):
    split_lanes(u_in, u_ref)
    split_lanes(gk_in, gk_ref)
    split_lanes(gv_in, gv_ref)
    seg_scan_params(par_ref, wide_ref)
    adjoint_ends(bounds_ref, gk_ref, gv_ref, wide_ref, adj_ref, span, tiles)
    for _ in chain_backward(bounds_ref, adj_ref, last_ref[...], far_ref, span, tiles):
        pass
    acc_ref[...] = jnp.zeros_like(acc_ref)
    groups = span // GROUP

    @pl.loop(0, groups)
    def _(step):
        group = groups - 1 - step

        def body(keep):
            for lt in range(tiles):
                u = steps_of(u_ref, lt, group, span)
                gk = steps_of(gk_ref, lt, group, span)
                gv = steps_of(gv_ref, lt, group, span)
                gu = [jnp.zeros((SEG, LANES), jnp.float32)] * GROUP
                for n in range(STATES):
                    mine = slice(n * SEG, (n + 1) * SEG)
                    a, ck, cv = wide_ref[0, n, lt], wide_ref[1, n, lt], wide_ref[2, n, lt]
                    states = [ckpt_ref[group, lt, mine, :]]
                    for j in range(GROUP):
                        s = a * states[j]
                        if keep is not None:
                            s = s * keep[j]
                        states.append(s + u[j])
                    m = adj_ref[lt, mine, :]
                    sum_k, sum_v, sum_a = acc_ref[0, lt, mine, :], acc_ref[1, lt, mine, :], acc_ref[2, lt, mine, :]
                    for j in reversed(range(GROUP)):
                        lam = m + (ck * gk[j] + cv * gv[j])
                        gu[j] = gu[j] + lam
                        sum_k = sum_k + gk[j] * states[j + 1]
                        sum_v = sum_v + gv[j] * states[j + 1]
                        m = a * lam
                        if keep is not None:
                            m = m * keep[j]
                        sum_a = sum_a + m * states[j]
                    acc_ref[0, lt, mine, :] = sum_k
                    acc_ref[1, lt, mine, :] = sum_v
                    acc_ref[2, lt, mine, :] = sum_a
                    adj_ref[lt, mine, :] = m
                for j in range(GROUP):
                    gu_ref[lt, pl.ds(group * GROUP + j, SEG, stride=span), :] = gu[j]

        with_masks(bounds_ref, span, group, body)

    for lt in range(tiles):
        lanes = slice(lt * LANES, (lt + 1) * LANES)
        gu_out[:, lanes] = gu_ref[lt].astype(gu_out.dtype)
        for p in range(3):
            total = acc_ref[p, lt, pl.ds(0, STATES, stride=SEG), :]
            for seg in range(1, SEG):
                total = total + acc_ref[p, lt, pl.ds(seg, STATES, stride=SEG), :]
            sums_out[p, :, lanes] = total


LIMIT = pltpu.CompilerParams(vmem_limit_bytes=48 * 2**20)


def f32(*shape):
    return pltpu.VMEM(shape, jnp.float32)


def ssm_ends(bounds, u, par, far, name="ssm_ends"):
    rows, width = u.shape
    span, tiles = rows // SEG, width // LANES
    return pl.pallas_call(
        functools.partial(ends_kernel, span, tiles),
        out_shape=jax.ShapeDtypeStruct((STATES, width), jnp.float32),
        in_specs=[SMEM] + [VMEM] * 3, out_specs=VMEM,
        scratch_shapes=[f32(tiles, rows, LANES), f32(3, STATES, tiles, SEG, LANES), f32(tiles, STATES * SEG, LANES)],
        compiler_params=LIMIT, name=name)(bounds, u, par, far)


def ssm_forward(bounds, u, par, far, first, name="ssm_forward"):
    rows, width = u.shape
    span, tiles = rows // SEG, width // LANES
    return pl.pallas_call(
        functools.partial(forward_kernel, span, tiles),
        out_shape=(jax.ShapeDtypeStruct((rows, width), jnp.bfloat16), jax.ShapeDtypeStruct((rows, width), jnp.bfloat16),
                   jax.ShapeDtypeStruct((span // GROUP, tiles, STATES * SEG, LANES), jnp.float32)),
        in_specs=[SMEM] + [VMEM] * 4, out_specs=(VMEM,) * 3,
        scratch_shapes=[f32(tiles, rows, LANES)] * 3 + [f32(3, STATES, tiles, SEG, LANES), f32(tiles, STATES * SEG, LANES)],
        compiler_params=LIMIT, name=name)(bounds, u, par, far, first)


def ssm_adjoint_ends(bounds, gk, gv, par, far, name="ssm_adjoint_ends"):
    rows, width = gk.shape
    span, tiles = rows // SEG, width // LANES
    return pl.pallas_call(
        functools.partial(adjoint_ends_kernel, span, tiles),
        out_shape=jax.ShapeDtypeStruct((STATES, width), jnp.float32),
        in_specs=[SMEM] + [VMEM] * 4, out_specs=VMEM,
        scratch_shapes=[f32(tiles, rows, LANES)] * 2 + [f32(3, STATES, tiles, SEG, LANES), f32(tiles, STATES * SEG, LANES)],
        compiler_params=LIMIT, name=name)(bounds, gk, gv, par, far)


def ssm_backward(bounds, u, gk, gv, par, far, last, ckpt, name="ssm_backward"):
    rows, width = u.shape
    span, tiles = rows // SEG, width // LANES
    return pl.pallas_call(
        functools.partial(backward_kernel, span, tiles),
        out_shape=(jax.ShapeDtypeStruct((rows, width), jnp.bfloat16), jax.ShapeDtypeStruct((3, STATES, width), jnp.float32)),
        in_specs=[SMEM] + [VMEM] * 7, out_specs=(VMEM,) * 2,
        scratch_shapes=[f32(tiles, rows, LANES)] * 4 + [f32(3, STATES, tiles, SEG, LANES), f32(tiles, STATES * SEG, LANES), f32(3, tiles, STATES * SEG, LANES)],
        compiler_params=LIMIT, name=name)(bounds, u, gk, gv, par, far, last, ckpt)


QT = 256
NEG = -1e30
SCALE = HEAD ** (-0.5)


def tiles_of(rows, shift):
    out = []
    for r in range(0, rows, QT):
        first = max(0, r + shift - (BLOCK + CTX)) if shift == 0 else 0
        out.append((r, first, r + shift + QT))
    return out


def lowest_key(starts_ref, row0, shift):
    if shift:
        return jnp.full((1, QT), starts_ref[0], jnp.int32)
    rows = lax.broadcasted_iota(jnp.int32, (1, QT), 1) + row0
    start = jnp.zeros((1, QT), jnp.int32)
    for k in range(starts_ref.shape[0]):
        start = jnp.where(rows >= starts_ref[k], starts_ref[k], start)
    block = ((rows - start) // BLOCK) * BLOCK - CTX
    return start + jnp.maximum(block, 0)


def allowed_keys(starts_ref, q0, k0, k1, shift):
    low = lowest_key(starts_ref, q0, shift)
    high = lax.broadcasted_iota(jnp.int32, (1, QT), 1) + (q0 + shift)
    keys = lax.broadcasted_iota(jnp.int32, (k1 - k0, QT), 0) + k0
    return (keys >= low) & (keys <= high)


def dot_nt(a, b):
    return lax.dot_general(a, b, (((1,), (1,)), ((), ())), preferred_element_type=jnp.float32)


def dot_nn(a, b):
    return lax.dot_general(a, b, (((1,), (0,)), ((), ())), preferred_element_type=jnp.float32)


def attend_kernel(tiles, shift, starts_ref, q_ref, k_ref, v_ref, o_ref, lse_ref, vt_ref):
    vt_ref[...] = v_ref[...].T
    for q0, k0, k1 in tiles:
        scores = dot_nt(k_ref[k0:k1, :], q_ref[q0 : q0 + QT, :]) * SCALE
        scores = jnp.where(allowed_keys(starts_ref, q0, k0, k1, shift), scores, NEG)
        top = jnp.max(scores, axis=0, keepdims=True)
        exps = jnp.exp(scores - top)
        total = jnp.sum(exps, axis=0, keepdims=True)
        probs = (exps * (1.0 / total)).astype(jnp.bfloat16)
        mixed = dot_nn(vt_ref[:, k0:k1], probs)
        o_ref[q0 : q0 + QT, :] = mixed.T.astype(o_ref.dtype)
        lse_ref[0, 0, q0 : q0 + QT] = (top + jnp.log(total))[0]


def attend(starts, q, k, v, shift, name):
    rows, width = q.shape
    heads = width // HEAD
    keys = k.shape[0]
    lane = lambda h: (0, h)
    return pl.pallas_call(
        functools.partial(attend_kernel, tiles_of(rows, shift), shift),
        grid=(heads,),
        out_shape=(jax.ShapeDtypeStruct((rows, width), jnp.bfloat16), jax.ShapeDtypeStruct((heads, 1, rows), jnp.float32)),
        in_specs=[SMEM, pl.BlockSpec((rows, HEAD), lane), pl.BlockSpec((keys, HEAD), lane), pl.BlockSpec((keys, HEAD), lane)],
        out_specs=(pl.BlockSpec((rows, HEAD), lane), pl.BlockSpec((1, 1, rows), lambda h: (h, 0, 0))),
        scratch_shapes=[pltpu.VMEM((HEAD, keys), jnp.bfloat16)],
        compiler_params=pltpu.CompilerParams(vmem_limit_bytes=40 * 2**20),
        name=name)(starts, q, k, v)


def attend_back_kernel(tiles, shift, starts_ref, q_ref, k_ref, v_ref, g_ref, lse_ref, dq_ref, dk_ref, dv_ref, kt_ref):
    kt_ref[...] = k_ref[...].T
    dk_ref[...] = jnp.zeros_like(dk_ref)
    dv_ref[...] = jnp.zeros_like(dv_ref)
    for q0, k0, k1 in tiles:
        q = q_ref[q0 : q0 + QT, :]
        g = g_ref[q0 : q0 + QT, :]
        lse = lse_ref[0, :, q0 : q0 + QT]
        scores = dot_nt(k_ref[k0:k1, :], q) * SCALE
        probs = jnp.where(allowed_keys(starts_ref, q0, k0, k1, shift), jnp.exp(scores - lse), 0.0)
        grad_probs = dot_nt(v_ref[k0:k1, :], g)
        dv_ref[k0:k1, :] += dot_nn(probs.astype(jnp.bfloat16), g)
        delta = jnp.sum(probs * grad_probs, axis=0, keepdims=True)
        grad_scores = (probs * (grad_probs - delta)).astype(jnp.bfloat16)
        dk_ref[k0:k1, :] += dot_nn(grad_scores, q) * SCALE
        dq_ref[q0 : q0 + QT, :] = (dot_nn(kt_ref[:, k0:k1], grad_scores) * SCALE).T.astype(dq_ref.dtype)


def attend_back(starts, q, k, v, g, lse, shift, name):
    rows, width = q.shape
    heads = width // HEAD
    keys = k.shape[0]
    lane = lambda h: (0, h)
    rspec, kspec = pl.BlockSpec((rows, HEAD), lane), pl.BlockSpec((keys, HEAD), lane)
    return pl.pallas_call(
        functools.partial(attend_back_kernel, tiles_of(rows, shift), shift),
        grid=(heads,),
        out_shape=(jax.ShapeDtypeStruct((rows, width), jnp.bfloat16), jax.ShapeDtypeStruct((keys, width), jnp.float32), jax.ShapeDtypeStruct((keys, width), jnp.float32)),
        in_specs=[SMEM, rspec, kspec, kspec, rspec, pl.BlockSpec((1, 1, rows), lambda h: (h, 0, 0))],
        out_specs=(rspec, kspec, kspec),
        scratch_shapes=[pltpu.VMEM((HEAD, keys), jnp.bfloat16)],
        compiler_params=pltpu.CompilerParams(vmem_limit_bytes=40 * 2**20),
        name=name)(starts, q, k, v, g, lse)


def gather_features(values_in):
    return lax.all_gather(values_in, "mp", axis=1, tiled=True)


def reduce_features(values_in):
    return lax.psum_scatter(
        values_in.astype(jnp.bfloat16), "mp", scatter_dimension=1, tiled=True
    ).astype(jnp.float32)


def from_behind(value, axis, steps):
    count = lax.axis_size(axis)
    initial, last = (max(0, -steps), min(count, count - steps))
    return lax.ppermute(value, axis, [(source, source + steps) for source in range(initial, last)])


def norm_forward(values_in, gain_vec):
    row_mean = jnp.mean(values_in, axis=1, keepdims=True)
    centred = values_in - row_mean
    row_var = jnp.mean(centred * centred, axis=1, keepdims=True)
    inverse = lax.rsqrt(row_var + EPS)
    normed = centred * inverse
    return (normed, inverse, normed * gain_vec)


def norm_backward(upstream, normed, inverse, gain_vec):
    gain_grad = jnp.sum(upstream * normed, axis=0)
    scaled = upstream * gain_vec
    plain_mean = jnp.mean(scaled, axis=1, keepdims=True)
    cross_mean = jnp.mean(scaled * normed, axis=1, keepdims=True)
    return (inverse * (scaled - plain_mean - normed * cross_mean), gain_grad)


def gelu_exact(values_in):
    return jax.nn.gelu(values_in, approximate=False)


def fold_pieces(pieces, decay_rate, gap_count):
    live_rows = gap_count >= 0
    weights = jnp.exp(
        -decay_rate[None]
        * (LONG_DEV * jnp.maximum(gap_count, 0)).astype(jnp.float32)[:, None, None]
    )
    return jnp.sum(jnp.where(live_rows[:, None, None], weights * pieces, 0.0), axis=0)


def dot(left, right, dims):
    return lax.dot_general(left, right, ((dims[0], dims[1]), ((), ())), preferred_element_type=jnp.float32)


def on_device(
    tokens,
    gain_one,
    gain_two,
    w_in,
    w_query,
    w_out,
    w_up,
    w_down,
    decay_rate,
    b_in,
    c_key,
    c_val,
    short_lengths,
    cotangent,
):
    low = jnp.bfloat16
    device = lax.axis_index("dp")
    lengths = short_lengths[0]
    ends = jnp.cumsum(lengths).astype(jnp.int32)
    short_starts = jnp.concatenate([jnp.zeros((1,), jnp.int32), ends[:-1]])
    no_bound = jnp.full((1,), -1, jnp.int32)
    long_low = jnp.where(device > 0, 0, CTX).astype(jnp.int32).reshape(1)
    rate_t = decay_rate.T
    root = jnp.sqrt(-jnp.expm1(-2.0 * rate_t))
    drive = root * b_in.T
    ck_t, cv_t = c_key.T, c_val.T
    decay = jnp.exp(-rate_t)
    par = jnp.stack([decay, drive * ck_t, drive * cv_t])
    short_rows = tokens.shape[0] - LONG_DEV
    far_long = jnp.exp(-rate_t * (LONG_DEV // SEG))
    far_short = jnp.exp(-rate_t * (short_rows // SEG))

    tokens_full = gather_features(tokens).astype(jnp.float32)
    cotangent_full = gather_features(cotangent)
    normed_one, inverse_one, hidden_one = norm_forward(tokens_full, gain_one)
    normed_one_low = hidden_one.astype(low)
    ssm_input = jnp.dot(normed_one_low, w_in, preferred_element_type=jnp.float32)
    queries = jnp.dot(normed_one_low, w_query, preferred_element_type=jnp.float32).astype(low)
    u_long, u_short = ssm_input[:LONG_DEV], ssm_input[LONG_DEV:]
    local_end = ssm_ends(no_bound, u_long, par, far_long)
    pieces = lax.all_gather(local_end[None], "dp", axis=0, tiled=True)
    others = jnp.arange(pieces.shape[0], dtype=jnp.int32)
    state_in = fold_pieces(pieces, rate_t, device - 1 - others)
    zero_state = jnp.zeros_like(state_in)
    k_short, v_short, ckpt_short = ssm_forward(short_starts, u_short, par, far_short, zero_state, "ssm_short")
    k_long, v_long, ckpt_long = ssm_forward(no_bound, u_long, par, far_long, state_in, "ssm_long")
    ctx_k, ctx_v = from_behind((k_long[LONG_DEV - CTX :], v_long[LONG_DEV - CTX :]), "dp", 1)
    k_long = jnp.concatenate([ctx_k, k_long])
    v_long = jnp.concatenate([ctx_v, v_long])
    q_long, q_short = queries[:LONG_DEV], queries[LONG_DEV:]
    att_short, lse_short = attend(short_starts, q_short, k_short, v_short, 0, "attend_short")
    att_long, lse_long = attend(long_low, q_long, k_long, v_long, CTX, "attend_long")
    attended = jnp.concatenate([att_long, att_short])
    middle = tokens.astype(jnp.float32) + reduce_features(
        jnp.dot(attended, w_out, preferred_element_type=jnp.float32)
    )
    middle_full = gather_features(middle.astype(low)).astype(jnp.float32)
    normed_two, inverse_two, hidden_two = norm_forward(middle_full, gain_two)
    normed_two_low = hidden_two.astype(low)
    pre_act = jnp.dot(normed_two_low, w_up, preferred_element_type=jnp.float32)
    act_value, act_pull = jax.vjp(gelu_exact, pre_act)
    act_low = act_value.astype(low)
    result = (
        middle + reduce_features(jnp.dot(act_low, w_down, preferred_element_type=jnp.float32))
    ).astype(low)
    grad_w_down = dot(act_low, cotangent_full, ((0,), (0,)))
    grad_act = dot(cotangent_full, w_down, ((1,), (1,)))
    grad_pre = act_pull(grad_act)[0].astype(low)
    grad_w_up = dot(normed_two_low, grad_pre, ((0,), (0,)))
    grad_hidden_two = dot(grad_pre, w_up, ((1,), (1,)))
    middle_part, grad_gain_two = norm_backward(grad_hidden_two, normed_two, inverse_two, gain_two)
    grad_middle = cotangent.astype(jnp.float32) + reduce_features(middle_part)
    grad_mid_full = gather_features(grad_middle.astype(low))
    grad_w_out = dot(attended, grad_mid_full, ((0,), (0,)))
    grad_attended = dot(grad_mid_full, w_out, ((1,), (1,))).astype(low)

    gq_long, gk_long, gv_long = attend_back(
        long_low, q_long, k_long, v_long, grad_attended[:LONG_DEV], lse_long, CTX, "attend_back_long"
    )
    back_k, back_v = from_behind((gk_long[:CTX].astype(low), gv_long[:CTX].astype(low)), "dp", -1)
    gq_short, gk_short, gv_short = attend_back(
        short_starts, q_short, k_short, v_short, grad_attended[LONG_DEV:], lse_short, 0, "attend_back_short"
    )
    gk_long = gk_long[CTX:].at[LONG_DEV - CTX :].add(back_k.astype(jnp.float32))
    gv_long = gv_long[CTX:].at[LONG_DEV - CTX :].add(back_v.astype(jnp.float32))
    local_in = ssm_adjoint_ends(no_bound, gk_long, gv_long, par, far_long)
    grad_pieces = lax.all_gather(local_in[None], "dp", axis=0, tiled=True)
    grad_end = fold_pieces(grad_pieces, rate_t, others - device - 1)
    gu_short, sums_short = ssm_backward(
        short_starts, u_short, gk_short, gv_short, par, far_short, zero_state, ckpt_short, "ssm_back_short"
    )
    gu_long, sums_long = ssm_backward(
        no_bound, u_long, gk_long, gv_long, par, far_long, grad_end, ckpt_long, "ssm_back_long"
    )
    sums = sums_short + sums_long
    grad_ssm = jnp.concatenate([gu_long, gu_short])
    grad_queries = jnp.concatenate([gq_long, gq_short])
    grad_w_in = dot(normed_one_low, grad_ssm, ((0,), (0,)))
    grad_w_query = dot(normed_one_low, grad_queries, ((0,), (0,)))
    grad_hidden_one = dot(grad_ssm, w_in, ((1,), (1,))) + dot(grad_queries, w_query, ((1,), (1,)))
    token_part, grad_gain_one = norm_backward(grad_hidden_one, normed_one, inverse_one, gain_one)
    grad_tokens = (grad_middle + reduce_features(token_part)).astype(low)

    grad_w_in, grad_w_query, grad_w_out, grad_w_up, grad_w_down = (
        g.astype(jnp.float32)
        for g in lax.psum(
            tuple(g.astype(low) for g in (grad_w_in, grad_w_query, grad_w_out, grad_w_up, grad_w_down)), "dp"
        )
    )
    sums = lax.psum(sums, "dp")
    grad_ck = (drive * sums[0]).T
    grad_cv = (drive * sums[1]).T
    grad_drive = ck_t * sums[0] + cv_t * sums[1]
    grad_b = (root * grad_drive).T
    grad_rate = (grad_drive * b_in.T * jnp.exp(-2.0 * rate_t) / root - sums[2]).T
    grad_gain_one, grad_gain_two = lax.psum((grad_gain_one, grad_gain_two), ("dp", "mp"))
    return (
        result,
        grad_tokens,
        grad_gain_one,
        grad_gain_two,
        grad_w_in,
        grad_w_query,
        grad_w_out,
        grad_w_up,
        grad_w_down,
        grad_rate,
        grad_b,
        grad_ck,
        grad_cv,
    )


def solution(mesh):
    placed = (
        P("dp", "mp"),
        P(),
        P(),
        P(None, "mp"),
        P(None, "mp"),
        P("mp", None),
        P(None, "mp"),
        P("mp", None),
        P("mp", None),
        P("mp", None),
        P("mp", None),
        P("mp", None),
        P("dp", None),
        P("dp", "mp"),
    )
    return jax.shard_map(
        on_device,
        mesh=mesh,
        in_specs=placed,
        out_specs=(
            P("dp", "mp"),
            P("dp", "mp"),
            P(),
            P(),
            P(None, "mp"),
            P(None, "mp"),
            P("mp", None),
            P(None, "mp"),
            P("mp", None),
            P("mp", None),
            P("mp", None),
            P("mp", None),
            P("mp", None),
        ),
        check_vma=False,
    )
```

time: 4970 us -> 738 us (0.15); the launches traced: 4910 us -> 732 us
  other arithmetic: 1500 us -> 62 us
  local copies, waits for them, and re-layouts: 1430 us -> 6.41 us
  matrix products: 1170 us -> 92 us
  waiting for transfers between devices: 611 us -> 322 us
  Pallas kernels: 0 us -> 78 us
  loops' own time: 59.2 us -> 0 us
    dot_general x295 -> x11, matrix products: 1150 us -> 74.2 us  [the longest x10 70.9 us: dot(): lax.dot_general(left, right, ((dims[0], dims[1]), ((), ())), preferred_el...]
    add_any x195 -> x0, other arithmetic: 529 us -> none  [the longest x128 360 us: ssm_outputs(): lax.scan(jax.checkpoint(one_block), (state_in, jnp.zeros((), jnp.int32)),...]
    dynamic_slice x256 -> x0, local copies, waits for them, and re-layouts: 319 us -> none  [the longest x192 233 us: ssm_outputs(): lax.scan(jax.checkpoint(one_block), (state_in, jnp.zeros((), jnp.int32)),...]
    psum x2 -> x1, waiting for transfers between devices: 402 us -> 105 us  [on_device(): lax.psum(tuple((g.astype(low) for g in (grad_w_in, grad_w_query, grad_w_o...]
    dynamic_update_slice x280 -> x0, local copies, waits for them, and re-layouts: 273 us -> none  [the longest x256 223 us: ssm_outputs(): lax.scan(jax.checkpoint(one_block), (state_in, jnp.zeros((), jnp.int32)),...]
    mul x131 -> x0, other arithmetic: 194 us -> none  [the longest x64 135 us: ssm_outputs(): lead_powers = powers * jnp.exp(-decay_rate)[None]]
    squeeze x192 -> x0, local copies, waits for them, and re-layouts: 190 us -> none  [ssm_outputs(): lax.scan(jax.checkpoint(one_block), (state_in, jnp.zeros((), jnp.int32)),...]
    while x1727 -> x0, local copies, waits for them, and re-layouts: 179 us -> none
where the time goes in v1:
time: 738 us; the launch traced here: 732 us
  waiting for transfers between devices  322 us (44%)
  blocking collectives  147 us (20%)
  matrix products  92 us (12%)
  Pallas kernels  78 us (11%)
  other arithmetic  62 us (8%)
  between operations  15.3 us (2%)
  starting transfers between devices  9.1 us (1%)
    reduce_scatter x4, waiting for transfers between devices, reduce_features(): lax.psum_scatter(values_in.astype(jnp.bfloat16), 'mp', scatter_dimension=...  122 us
    psum x1, waiting for transfers between devices, on_device(): lax.psum(tuple((g.astype(low) for g in (grad_w_in, grad_w_query, grad_w_o...  105 us
    all_gather x4, waiting for transfers between devices, gather_features(): return lax.all_gather(values_in, 'mp', axis=1, tiled=True)  93.4 us
    dot_general x10, matrix products, dot(): lax.dot_general(left, right, ((dims[0], dims[1]), ((), ())), preferred_el...  70.9 us
    psum x1, blocking collectives, on_device(): lax.psum((grad_gain_one, grad_gain_two), ('dp', 'mp'))  44.4 us
    psum x1, blocking collectives, on_device(): sums = lax.psum(sums, 'dp')  37.9 us
    all_gather x1, blocking collectives, on_device(): grad_pieces = lax.all_gather(local_in[None], 'dp', axis=0, tiled=True)  34.1 us
    pallas_call x2, Pallas kernels, ssm_backward(): pl.pallas_call(functools.partial(backward_kernel, span, tiles), out_shape...  33.4 us
  transfers between devices with their start and end apart: 13, of which 7 were waited for; matrix products, arithmetic and copies ran while one was open for 13% of the time, Pallas kernels for 10%

profile of v1, /device:TPU:0, one launch (start us, length us, event | category | flops | bytes accessed | tf_op | source)
XLA Modules:
  0.0 731.8 jit_solution(2667952651008923057)
XLA Ops:
  11.2 36.1 %all-gather.7.cloned.1.call-done = bf16[2048,1024]{1,0:T(8,128)(2,1)} async-done(((bf16[2048,256]{1,0:T(8,128)(2,1)}), bf16[2048,1024]{1,0:T(8,128)(2,1)}) %all-gather.7.cloned.1.call-update) | async-done | bytes 4194320 | tf_op jit(solution)/shard_map/all_gather | solution.py:431
  47.3 3.0 convert_reduce_fusion.1
  50.3 3.0 fusion.25
  57.2 30.6 %all-gather = f32[128,256]{1,0:T(8,128)S(1)} all-gather(f32[16,256]{1,0:T(8,128)S(1)} %ssm_ends.1), channel_id=2, replica_groups=mesh['dp'=8,'mp'=4] {'dp'}, dimensions={0}, use_global_device_ids=true | all-gather | bytes 147456 | tf_op jit(solution)/shard_map/all_gather | solution.py:521
  87.9 3.8 ssm_long.1
  91.7 3.4 collective-permute-start
  96.7 2.1 collective-permute-start.1
  98.8 13.9 %ssm_short.1 = (bf16[1536,256]{1,0:T(8,128)(2,1)S(1)}, bf16[1536,256]{1,0:T(8,128)(2,1)S(1)}, f32[24,2,128,128]{3,2,1,0:T(8,128)}) custom-call(s32[2]{0:T(128)S(1)} %pad_add_fusion.bounds_ref.starts_ref, f32[1536,256]{1,0:T(8,128)S(1)} %slice.117.u_in, f32[3,16,256]{2,1,0:T(8,128)S(1)} %pad_maximum_fusion.par_ref, f32[16,256]{1,0:T(8,128)S(1)} %get-tuple-element.99.far_ref, ...), custom_call_target="tpu_custom_call" | custom-call | tf_op jit(solution)/shard_map/ssm_short/pallas_call | solution.py:295
  113.9 8.9 %attend_short.1 = (bf16[1536,256]{1,0:T(8,128)(2,1)S(1)}, f32[2,1,1536]{2,1,0:T(1,128)S(1)}) custom-call(s32[2]{0:T(128)S(1)} %pad_add_fusion.bounds_ref.starts_ref, bf16[1536,256]{1,0:T(8,128)(2,1)S(1)} %slice.116.q_ref, bf16[1536,256]{1,0:T(8,128)(2,1)S(1)} %get-tuple-element.60.k_ref, bf16[1536,256]{1,0:T(8,128)(2,1)S(1)} %get-tuple-element.61.v_ref), custom_call_target="tpu_custom_call" | custom-call | tf_op jit(solution)/shard_map/attend_short/pallas_call | solution.py:384
  123.8 2.7 attend_long.1
  128.3 3.3 convolution_convert_fusion
  131.7 45.1 %reduce-scatter.5.cloned.1.call-done = bf16[2048,256]{1,0:T(8,128)(2,1)} async-done(((bf16[2048,1024]{1,0:T(8,128)(2,1)}), bf16[2048,256]{1,0:T(8,128)(2,1)}) %reduce-scatter.5.cloned.1.call-update) | async-done | bytes 1048592 | tf_op jit(solution)/shard_map/reduce_scatter | solution.py:435
  176.7 2.8 fusion.32
  180.4 34.3 %all-gather.9.cloned.1.call-done = bf16[2048,1024]{1,0:T(8,128)(2,1)} async-done(((bf16[2048,256]{1,0:T(8,128)(2,1)}), bf16[2048,1024]{1,0:T(8,128)(2,1)}) %all-gather.9.cloned.1.call-update) | async-done | bytes 4194320 | tf_op jit(solution)/shard_map/all_gather | solution.py:431
  214.7 3.0 convert_reduce_fusion
  217.7 3.1 fusion.18
  221.5 6.9 fusion.44
  228.3 23.0 %all-gather.11.cloned.1.call-done = bf16[2048,1024]{1,0:T(8,128)(2,1)} async-done(((bf16[2048,256]{1,0:T(8,128)(2,1)}), bf16[2048,1024]{1,0:T(8,128)(2,1)}) %all-gather.11.cloned.1.call-update) | async-done | bytes 4194320 | tf_op jit(solution)/shard_map/all_gather | solution.py:431
  251.3 26.7 %add_convert_fusion = (bf16[2048,1024]{1,0:T(8,128)(2,1)S(1)}, f32[2048,1024]{1,0:T(8,128)}) fusion(f32[2048,1024]{1,0:T(8,128)} %fusion.44, bf16[2048,1024]{1,0:T(8,128)(2,1)} %all-gather.11.cloned.1.call-done, bf16[1024,1024]{1,0:T(8,128)(2,1)S(1)} %copy-done), kind=kOutput, calls=%fused_computation.32 | convolution fusion | flops 4445962240 | bytes 27262976 | tf_op jit(solution)/shard_map/dot_general | solution.py:477
  278.0 7.2 fusion.17
  285.2 4.0 fusion.16
  289.2 44.6 %reduce-scatter.9.cloned.1.call-done = bf16[2048,256]{1,0:T(8,128)(2,1)} async-done(((bf16[2048,1024]{1,0:T(8,128)(2,1)}), bf16[2048,256]{1,0:T(8,128)(2,1)}) %reduce-scatter.9.cloned.1.call-update) | async-done | bytes 1048592 | tf_op jit(solution)/shard_map/reduce_scatter | solution.py:435
  333.8 2.8 fusion.33
  336.7 10.1 %multiply_convert_fusion = bf16[2048,1024]{1,0:T(8,128)(2,1)} fusion(f32[2048,1024]{1,0:T(8,128)} %get-tuple-element.93, f32[2048,1024]{1,0:T(8,128)} %fusion.44), kind=kLoop, calls=%fused_computation.33 | loop fusion | flops 6291456 | bytes 20971520 | tf_op jit(solution)/shard_map/convert_element_type | solution.py:542
  346.8 8.3 %convolution_convert_fusion.1 = bf16[2048,1024]{1,0:T(8,128)(2,1)} fusion(bf16[2048,1024]{1,0:T(8,128)(2,1)} %multiply_convert_fusion, bf16[1024,1024]{1,0:T(8,128)(2,1)S(1)} %copy-done), kind=kOutput, calls=%fused_computation.51 | convolution fusion | flops 4297064448 | bytes 10485760 | tf_op jit(solution)/shard_map/dot_general | solution.py:544
  356.5 9.6 %convolution_convert_fusion.4 = bf16[1024,1024]{1,0:T(8,128)(2,1)} fusion(bf16[2048,1024]{1,0:T(8,128)(2,1)} %multiply_convert_fusion, bf16[2048,1024]{1,0:T(8,128)(2,1)} %all-gather.11.cloned.1.call-done), kind=kOutput, calls=%fused_computation.60 | convolution fusion | flops 4296015872 | bytes 10485760 | tf_op jit(solution)/shard_map/dot_general | solution.py:477
  366.1 6.9 convolution_convert_fusion.5
  373.0 3.7 convolution_convert_fusion.2
  376.8 2.9 attend_back_long.1
  382.6 9.2 %attend_back_short.1 = (bf16[1536,256]{1,0:T(8,128)(2,1)S(1)}, f32[1536,256]{1,0:T(8,128)S(1)}, f32[1536,256]{1,0:T(8,128)S(1)}) custom-call(s32[2]{0:T(128)S(1)} %pad_add_fusion.bounds_ref.starts_ref, bf16[1536,256]{1,0:T(8,128)(2,1)S(1)} %slice.116.q_ref, bf16[1536,256]{1,0:T(8,128)(2,1)S(1)} %copy-done.6, bf16[1536,256]{1,0:T(8,128)(2,1)S(1)} %copy-done.8, ...), custom_call_target="tpu_custom_call" | custom-call | tf_op jit(solution)/shard_map/attend_back_short/pallas_call | solution.py:419
  395.1 4.4 convolution_convert_fusion.6
  399.6 25.7 %ssm_back_short.1 = (bf16[1536,256]{1,0:T(8,128)(2,1)S(1)}, f32[3,16,256]{2,1,0:T(8,128)S(1)}) custom-call(s32[2]{0:T(128)S(1)} %pad_add_fusion.bounds_ref.starts_ref, f32[1536,256]{1,0:T(8,128)S(1)} %copy-done.2, f32[1536,256]{1,0:T(8,128)S(1)} %get-tuple-element.69.gk_in, f32[1536,256]{1,0:T(8,128)S(1)} %get-tuple-element.70.gv_in, ...), custom_call_target="tpu_custom_call" | custom-call | tf_op jit(solution)/shard_map/ssm_back_short/pallas_call | solution.py:318
  425.3 2.2 ssm_adjoint_ends.1
  427.5 34.1 %all-gather.1 = f32[128,256]{1,0:T(8,128)S(1)} all-gather(f32[16,256]{1,0:T(8,128)S(1)} %ssm_adjoint_ends.1), channel_id=3, replica_groups=mesh['dp'=8,'mp'=4] {'dp'}, dimensions={0}, use_global_device_ids=true | all-gather | bytes 147456 | tf_op jit(solution)/shard_map/all_gather | solution.py:567
  461.7 7.7 %ssm_back_long.1 = (bf16[512,256]{1,0:T(8,128)(2,1)S(1)}, f32[3,16,256]{2,1,0:T(8,128)S(1)}) custom-call(s32[1]{0:T(128)} %constant.117.clone.1.bounds_ref, f32[512,256]{1,0:T(8,128)S(1)} %copy-done.4, f32[512,256]{1,0:T(8,128)S(1)} %add_dynamic-update-slice_fusion.1.gk_in, f32[512,256]{1,0:T(8,128)S(1)} %add_dynamic-update-slice_fusion.gv_in, ...), custom_call_target="tpu_custom_call" | custom-call | tf_op jit(solution)/shard_map/ssm_back_long/pallas_call | solution.py:318
  469.6 4.3 convolution_convert_fusion.8
  474.0 2.5 fusion.49
  476.7 3.6 fusion.24
  480.3 4.0 fusion.23
  484.5 2.9 add_convert_fusion.2
  487.4 44.4 %all-reduce = (f32[1024]{0:T(1024)}, f32[1024]{0:T(1024)}) all-reduce(f32[1024]{0:T(1024)S(1)} %get-tuple-element.79, f32[1024]{0:T(1024)S(1)} %copy-done.53), channel_id=1, replica_groups=mesh['dp'=8,'mp'=4] {'dp','mp'}, use_global_device_ids=true, to_apply=%region_16.17 | all-reduce | flops 2048 | bytes 16384 | tf_op jit(solution)/shard_map/psum | solution.py:596
  531.8 37.9 %psum.63 = f32[3,16,256]{2,1,0:T(8,128)S(1)} all-reduce(f32[3,16,256]{2,1,0:T(8,128)S(1)} %add.93), channel_id=1, replica_groups=mesh['dp'=8,'mp'=4] {'dp'}, use_global_device_ids=true, to_apply=%region_24.25 | all-reduce | flops 12288 | bytes 98304 | tf_op jit(solution)/shard_map/psum | solution.py:590
  571.1 105.0 %all-reduce.4.cloned.1.call-done = (bf16[1024,256]{1,0:T(8,128)(2,1)}, bf16[1024,256]{1,0:T(8,128)(2,1)}, bf16[256,1024]{1,0:T(8,128)(2,1)}, bf16[1024,1024]{1,0:T(8,128)(2,1)}, bf16[1024,1024]{1,0:T(8,128)(2,1)}) async-done(((bf16[1024,256]{1,0:T(8,128)(2,1)}, bf16[1024,256]{1,0:T(8,128)(2,1)}, bf16[256,1024]{1,0:T(8,128)(2,1)}, bf16[1024,1024]{1,0:T(8,128)(2,1)}, bf16[1024,1024]{1,0:T(8,128)(2,1)}), ...) | async-done | bytes 5767184 | tf_op jit(solution)/shard_map/psum | solution.py:586
  676.1 2.2 convert_element_type.145
  682.5 4.4 convert_element_type.151
  687.0 2.5 convert_element_type.153
  689.5 32.5 %reduce-scatter.11.cloned.1.call-done = bf16[2048,256]{1,0:T(8,128)(2,1)} async-done(((bf16[2048,1024]{1,0:T(8,128)(2,1)}), bf16[2048,256]{1,0:T(8,128)(2,1)}) %reduce-scatter.11.cloned.1.call-update) | async-done | bytes 1048592 | tf_op jit(solution)/shard_map/reduce_scatter | solution.py:435
  721.9 2.9 add_convert_fusion.1
  (204 shorter events, 28.5 us)
Async XLA Ops:
  7.2 244.1 %copy-start = (bf16[1024,1024]{1,0:T(8,128)(2,1)S(1)}, bf16[1024,1024]{1,0:T(8,128)(2,1)}, u32[]{:S(2)}) copy-start(bf16[1024,1024]{1,0:T(8,128)(2,1)} %param.25) | copy-start | bytes 6291460
  7.2 46.1 %copy-start.50 = (f32[1024]{0:T(1024)S(1)}, f32[1024]{0:T(1024)}, u32[]{:S(2)}) copy-start(f32[1024]{0:T(1024)} %param.19) | copy-start | bytes 12292
  7.2 40.1 %all-gather.7.cloned.1.call-start = ((), (), s32[]{:S(2)}) async-start(), calls=%async_computation.4 | async-start | bytes 5242880 | tf_op jit(solution)/shard_map/all_gather | solution.py:431
  7.9 168.8 %reduce-scatter.5.cloned.1.call-start = ((), (), s32[]{:S(2)}) async-start(), calls=%async_computation.5 | async-start | bytes 5242880 | tf_op jit(solution)/shard_map/reduce_scatter | solution.py:435
  9.7 78.2 %copy-start.13 = (f32[16,256]{1,0:T(8,128)}, f32[16,256]{1,0:T(8,128)S(1)}, u32[]{:S(2)}) copy-start(f32[16,256]{1,0:T(8,128)S(1)} %get-tuple-element.101.far_ref) | copy-start | bytes 49156
  9.7 89.1 %copy-start.17 = (f32[16,256]{1,0:T(8,128)}, f32[16,256]{1,0:T(8,128)S(1)}, u32[]{:S(2)}) copy-start(f32[16,256]{1,0:T(8,128)S(1)} %get-tuple-element.99.far_ref) | copy-start | bytes 49156
  11.2 76.6 %copy-start.34 = (f32[16,256]{1,0:T(8,128)}, f32[16,256]{1,0:T(8,128)S(1)}, u32[]{:S(2)}) copy-start(f32[16,256]{1,0:T(8,128)S(1)} %negate_bitcast_fusion) | copy-start | bytes 49156
  11.2 43.6 %copy-start.32 = (bf16[1024,256]{1,0:T(8,128)(2,1)S(1)}, bf16[1024,256]{1,0:T(8,128)(2,1)}, u32[]{:S(2)}) copy-start(bf16[1024,256]{1,0:T(8,128)(2,1)} %param.21) | copy-start | bytes 1572868
  53.4 41.8 %copy-start.58 = (bf16[1024,256]{1,0:T(8,128)(2,1)S(1)}, bf16[1024,256]{1,0:T(8,128)(2,1)}, u32[]{:S(2)}) copy-start(bf16[1024,256]{1,0:T(8,128)(2,1)} %param.22) | copy-start | bytes 1572868
  54.8 41.6 %copy-start.26 = (bf16[2048,1024]{1,0:T(8,128)(2,1)}, bf16[2048,1024]{1,0:T(8,128)(2,1)S(1)}, u32[]{:S(2)}) copy-start(bf16[2048,1024]{1,0:T(8,128)(2,1)S(1)} %fusion.19) | copy-start | bytes 12582916
  56.2 40.3 %copy-start.3 = (f32[512,256]{1,0:T(8,128)}, f32[512,256]{1,0:T(8,128)S(1)}, u32[]{:S(2)}) copy-start(f32[512,256]{1,0:T(8,128)S(1)} %slice.115.u_in) | copy-start | bytes 1572868
  91.7 32.0 %collective-permute-start = (bf16[128,256]{1,0:T(8,128)(2,1)S(1)}, bf16[128,256]{1,0:T(8,128)(2,1)S(1)}, u32[]{:S(2)}, u32[]{:S(2)}) collective-permute-start(bf16[128,256]{1,0:T(8,128)(2,1)S(1)} %slice.97), channel_id=1, source_target_pairs={{0,4},{4,8},{8,12},{12,16},{16,20},{20,24},{24,28},{1,5},{5,9},{9,... | collective-permute-start | bytes 196616 | tf_op jit(solution)/shard_map/ppermute | solution.py:443
  96.4 31.9 %copy-start.31 = (bf16[256,1024]{1,0:T(8,128)(2,1)S(1)}, bf16[256,1024]{1,0:T(8,128)(2,1)}, u32[]{:S(2)}) copy-start(bf16[256,1024]{1,0:T(8,128)(2,1)} %param.23) | copy-start | bytes 1572868
  96.7 27.1 %collective-permute-start.1 = (bf16[128,256]{1,0:T(8,128)(2,1)S(1)}, bf16[128,256]{1,0:T(8,128)(2,1)S(1)}, u32[]{:S(2)}, u32[]{:S(2)}) collective-permute-start(bf16[128,256]{1,0:T(8,128)(2,1)S(1)} %slice.98), channel_id=1, source_target_pairs={{0,4},{4,8},{8,12},{12,16},{16,20},{20,24},{24,28},{1,5},{5,9},{9,... | collective-permute-start | bytes 196616 | tf_op jit(solution)/shard_map/ppermute | solution.py:443
  98.8 28.5 %copy-start.15 = (f32[16,256]{1,0:T(8,128)}, f32[16,256]{1,0:T(8,128)S(1)}, u32[]{:S(2)}) copy-start(f32[16,256]{1,0:T(8,128)S(1)} %broadcast_in_dim.27.first_ref.last_ref) | copy-start | bytes 49156
  131.6 89.9 %copy-start.52 = (f32[1024]{0:T(1024)S(1)}, f32[1024]{0:T(1024)}, u32[]{:S(2)}) copy-start(f32[1024]{0:T(1024)} %param.20) | copy-start | bytes 12292
  131.6 83.1 %all-gather.9.cloned.1.call-start = ((), (), s32[]{:S(2)}) async-start(), calls=%async_computation.6 | async-start | bytes 5242880 | tf_op jit(solution)/shard_map/all_gather | solution.py:431
  179.5 71.7 %all-gather.11.cloned.1.call-start = ((), (), s32[]{:S(2)}) async-start(), calls=%async_computation.8 | async-start | bytes 5242880 | tf_op jit(solution)/shard_map/all_gather | solution.py:431
  180.1 153.7 %reduce-scatter.9.cloned.1.call-start = ((), (), s32[]{:S(2)}) async-start(), calls=%async_computation.9 | async-start | bytes 5242880 | tf_op jit(solution)/shard_map/reduce_scatter | solution.py:435
  251.3 26.7 %copy-start.22 = (bf16[2048,1024]{1,0:T(8,128)(2,1)S(1)}, bf16[2048,1024]{1,0:T(8,128)(2,1)}, u32[]{:S(2)}) copy-start(bf16[2048,1024]{1,0:T(8,128)(2,1)} %all-gather.9.cloned.1.call-done) | copy-start | bytes 12582916
  251.3 26.7 %copy-start.48 = (f32[2048]{0:T(1024)S(1)}, f32[2048]{0:T(1024)}, u32[]{:S(2)}) copy-start(f32[2048]{0:T(1024)} %copy-done.47) | copy-start | bytes 24580
  251.3 26.7 %copy-start.57 = (bf16[1024,1024]{1,0:T(8,128)(2,1)S(1)}, bf16[1024,1024]{1,0:T(8,128)(2,1)}, u32[]{:S(2)}) copy-start(bf16[1024,1024]{1,0:T(8,128)(2,1)} %param.24) | copy-start | bytes 6291460
  289.2 83.8 %all-gather.13.cloned.1.call-start = ((), (), s32[]{:S(2)}) async-start(), calls=%async_computation.10 | async-start | bytes 5242880 | tf_op jit(solution)/shard_map/all_gather | solution.py:431
  336.6 147.8 %reduce-scatter.7.cloned.1.call-start = ((), (), s32[]{:S(2)}) async-start(), calls=%async_computation.7 | async-start | bytes 5242880 | tf_op jit(solution)/shard_map/reduce_scatter | solution.py:435
  355.1 320.9 %all-reduce.4.cloned.1.call-start = ((), (), s32[]{:S(2)}) async-start(), calls=%async_computation.12 | async-start | bytes 11534336 | tf_op jit(solution)/shard_map/psum | solution.py:586
  356.5 9.6 %copy-start.23 = (bf16[2048,1024]{1,0:T(8,128)(2,1)S(1)}, bf16[2048,1024]{1,0:T(8,128)(2,1)}, u32[]{:S(2)}) copy-start(bf16[2048,1024]{1,0:T(8,128)(2,1)} %all-gather.9.cloned.1.call-done) | copy-start | bytes 12582916
  356.5 9.6 %copy-start.49 = (f32[2048]{0:T(1024)S(1)}, f32[2048]{0:T(1024)}, u32[]{:S(2)}) copy-start(f32[2048]{0:T(1024)} %copy-done.47) | copy-start | bytes 24580
  356.5 9.6 %copy-start.61 = (bf16[2048,1024]{1,0:T(8,128)(2,1)S(1)}, bf16[2048,1024]{1,0:T(8,128)(2,1)}, u32[]{:S(2)}) copy-start(bf16[2048,1024]{1,0:T(8,128)(2,1)} %copy-done.60) | copy-start | bytes 12582916
  373.0 9.6 %copy-start.6 = (bf16[1536,256]{1,0:T(8,128)(2,1)S(1)}, bf16[1536,256]{1,0:T(8,128)(2,1)}, u32[]{:S(2)}) copy-start(bf16[1536,256]{1,0:T(8,128)(2,1)} %copy-done.5) | copy-start | bytes 2359300
  373.0 9.6 %copy-start.8 = (bf16[1536,256]{1,0:T(8,128)(2,1)S(1)}, bf16[1536,256]{1,0:T(8,128)(2,1)}, u32[]{:S(2)}) copy-start(bf16[1536,256]{1,0:T(8,128)(2,1)} %copy-done.7) | copy-start | bytes 2359300
  373.0 20.0 %copy-start.27 = (bf16[2048,1024]{1,0:T(8,128)(2,1)S(1)}, bf16[2048,1024]{1,0:T(8,128)(2,1)}, u32[]{:S(2)}) copy-start(bf16[2048,1024]{1,0:T(8,128)(2,1)} %copy-done.26) | copy-start | bytes 12582916
  376.8 18.2 %copy-start.29 = (bf16[2048,256]{1,0:T(8,128)(2,1)S(1)}, bf16[2048,256]{1,0:T(8,128)(2,1)}, u32[]{:S(2)}) copy-start(bf16[2048,256]{1,0:T(8,128)(2,1)} %copy-done.28) | copy-start | bytes 3145732
  379.8 45.5 %collective-permute-start.2 = (bf16[128,256]{1,0:T(8,128)(2,1)S(1)}, bf16[128,256]{1,0:T(8,128)(2,1)S(1)}, u32[]{:S(2)}, u32[]{:S(2)}) collective-permute-start(bf16[128,256]{1,0:T(8,128)(2,1)S(1)} %slice.145), channel_id=1, source_target_pairs={{4,0},{8,4},{12,8},{16,12},{20,16},{24,20},{28,24},{5,1},{9,5},{13... | collective-permute-start | bytes 196616 | tf_op jit(solution)/shard_map/ppermute | solution.py:443
  381.1 44.2 %collective-permute-start.3 = (bf16[128,256]{1,0:T(8,128)(2,1)S(1)}, bf16[128,256]{1,0:T(8,128)(2,1)S(1)}, u32[]{:S(2)}, u32[]{:S(2)}) collective-permute-start(bf16[128,256]{1,0:T(8,128)(2,1)S(1)} %slice.144), channel_id=1, source_target_pairs={{4,0},{8,4},{12,8},{16,12},{20,16},{24,20},{28,24},{5,1},{9,5},{13... | collective-permute-start | bytes 196616 | tf_op jit(solution)/shard_map/ppermute | solution.py:443
  395.0 30.3 %copy-start.14 = (f32[16,256]{1,0:T(8,128)S(1)}, f32[16,256]{1,0:T(8,128)}, u32[]{:S(2)}) copy-start(f32[16,256]{1,0:T(8,128)} %copy-done.13) | copy-start | bytes 49156
  395.0 66.6 %copy-start.35 = (f32[16,256]{1,0:T(8,128)S(1)}, f32[16,256]{1,0:T(8,128)}, u32[]{:S(2)}) copy-start(f32[16,256]{1,0:T(8,128)} %copy-done.34) | copy-start | bytes 49156
  395.0 66.6 %copy-start.54 = (f32[8]{0:T(128)S(1)}, f32[8]{0:T(128)}, u32[]{:S(2)}) copy-start(f32[8]{0:T(128)} %multiply_convert_fusion.1) | copy-start | bytes 100
  395.1 66.6 %copy-start.55 = (pred[8]{0:T(512)(128)(4,1)S(1)}, pred[8]{0:T(512)(128)(4,1)}, u32[]{:S(2)}) copy-start(pred[8]{0:T(512)(128)(4,1)} %fusion.42) | copy-start | bytes 28
  395.1 66.7 %copy-start.4 = (f32[512,256]{1,0:T(8,128)S(1)}, f32[512,256]{1,0:T(8,128)}, u32[]{:S(2)}) copy-start(f32[512,256]{1,0:T(8,128)} %copy-done.3) | copy-start | bytes 1572868
  395.1 66.7 %copy-start.12 = (f32[8,2,128,128]{3,2,1,0:T(8,128)S(1)}, f32[8,2,128,128]{3,2,1,0:T(8,128)}, u32[]{:S(2)}) copy-start(f32[8,2,128,128]{3,2,1,0:T(8,128)} %copy-done.11) | copy-start | bytes 3145732
  473.9 248.0 %reduce-scatter.11.cloned.1.call-start = ((), (), s32[]{:S(2)}) async-start(), calls=%async_computation.11 | async-start | bytes 5242880 | tf_op jit(solution)/shard_map/reduce_scatter | solution.py:435
  484.4 85.4 %copy-start.33 = (f32[256,16]{0,1:T(8,128)S(1)}, f32[256,16]{0,1:T(8,128)}, u32[]{:S(2)}) copy-start(f32[256,16]{0,1:T(8,128)} %param.26) | copy-start | bytes 49156
  484.4 85.4 %copy-start.42 = (f32[256,16]{0,1:T(8,128)S(1)}, f32[256,16]{0,1:T(8,128)}, u32[]{:S(2)}) copy-start(f32[256,16]{0,1:T(8,128)} %param.29) | copy-start | bytes 49156
  484.4 85.4 %copy-start.45 = (f32[256,16]{0,1:T(8,128)S(1)}, f32[256,16]{0,1:T(8,128)}, u32[]{:S(2)}) copy-start(f32[256,16]{0,1:T(8,128)} %param.28) | copy-start | bytes 49156
  484.4 86.0 %copy-start.37 = (f32[16,256]{1,0:T(8,128)S(1)}, f32[16,256]{1,0:T(8,128)}, u32[]{:S(2)}) copy-start(f32[16,256]{1,0:T(8,128)} %copy-done.36) | copy-start | bytes 49156
  484.4 86.0 %copy-start.46 = (f32[256,16]{0,1:T(8,128)S(1)}, f32[256,16]{0,1:T(8,128)}, u32[]{:S(2)}) copy-start(f32[256,16]{0,1:T(8,128)} %param.27) | copy-start | bytes 49156
  676.1 10.9 %copy-start.30 = (bf16[1024,1024]{1,0:T(8,128)(2,1)S(1)}, bf16[1024,1024]{1,0:T(8,128)(2,1)}, u32[]{:S(2)}) copy-start(bf16[1024,1024]{1,0:T(8,128)(2,1)} %get-tuple-element.89) | copy-start | bytes 6291460
  676.1 45.8 %copy-start.25 = (bf16[2048,256]{1,0:T(8,128)(2,1)S(1)}, bf16[2048,256]{1,0:T(8,128)(2,1)}, u32[]{:S(2)}) copy-start(bf16[2048,256]{1,0:T(8,128)(2,1)} %param.31) | copy-start | bytes 3145732
  (27 other events, 101.7 us)
Sparse Core Ops, SparseCore 0:
  9.6 37.7 all-gather.6
  131.7 44.9 reduce-scatter.4
  179.7 35.0 all-gather.8
  216.2 35.0 all-gather.10
  289.3 44.4 reduce-scatter.8
  336.8 35.0 all-gather.12
  374.9 44.4 reduce-scatter.6
  474.0 202.0 all-reduce.3
  678.6 43.2 reduce-scatter.10

commit v2 on v1

--- a/solution.py
+++ b/solution.py
@@ -427,6 +427,259 @@
         name=name)(starts, q, k, v, g, lse)
 
 
+ROWS = 256
+SUB = 32
+DEEP = 3
+MESH = pl.DeviceIdType.MESH
+
+
+def group_of_four():
+    me = lax.axis_index("mp")
+    mate = me + 1 - 2 * (me % 2)
+    return me, mate, (me + 2) % 4, (mate + 2) % 4
+
+
+def greet_group():
+    _, mate, over, _ = group_of_four()
+    dp = lax.axis_index("dp")
+    barrier = pltpu.get_barrier_semaphore()
+    for peer in (mate, over):
+        pl.semaphore_signal(barrier, inc=1, device_id=(dp, peer), device_id_type=MESH)
+    pl.semaphore_wait(barrier, 2)
+
+
+class Mover:
+    def __init__(self, send_sem, recv_sem):
+        self.send_sem, self.recv_sem = send_sem, recv_sem
+        self.dp = lax.axis_index("dp")
+
+    def copy(self, src, dst, kind, c, peer):
+        return pltpu.make_async_remote_copy(
+            src_ref=src, dst_ref=dst, send_sem=self.send_sem.at[kind, c], recv_sem=self.recv_sem.at[kind, c],
+            device_id=(self.dp, peer), device_id_type=MESH)
+
+
+class Gather:
+    def __init__(self, mover, base, full, rows):
+        self.mover, self.base, self.full, self.rows = mover, base, full, rows
+        self.me, self.mate, self.over, self.far = group_of_four()
+
+    def at(self, owner, c):
+        return self.full.at[owner, pl.ds(pl.multiple_of(c * self.rows, self.rows), self.rows)]
+
+    def near(self, c):
+        return self.mover.copy(self.at(self.me, c), self.at(self.me, c), self.base, c, self.mate)
+
+    def across(self, c):
+        return self.mover.copy(self.at(self.me, c), self.at(self.me, c), self.base + 1, c, self.over)
+
+    def onward(self, c):
+        return self.mover.copy(self.at(self.over, c), self.at(self.over, c), self.base + 2, c, self.mate)
+
+    def start(self, c):
+        self.across(c).start()
+        self.near(c).start()
+
+    def forward(self, c):
+        self.across(c).wait_recv()
+        self.onward(c).start()
+
+    def finish(self, c):
+        self.near(c).wait()
+        self.across(c).wait_send()
+        self.onward(c).wait()
+
+
+class Scatter:
+    def __init__(self, mover, base, part, near, across, joint):
+        self.mover, self.base = mover, base
+        self.part, self.near, self.across, self.joint = part, near, across, joint
+        self.me, self.mate, self.over, self.far = group_of_four()
+
+    def to_join(self, c):
+        return self.mover.copy(self.part.at[c % DEEP, self.far], self.near.at[c, 1], self.base + 1, c, self.mate)
+
+    def to_keep(self, c):
+        return self.mover.copy(self.part.at[c % DEEP, self.mate], self.near.at[c, 0], self.base, c, self.mate)
+
+    def joined(self, c):
+        return self.mover.copy(self.joint.at[c % DEEP], self.across.at[c], self.base + 2, c, self.over)
+
+    def start(self, c, parts):
+        for d in range(4):
+            self.part[c % DEEP, d] = parts(d).astype(jnp.bfloat16)
+        self.to_join(c).start()
+        self.to_keep(c).start()
+
+    def combine(self, c):
+        s = c % DEEP
+        self.to_join(c).wait_recv()
+        self.joint[s] = (self.part[s, self.over].astype(jnp.float32) + self.near[c, 1].astype(jnp.float32)).astype(jnp.bfloat16)
+        self.joined(c).start()
+
+    def finish(self, c):
+        self.to_join(c).wait_send()
+        self.to_keep(c).wait()
+        self.joined(c).wait()
+        return (self.part[c % DEEP, self.me].astype(jnp.float32) + self.near[c, 0].astype(jnp.float32)
+                + self.across[c].astype(jnp.float32))
+
+
+def mm(left, right, left_dim, right_dim):
+    return lax.dot_general(left, right, (((left_dim,), (right_dim,)), ((), ())), preferred_element_type=jnp.float32)
+
+
+def cut(d, width):
+    return slice(d * width, (d + 1) * width)
+
+
+def normed(full, c, sub, rows):
+    first = pl.multiple_of(c * rows + sub * SUB, SUB)
+    return jnp.concatenate([full[d, pl.ds(first, SUB), :].astype(jnp.float32) for d in range(4)], axis=1)
+
+
+def middle_kernel(chunks, att_ref, tok_ref, cot_ref, w_out_ref, w_up_ref, w_down_ref, gain_ref,
+                  result_ref, gm_ref, gatt_ref, gdown_ref, gup_ref, gout_ref, ggain_ref,
+                  mid_full, gm_full, mid_ref, part, near, across, joint, n2_ref, act_ref, gpre_ref, pre_ref, gact_ref, mean_ref, inv_ref,
+                  send_sem, recv_sem):
+    width = att_ref.shape[1]
+    rows = ROWS
+    me = lax.axis_index("mp")
+    mover = Mover(send_sem, recv_sem)
+    sums = [Scatter(mover, 3 * r, part.at[r], near.at[r], across.at[r], joint.at[r]) for r in range(3)]
+    gather_mid = Gather(mover, 9, mid_full, rows)
+    gather_gm = Gather(mover, 12, gm_full, rows)
+    greet_group()
+    gdown_ref[...] = jnp.zeros_like(gdown_ref)
+    gup_ref[...] = jnp.zeros_like(gup_ref)
+    gout_ref[...] = jnp.zeros_like(gout_ref)
+    ggain_ref[...] = jnp.zeros_like(ggain_ref)
+
+    def span(c):
+        return pl.ds(pl.multiple_of(c * rows, rows), rows)
+
+    def project(c):
+        att = att_ref[span(c), :]
+        sums[0].start(c, lambda d: mm(att, w_out_ref[:, cut(d, width)], 1, 0))
+
+    def add_middle(c):
+        middle = tok_ref[span(c), :].astype(jnp.float32) + sums[0].finish(c)
+        mid_ref[span(c), :] = middle
+        mid_full[me, span(c), :] = middle.astype(jnp.bfloat16)
+        gather_mid.start(c)
+
+    def feed_forward(c):
+        gather_mid.finish(c)
+
+        @pl.loop(0, rows // SUB)
+        def _(sub):
+            mine = pl.ds(pl.multiple_of(sub * SUB, SUB), SUB)
+            v = normed(mid_full, c, sub, rows)
+            mean = jnp.mean(v, axis=1, keepdims=True)
+            centred = v - mean
+            inv = lax.rsqrt(jnp.mean(centred * centred, axis=1, keepdims=True) + EPS)
+            mean_ref[mine, :] = mean
+            inv_ref[mine, :] = inv
+            n2_ref[mine, :] = (centred * inv * gain_ref[...]).astype(jnp.bfloat16)
+
+        cot = cot_ref[span(c), :]
+        pre_ref[...] = mm(n2_ref[...], w_up_ref[...], 1, 0)
+        gact_ref[...] = mm(cot, w_down_ref[...], 1, 1)
+
+        @pl.loop(0, rows // SUB)
+        def _(sub):
+            mine = pl.ds(pl.multiple_of(sub * SUB, SUB), SUB)
+            v = pre_ref[mine, :]
+            cdf = 0.5 * (1.0 + lax.erf(v * (0.5**0.5)))
+            act_ref[mine, :] = (v * cdf).astype(jnp.bfloat16)
+            slope = cdf + v * (jnp.exp(-0.5 * v * v) * 0.3989422804014327)
+            gpre_ref[mine, :] = (slope * gact_ref[mine, :]).astype(jnp.bfloat16)
+
+        sums[1].start(c, lambda d: mm(act_ref[...], w_down_ref[:, cut(d, width)], 1, 0))
+        gact_ref[...] = mm(gpre_ref[...], w_up_ref[...], 1, 1)
+
+        @pl.loop(0, rows // SUB)
+        def _(sub):
+            mine = pl.ds(pl.multiple_of(sub * SUB, SUB), SUB)
+            xhat = (normed(mid_full, c, sub, rows) - mean_ref[mine, :]) * inv_ref[mine, :]
+            up = gact_ref[mine, :]
+            both = up * xhat
+            ggain_ref[...] += jnp.sum(both.reshape(SUB // 8, 8, both.shape[1]), axis=0)
+            scaled = up * gain_ref[...]
+            plain = jnp.mean(scaled, axis=1, keepdims=True)
+            cross = jnp.mean(scaled * xhat, axis=1, keepdims=True)
+            gact_ref[mine, :] = inv_ref[mine, :] * (scaled - plain - xhat * cross)
+
+        sums[2].start(c, lambda d: gact_ref[:, cut(d, width)])
+        gdown_ref[...] += mm(act_ref[...], cot, 0, 0)
+        gup_ref[...] += mm(n2_ref[...], gpre_ref[...], 0, 0)
+
+    def finish_sums(c):
+        own = pl.ds(pl.multiple_of(me * width, width), width)
+        gm = cot_ref[span(c), own].astype(jnp.float32) + sums[2].finish(c)
+        gm_ref[span(c), :] = gm
+        gm_full[me, span(c), :] = gm.astype(jnp.bfloat16)
+        gather_gm.start(c)
+        result_ref[span(c), :] = (mid_ref[span(c), :] + sums[1].finish(c)).astype(result_ref.dtype)
+
+    def back_project(c):
+        gather_gm.finish(c)
+        att = att_ref[span(c), :]
+        total = None
+        for d in range(4):
+            gm = gm_full[d, span(c), :]
+            gout_ref[:, cut(d, width)] += mm(att, gm, 0, 0)
+            term = mm(gm, w_out_ref[:, cut(d, width)], 1, 1)
+            total = term if total is None else total + term
+        gatt_ref[span(c), :] = total.astype(gatt_ref.dtype)
+
+    def combine_late(c):
+        sums[2].combine(c)
+        sums[1].combine(c)
+
+    stages = [(add_middle, 2), (finish_sums, 6), (sums[0].combine, 1), (combine_late, 5), (gather_mid.forward, 3),
+              (gather_gm.forward, 7), (project, 0), (feed_forward, 4), (back_project, 8)]
+
+    @pl.loop(0, chunks + 8)
+    def _(i):
+        for stage, lag in stages:
+            @pl.when(jnp.logical_and(i >= lag, i < chunks + lag))
+            def _(stage=stage, lag=lag):
+                stage(i - lag)
+
+
+def middle_phase(att, tok, cot_full, w_out, w_up, w_down, gain):
+    rows, width = att.shape
+    full = cot_full.shape[1]
+    hidden = w_up.shape[1]
+    chunks = rows // ROWS
+    bf = jnp.bfloat16
+
+    def out(shape, dtype):
+        return jax.ShapeDtypeStruct(shape, dtype)
+
+    def buf(*shape, dtype=bf):
+        return pltpu.VMEM(shape, dtype)
+
+    return pl.pallas_call(
+        functools.partial(middle_kernel, chunks),
+        out_shape=(out((rows, width), bf), out((rows, width), jnp.float32), out((rows, width), bf),
+                   out((hidden, full), jnp.float32), out((full, hidden), jnp.float32), out((width, full), jnp.float32),
+                   out((8, full), jnp.float32)),
+        in_specs=[VMEM] * 7, out_specs=(VMEM,) * 7,
+        scratch_shapes=[
+            buf(4, rows, width), buf(4, rows, width), buf(rows, width, dtype=jnp.float32),
+            buf(3, DEEP, 4, ROWS, width), buf(3, chunks, 2, ROWS, width), buf(3, chunks, ROWS, width), buf(3, DEEP, ROWS, width),
+            buf(ROWS, full), buf(ROWS, hidden), buf(ROWS, hidden),
+            buf(ROWS, hidden, dtype=jnp.float32), buf(ROWS, hidden, dtype=jnp.float32),
+            buf(ROWS, 1, dtype=jnp.float32), buf(ROWS, 1, dtype=jnp.float32),
+            pltpu.SemaphoreType.DMA((15, chunks)), pltpu.SemaphoreType.DMA((15, chunks)),
+        ],
+        compiler_params=pltpu.CompilerParams(collective_id=0, has_side_effects=True, vmem_limit_bytes=60 * 2**20),
+        cost_estimate=pl.CostEstimate(flops=30 * 10**9, bytes_accessed=30 * 10**6, transcendentals=4 * 10**6),
+        name="middle_phase")(att, tok, cot_full, w_out, w_up, w_down, gain)
+
+
 def gather_features(values_in):
     return lax.all_gather(values_in, "mp", axis=1, tiled=True)
 
@@ -531,28 +784,10 @@
     att_short, lse_short = attend(short_starts, q_short, k_short, v_short, 0, "attend_short")
     att_long, lse_long = attend(long_low, q_long, k_long, v_long, CTX, "attend_long")
     attended = jnp.concatenate([att_long, att_short])
-    middle = tokens.astype(jnp.float32) + reduce_features(
-        jnp.dot(attended, w_out, preferred_element_type=jnp.float32)
-    )
-    middle_full = gather_features(middle.astype(low)).astype(jnp.float32)
-    normed_two, inverse_two, hidden_two = norm_forward(middle_full, gain_two)
-    normed_two_low = hidden_two.astype(low)
-    pre_act = jnp.dot(normed_two_low, w_up, preferred_element_type=jnp.float32)
-    act_value, act_pull = jax.vjp(gelu_exact, pre_act)
-    act_low = act_value.astype(low)
-    result = (
-        middle + reduce_features(jnp.dot(act_low, w_down, preferred_element_type=jnp.float32))
-    ).astype(low)
-    grad_w_down = dot(act_low, cotangent_full, ((0,), (0,)))
-    grad_act = dot(cotangent_full, w_down, ((1,), (1,)))
-    grad_pre = act_pull(grad_act)[0].astype(low)
-    grad_w_up = dot(normed_two_low, grad_pre, ((0,), (0,)))
-    grad_hidden_two = dot(grad_pre, w_up, ((1,), (1,)))
-    middle_part, grad_gain_two = norm_backward(grad_hidden_two, normed_two, inverse_two, gain_two)
-    grad_middle = cotangent.astype(jnp.float32) + reduce_features(middle_part)
-    grad_mid_full = gather_features(grad_middle.astype(low))
-    grad_w_out = dot(attended, grad_mid_full, ((0,), (0,)))
-    grad_attended = dot(grad_mid_full, w_out, ((1,), (1,))).astype(low)
+    result, grad_middle, grad_attended, grad_w_down, grad_w_up, grad_w_out, gain_parts = middle_phase(
+        attended, tokens, cotangent_full, w_out, w_up, w_down, gain_two[None]
+    )
+    grad_gain_two = jnp.sum(gain_parts, axis=0)
 
     gq_long, gk_long, gv_long = attend_back(
         long_low, q_long, k_long, v_long, grad_attended[:LONG_DEV], lse_long, CTX, "attend_back_long"

time: 738 us -> 632 us (0.86)
  waiting for transfers between devices: 322 us -> 178 us
  Pallas kernels: 78 us -> 218 us
  matrix products: 92 us -> 13.8 us
  other arithmetic: 62 us -> 33.4 us
    pallas_call x0 -> x1, Pallas kernels: none -> 140 us  [middle_phase(): pl.pallas_call(functools.partial(middle_kernel, chunks), out_shape=(out((...]
    reduce_scatter x4 -> x1, waiting for transfers between devices: 122 us -> 35.7 us  [reduce_features(): lax.psum_scatter(values_in.astype(jnp.bfloat16), 'mp', scatter_dimension=...]
    dot_general x10 -> x4, matrix products: 70.9 us -> 11.3 us  [dot(): lax.dot_general(left, right, ((dims[0], dims[1]), ((), ())), preferred_el...]
    all_gather x4 -> x2, waiting for transfers between devices: 93.4 us -> 34.4 us  [gather_features(): return lax.all_gather(values_in, 'mp', axis=1, tiled=True)]
    dot_general x3 -> x0, matrix products: 18.4 us -> none  [the longest x1 8.32 us: on_device(): jnp.dot(act_low, w_down, preferred_element_type=jnp.float32)]
    convert_element_type x4 -> x3, other arithmetic: 18.5 us -> 4.3 us  [on_device(): g.astype(low)]
  transfers between devices with their start and end apart: 13 -> 8, of which waited for: 7 -> 3; matrix products, arithmetic and copies ran while one was open for 13% -> 7% of each run, Pallas kernels for 10% -> 10%
where the time goes in v2:
time: 632 us; the launch traced here: 626 us
  Pallas kernels  218 us (34%)
  waiting for transfers between devices  178 us (28%)
  blocking collectives  149 us (24%)
  other arithmetic  33.4 us (5%)
  between operations  14.9 us (2%)
  matrix products  13.8 us (2%)
  local copies, waits for them, and re-layouts  11 us (2%)
  starting transfers between devices  8.47 us (1%)
    pallas_call x1, Pallas kernels, middle_phase(): pl.pallas_call(functools.partial(middle_kernel, chunks), out_shape=(out((...  140 us
    psum x1, waiting for transfers between devices, on_device(): lax.psum(tuple((g.astype(low) for g in (grad_w_in, grad_w_query, grad_w_o...  106 us
    psum x1, blocking collectives, on_device(): lax.psum((grad_gain_one, grad_gain_two), ('dp', 'mp'))  45.1 us
    psum x1, blocking collectives, on_device(): sums = lax.psum(sums, 'dp')  38.3 us
    reduce_scatter x1, waiting for transfers between devices, reduce_features(): lax.psum_scatter(values_in.astype(jnp.bfloat16), 'mp', scatter_dimension=...  35.7 us
    all_gather x1, blocking collectives, on_device(): grad_pieces = lax.all_gather(local_in[None], 'dp', axis=0, tiled=True)  34.7 us
    all_gather x2, waiting for transfers between devices, gather_features(): return lax.all_gather(values_in, 'mp', axis=1, tiled=True)  34.4 us
    pallas_call x2, Pallas kernels, ssm_backward(): pl.pallas_call(functools.partial(backward_kernel, span, tiles), out_shape...  33.8 us
  transfers between devices with their start and end apart: 8, of which 3 were waited for; matrix products, arithmetic and copies ran while one was open for 7% of the time, Pallas kernels for 10%

profile of v2, /device:TPU:0, one launch (start us, length us, event | category | flops | bytes accessed | tf_op | source)
XLA Modules:
  0.0 626.3 jit_solution(1474764743310609856)
XLA Ops:
  13.0 34.4 %all-gather.5.cloned.1.call-done = bf16[2048,1024]{1,0:T(8,128)(2,1)} async-done(((bf16[2048,256]{1,0:T(8,128)(2,1)}), bf16[2048,1024]{1,0:T(8,128)(2,1)}) %all-gather.5.cloned.1.call-update) | async-done | bytes 4194320 | tf_op jit(solution)/shard_map/all_gather | solution.py:684
  47.3 3.0 convert_reduce_fusion
  50.8 1.4 fusion.12
  52.2 1.4 fusion.6
  53.7 1.3 fusion.23
  55.0 1.0 ssm_ends.1
  56.0 30.6 %all-gather = f32[128,256]{1,0:T(8,128)S(1)} all-gather(f32[16,256]{1,0:T(8,128)S(1)} %ssm_ends.1), channel_id=2, replica_groups=mesh['dp'=8,'mp'=4] {'dp'}, dimensions={0}, use_global_device_ids=true | all-gather | bytes 147456 | tf_op jit(solution)/shard_map/all_gather | solution.py:774
  86.7 3.8 ssm_long.1
  90.5 1.0 copy-done.11
  91.5 3.4 collective-permute-start.1
  94.8 1.3 convolution_convert_fusion
  96.4 2.1 collective-permute-start
  98.5 13.9 %ssm_short.1 = (bf16[1536,256]{1,0:T(8,128)(2,1)S(1)}, bf16[1536,256]{1,0:T(8,128)(2,1)S(1)}, f32[24,2,128,128]{3,2,1,0:T(8,128)}) custom-call(s32[2]{0:T(128)S(1)} %pad_add_fusion.bounds_ref.starts_ref, f32[1536,256]{1,0:T(8,128)S(1)} %slice.117.u_in, f32[3,16,256]{2,1,0:T(8,128)S(1)} %pad_maximum_fusion.1.par_ref, ...), custom_call_target="tpu_custom_call" | custom-call | tf_op jit(solution)/shard_map/ssm_short/pallas_call | solution.py:295
  112.4 8.9 %attend_short.1 = (bf16[1536,256]{1,0:T(8,128)(2,1)S(1)}, f32[2,1,1536]{2,1,0:T(1,128)S(1)}) custom-call(s32[2]{0:T(128)S(1)} %pad_add_fusion.bounds_ref.starts_ref, bf16[1536,256]{1,0:T(8,128)(2,1)S(1)} %slice.116.q_ref, bf16[1536,256]{1,0:T(8,128)(2,1)S(1)} %get-tuple-element.67.k_ref, bf16[1536,256]{1,0:T(8,128)(2,1)S(1)} %get-tuple-element.68.v_ref), custom_call_target="tpu_custom_call" | custom-call | tf_op jit(solution)/shard_map/attend_short/pallas_call | solution.py:384
  122.3 2.7 attend_long.1
  125.1 1.0 pad_maximum_fusion.att_ref
  126.1 139.6 %middle_phase.1 = (bf16[2048,256]{1,0:T(8,128)(2,1)}, f32[2048,256]{1,0:T(8,128)}, bf16[2048,256]{1,0:T(8,128)(2,1)}, f32[1024,1024]{1,0:T(8,128)}, f32[1024,102...) custom-call(bf16[2048,256]{1,0:T(8,128)(2,1)} %pad_maximum_fusion.att_ref, bf16[2048,256]{1,0:T(8,128)(2,1)} %tok_ref.1, ...), custom_call_target="tpu_custom_call" | custom-call | flops 30000001024 | bytes 30000000 | tf_op jit(solution)/shard_map/middle_phase/pallas_call | solution.py:664
  265.8 1.3 slice.110.g_ref
  267.1 1.0 slice.103.g_ref
  268.1 1.0 copy-done.8
  269.0 1.0 copy-done.10
  270.0 3.1 attend_back_long.1
  273.1 1.3 collective-permute-start.3
  274.5 9.2 %attend_back_short.1 = (bf16[1536,256]{1,0:T(8,128)(2,1)S(1)}, f32[1536,256]{1,0:T(8,128)S(1)}, f32[1536,256]{1,0:T(8,128)S(1)}) custom-call(s32[2]{0:T(128)S(1)} %pad_add_fusion.bounds_ref.starts_ref, bf16[1536,256]{1,0:T(8,128)(2,1)S(1)} %slice.116.q_ref, bf16[1536,256]{1,0:T(8,128)(2,1)S(1)} %copy-done.2, bf16[1536,256]{1,0:T(8,128)(2,1)S(1)} %copy-done.4, ...), custom_call_target="tpu_custom_call" | custom-call | tf_op jit(solution)/shard_map/attend_back_short/pallas_call | solution.py:419
  283.8 2.1 convolution_convert_fusion.1
  286.0 1.6 collective-permute-start.2
  287.6 1.7 convert_element_type.86
  289.3 1.7 convert_element_type.88
  291.9 25.8 %ssm_back_short.1 = (bf16[1536,256]{1,0:T(8,128)(2,1)S(1)}, f32[3,16,256]{2,1,0:T(8,128)S(1)}) custom-call(s32[2]{0:T(128)S(1)} %pad_add_fusion.bounds_ref.starts_ref, f32[1536,256]{1,0:T(8,128)S(1)} %slice.117.u_in, f32[1536,256]{1,0:T(8,128)S(1)} %get-tuple-element.79.gk_in, f32[1536,256]{1,0:T(8,128)S(1)} %get-tuple-element.80.gv_in, ...), custom_call_target="tpu_custom_call" | custom-call | tf_op jit(solution)/shard_map/ssm_back_short/pallas_call | solution.py:318
  317.7 2.2 ssm_adjoint_ends.1
  319.9 34.7 %all-gather.1 = f32[128,256]{1,0:T(8,128)S(1)} all-gather(f32[16,256]{1,0:T(8,128)S(1)} %ssm_adjoint_ends.1), channel_id=3, replica_groups=mesh['dp'=8,'mp'=4] {'dp'}, dimensions={0}, use_global_device_ids=true | all-gather | bytes 147456 | tf_op jit(solution)/shard_map/all_gather | solution.py:802
  354.7 8.0 %ssm_back_long.1 = (bf16[512,256]{1,0:T(8,128)(2,1)S(1)}, f32[3,16,256]{2,1,0:T(8,128)S(1)}) custom-call(s32[1]{0:T(128)} %constant.82.clone.1.bounds_ref, f32[512,256]{1,0:T(8,128)S(1)} %slice.115.u_in, f32[512,256]{1,0:T(8,128)S(1)} %add_dynamic-update-slice_fusion.1.gk_in, f32[512,256]{1,0:T(8,128)S(1)} %add_dynamic-update-slice_fusion.gv_in, ...), custom_call_target="tpu_custom_call" | custom-call | tf_op jit(solution)/shard_map/ssm_back_long/pallas_call | solution.py:318
  362.9 4.3 convolution_convert_fusion.2
  367.2 1.0 copy-done.24
  368.2 1.3 fusion.24
  370.7 3.6 fusion.11
  374.3 4.1 fusion.10
  379.1 45.1 %all-reduce = (f32[1024]{0:T(1024)}, f32[1024]{0:T(1024)}) all-reduce(f32[1024]{0:T(1024)S(1)} %get-tuple-element.91, f32[1024]{0:T(1024)S(1)} %reduce_sum.79), channel_id=1, replica_groups=mesh['dp'=8,'mp'=4] {'dp','mp'}, use_global_device_ids=true, to_apply=%region_9.10 | all-reduce | flops 2048 | bytes 16384 | tf_op jit(solution)/shard_map/psum | solution.py:831
  424.2 38.3 %psum.63 = f32[3,16,256]{2,1,0:T(8,128)S(1)} all-reduce(f32[3,16,256]{2,1,0:T(8,128)S(1)} %add.70), channel_id=1, replica_groups=mesh['dp'=8,'mp'=4] {'dp'}, use_global_device_ids=true, to_apply=%region_17.18 | all-reduce | flops 12288 | bytes 98304 | tf_op jit(solution)/shard_map/psum | solution.py:825
  463.8 106.2 %all-reduce.4.cloned.1.call-done = (bf16[1024,256]{1,0:T(8,128)(2,1)}, bf16[1024,256]{1,0:T(8,128)(2,1)}, bf16[256,1024]{1,0:T(8,128)(2,1)}, bf16[1024,1024]{1,0:T(8,128)(2,1)}, bf16[1024,1024]{1,0:T(8,128)(2,1)}) async-done(((bf16[1024,256]{1,0:T(8,128)(2,1)}, bf16[1024,256]{1,0:T(8,128)(2,1)}, bf16[256,1024]{1,0:T(8,128)(2,1)}, bf16[1024,1024]{1,0:T(8,128)(2,1)}, bf16[1024,1024]{1,0:T(8,128)(2,1)}), ...) | async-done | bytes 5767184 | tf_op jit(solution)/shard_map/psum | solution.py:821
  570.0 4.2 convert_element_type.87
  574.3 2.7 convert_element_type.89
  576.9 1.0 convert_element_type.81
  578.0 1.0 convert_element_type.83
  579.0 1.1 convert_element_type.85
  580.1 35.7 %reduce-scatter.2.cloned.1.call-done = bf16[2048,256]{1,0:T(8,128)(2,1)} async-done(((bf16[2048,1024]{1,0:T(8,128)(2,1)}), bf16[2048,256]{1,0:T(8,128)(2,1)}) %reduce-scatter.2.cloned.1.call-update) | async-done | bytes 1048592 | tf_op jit(solution)/shard_map/reduce_scatter | solution.py:688
  615.9 2.5 add_convert_fusion
  618.4 1.0 copy.43
  (134 shorter events, 12.1 us)
Async XLA Ops:
  7.2 87.7 %copy-start = (bf16[1024,256]{1,0:T(8,128)(2,1)S(1)}, bf16[1024,256]{1,0:T(8,128)(2,1)}, u32[]{:S(2)}) copy-start(bf16[1024,256]{1,0:T(8,128)(2,1)} %param.22) | copy-start | bytes 1572868
  7.2 40.1 %all-gather.5.cloned.1.call-start = ((), (), s32[]{:S(2)}) async-start(), calls=%async_computation.1 | async-start | bytes 5242880 | tf_op jit(solution)/shard_map/all_gather | solution.py:684
  7.9 118.2 %all-gather.7.cloned.1.call-start = ((), (), s32[]{:S(2)}) async-start(), calls=%async_computation.2 | async-start | bytes 5242880 | tf_op jit(solution)/shard_map/all_gather | solution.py:684
  8.7 561.3 %all-reduce.4.cloned.1.call-start = ((), (), s32[]{:S(2)}) async-start(), calls=%async_computation.4 | async-start | bytes 11534336 | tf_op jit(solution)/shard_map/psum | solution.py:821
  11.5 40.7 %copy-start.29 = (f32[16,256]{1,0:T(8,128)}, f32[16,256]{1,0:T(8,128)S(1)}, u32[]{:S(2)}) copy-start(f32[16,256]{1,0:T(8,128)S(1)} %get-tuple-element.112) | copy-start | bytes 49156
  13.0 39.2 %copy-start.39 = (f32[1024]{0:T(1024)S(1)}, f32[1024]{0:T(1024)}, u32[]{:S(2)}) copy-start(f32[1024]{0:T(1024)} %param.19) | copy-start | bytes 12292
  47.3 3.4 copy-start.13
  52.2 1.4 copy-start.31
  52.2 1.4 copy-start.23
  53.7 58.7 %copy-start.17 = (bf16[2048,1024]{1,0:T(8,128)(2,1)}, bf16[2048,1024]{1,0:T(8,128)(2,1)S(1)}, u32[]{:S(2)}) copy-start(bf16[2048,1024]{1,0:T(8,128)(2,1)S(1)} %fusion.6) | copy-start | bytes 12582916
  90.5 1.0 copy-start.11
  91.5 30.7 %collective-permute-start.1 = (bf16[128,256]{1,0:T(8,128)(2,1)S(1)}, bf16[128,256]{1,0:T(8,128)(2,1)S(1)}, u32[]{:S(2)}, u32[]{:S(2)}) collective-permute-start(bf16[128,256]{1,0:T(8,128)(2,1)S(1)} %slice.98), channel_id=1, source_target_pairs={{0,4},{4,8},{8,12},{12,16},{16,20},{20,24},{24,28},{1,5},{5,9},{9,... | collective-permute-start | bytes 196616 | tf_op jit(solution)/shard_map/ppermute | solution.py:696
  96.3 26.0 %copy-start.5 = (bf16[512,256]{1,0:T(8,128)(2,1)}, bf16[512,256]{1,0:T(8,128)(2,1)S(1)}, u32[]{:S(2)}) copy-start(bf16[512,256]{1,0:T(8,128)(2,1)S(1)} %slice.114.q_ref) | copy-start | bytes 786436
  96.4 25.9 %collective-permute-start = (bf16[128,256]{1,0:T(8,128)(2,1)S(1)}, bf16[128,256]{1,0:T(8,128)(2,1)S(1)}, u32[]{:S(2)}, u32[]{:S(2)}) collective-permute-start(bf16[128,256]{1,0:T(8,128)(2,1)S(1)} %slice.97), channel_id=1, source_target_pairs={{0,4},{4,8},{8,12},{12,16},{16,20},{20,24},{24,28},{1,5},{5,9},{9,... | collective-permute-start | bytes 196616 | tf_op jit(solution)/shard_map/ppermute | solution.py:696
  112.4 8.9 %copy-start.3 = (bf16[1536,256]{1,0:T(8,128)(2,1)}, bf16[1536,256]{1,0:T(8,128)(2,1)S(1)}, u32[]{:S(2)}) copy-start(bf16[1536,256]{1,0:T(8,128)(2,1)S(1)} %get-tuple-element.68.v_ref) | copy-start | bytes 2359300
  122.3 2.8 copy-start.7
  122.3 2.8 copy-start.9
  126.1 142.0 %copy-start.6 = (bf16[512,256]{1,0:T(8,128)(2,1)S(1)}, bf16[512,256]{1,0:T(8,128)(2,1)}, u32[]{:S(2)}) copy-start(bf16[512,256]{1,0:T(8,128)(2,1)} %copy-done.5) | copy-start | bytes 786436
  265.8 8.7 %copy-start.2 = (bf16[1536,256]{1,0:T(8,128)(2,1)S(1)}, bf16[1536,256]{1,0:T(8,128)(2,1)}, u32[]{:S(2)}) copy-start(bf16[1536,256]{1,0:T(8,128)(2,1)} %copy-done.1) | copy-start | bytes 2359300
  265.8 8.7 %copy-start.4 = (bf16[1536,256]{1,0:T(8,128)(2,1)S(1)}, bf16[1536,256]{1,0:T(8,128)(2,1)}, u32[]{:S(2)}) copy-start(bf16[1536,256]{1,0:T(8,128)(2,1)} %copy-done.3) | copy-start | bytes 2359300
  268.1 1.0 copy-start.8
  269.0 1.0 copy-start.10
  270.0 13.8 %copy-start.18 = (bf16[2048,1024]{1,0:T(8,128)(2,1)S(1)}, bf16[2048,1024]{1,0:T(8,128)(2,1)}, u32[]{:S(2)}) copy-start(bf16[2048,1024]{1,0:T(8,128)(2,1)} %copy-done.17) | copy-start | bytes 12582916
  273.1 44.5 %collective-permute-start.3 = (bf16[128,256]{1,0:T(8,128)(2,1)S(1)}, bf16[128,256]{1,0:T(8,128)(2,1)S(1)}, u32[]{:S(2)}, u32[]{:S(2)}) collective-permute-start(bf16[128,256]{1,0:T(8,128)(2,1)S(1)} %slice.142), channel_id=1, source_target_pairs={{4,0},{8,4},{12,8},{16,12},{20,16},{24,20},{28,24},{5,1},{9,5},{13... | collective-permute-start | bytes 196616 | tf_op jit(solution)/shard_map/ppermute | solution.py:696
  283.8 2.1 copy-start.34
  283.8 3.8 copy-start.16
  285.9 3.4 copy-start.15
  286.0 31.7 %collective-permute-start.2 = (bf16[128,256]{1,0:T(8,128)(2,1)S(1)}, bf16[128,256]{1,0:T(8,128)(2,1)S(1)}, u32[]{:S(2)}, u32[]{:S(2)}) collective-permute-start(bf16[128,256]{1,0:T(8,128)(2,1)S(1)} %slice.143), channel_id=1, source_target_pairs={{4,0},{8,4},{12,8},{16,12},{20,16},{24,20},{28,24},{5,1},{9,5},{13... | collective-permute-start | bytes 196616 | tf_op jit(solution)/shard_map/ppermute | solution.py:696
  289.3 1.7 copy-start.21
  291.9 62.7 %copy-start.40 = (pred[8]{0:T(512)(128)(4,1)S(1)}, pred[8]{0:T(512)(128)(4,1)}, u32[]{:S(2)}) copy-start(pred[8]{0:T(512)(128)(4,1)} %fusion.21) | copy-start | bytes 28
  291.9 62.7 %copy-start.41 = (f32[8]{0:T(128)S(1)}, f32[8]{0:T(128)}, u32[]{:S(2)}) copy-start(f32[8]{0:T(128)} %multiply_convert_fusion) | copy-start | bytes 100
  291.9 62.8 %copy-start.12 = (f32[8,2,128,128]{3,2,1,0:T(8,128)S(1)}, f32[8,2,128,128]{3,2,1,0:T(8,128)}, u32[]{:S(2)}) copy-start(f32[8,2,128,128]{3,2,1,0:T(8,128)} %copy-done.11) | copy-start | bytes 3145732
  367.2 1.0 copy-start.24
  367.2 2.3 copy-start.32
  367.2 248.7 %reduce-scatter.2.cloned.1.call-start = ((), (), s32[]{:S(2)}) async-start(), calls=%async_computation.3 | async-start | bytes 5242880 | tf_op jit(solution)/shard_map/reduce_scatter | solution.py:688
  368.2 2.2 copy-start.14
  368.2 2.5 copy-start.35
  378.3 84.1 %copy-start.28 = (f32[256,16]{0,1:T(8,128)S(1)}, f32[256,16]{0,1:T(8,128)}, u32[]{:S(2)}) copy-start(f32[256,16]{0,1:T(8,128)} %param.26) | copy-start | bytes 49156
  378.3 84.1 %copy-start.33 = (f32[256,16]{0,1:T(8,128)S(1)}, f32[256,16]{0,1:T(8,128)}, u32[]{:S(2)}) copy-start(f32[256,16]{0,1:T(8,128)} %param.29) | copy-start | bytes 49156
  378.4 84.1 %copy-start.36 = (f32[256,16]{0,1:T(8,128)S(1)}, f32[256,16]{0,1:T(8,128)}, u32[]{:S(2)}) copy-start(f32[256,16]{0,1:T(8,128)} %param.28) | copy-start | bytes 49156
  378.4 84.8 %copy-start.30 = (f32[16,256]{1,0:T(8,128)S(1)}, f32[16,256]{1,0:T(8,128)}, u32[]{:S(2)}) copy-start(f32[16,256]{1,0:T(8,128)} %copy-done.29) | copy-start | bytes 49156
  378.4 84.8 %copy-start.37 = (f32[256,16]{0,1:T(8,128)S(1)}, f32[256,16]{0,1:T(8,128)}, u32[]{:S(2)}) copy-start(f32[256,16]{0,1:T(8,128)} %param.27) | copy-start | bytes 49156
  570.0 4.2 copy-start.19
  574.2 2.7 copy-start.27
  574.2 3.7 copy-start.26
  574.2 4.8 copy-start.25
  574.2 41.6 %copy-start.20 = (f32[2048,256]{1,0:T(8,128)S(1)}, f32[2048,256]{1,0:T(8,128)}, u32[]{:S(2)}) copy-start(f32[2048,256]{1,0:T(8,128)} %get-tuple-element.71) | copy-start | bytes 6291460
  615.8 2.5 copy-start.22
  (2 other events, 1.6 us)
Sparse Core Ops, SparseCore 0:
  9.6 37.7 all-gather.4
  48.9 35.0 all-gather.6
  367.3 202.6 all-reduce.3
  572.6 43.2 reduce-scatter.1

commit v3 on v2

--- a/solution.py
+++ b/solution.py
@@ -403,10 +403,10 @@
         scores = dot_nt(k_ref[k0:k1, :], q) * SCALE
         probs = jnp.where(allowed_keys(starts_ref, q0, k0, k1, shift), jnp.exp(scores - lse), 0.0)
         grad_probs = dot_nt(v_ref[k0:k1, :], g)
-        dv_ref[k0:k1, :] += dot_nn(probs.astype(jnp.bfloat16), g)
+        dv_ref[0, k0:k1, :] += dot_nn(probs.astype(jnp.bfloat16), g)
         delta = jnp.sum(probs * grad_probs, axis=0, keepdims=True)
         grad_scores = (probs * (grad_probs - delta)).astype(jnp.bfloat16)
-        dk_ref[k0:k1, :] += dot_nn(grad_scores, q) * SCALE
+        dk_ref[0, k0:k1, :] += dot_nn(grad_scores, q) * SCALE
         dq_ref[q0 : q0 + QT, :] = (dot_nn(kt_ref[:, k0:k1], grad_scores) * SCALE).T.astype(dq_ref.dtype)
 
 
@@ -416,12 +416,13 @@
     keys = k.shape[0]
     lane = lambda h: (0, h)
     rspec, kspec = pl.BlockSpec((rows, HEAD), lane), pl.BlockSpec((keys, HEAD), lane)
+    gspec = pl.BlockSpec((1, keys, HEAD), lambda h: (h, 0, 0))
     return pl.pallas_call(
         functools.partial(attend_back_kernel, tiles_of(rows, shift), shift),
         grid=(heads,),
-        out_shape=(jax.ShapeDtypeStruct((rows, width), jnp.bfloat16), jax.ShapeDtypeStruct((keys, width), jnp.float32), jax.ShapeDtypeStruct((keys, width), jnp.float32)),
+        out_shape=(jax.ShapeDtypeStruct((rows, width), jnp.bfloat16), jax.ShapeDtypeStruct((heads, keys, HEAD), jnp.float32), jax.ShapeDtypeStruct((heads, keys, HEAD), jnp.float32)),
         in_specs=[SMEM, rspec, kspec, kspec, rspec, pl.BlockSpec((1, 1, rows), lambda h: (h, 0, 0))],
-        out_specs=(rspec, kspec, kspec),
+        out_specs=(rspec, gspec, gspec),
         scratch_shapes=[pltpu.VMEM((HEAD, keys), jnp.bfloat16)],
         compiler_params=pltpu.CompilerParams(vmem_limit_bytes=40 * 2**20),
         name=name)(starts, q, k, v, g, lse)
@@ -539,8 +540,8 @@
 
 
 def middle_kernel(chunks, att_ref, tok_ref, cot_ref, w_out_ref, w_up_ref, w_down_ref, gain_ref,
-                  result_ref, gm_ref, gatt_ref, gdown_ref, gup_ref, gout_ref, ggain_ref,
-                  mid_full, gm_full, mid_ref, part, near, across, joint, n2_ref, act_ref, gpre_ref, pre_ref, gact_ref, mean_ref, inv_ref,
+                  result_ref, gm_ref, gatt_ref, grads_ref, ggain_ref,
+                  gdown_ref, gup_ref, gout_ref, mid_full, gm_full, mid_ref, part, near, across, joint, n2_ref, act_ref, gpre_ref, pre_ref, gact_ref, mean_ref, inv_ref,
                   send_sem, recv_sem):
     width = att_ref.shape[1]
     rows = ROWS
@@ -617,7 +618,8 @@
     def finish_sums(c):
         own = pl.ds(pl.multiple_of(me * width, width), width)
         gm = cot_ref[span(c), own].astype(jnp.float32) + sums[2].finish(c)
-        gm_ref[span(c), :] = gm
+        for lt in range(width // LANES):
+            gm_ref[lt, span(c), :] = gm[:, cut(lt, LANES)]
         gm_full[me, span(c), :] = gm.astype(jnp.bfloat16)
         gather_gm.start(c)
         result_ref[span(c), :] = (mid_ref[span(c), :] + sums[1].finish(c)).astype(result_ref.dtype)
@@ -647,6 +649,11 @@
             def _(stage=stage, lag=lag):
                 stage(i - lag)
 
+    first = 0
+    for total in (gdown_ref, gup_ref, gout_ref):
+        grads_ref[first : first + total.shape[0], :] = total[...].astype(jnp.bfloat16)
+        first += total.shape[0]
+
 
 def middle_phase(att, tok, cot_full, w_out, w_up, w_down, gain):
     rows, width = att.shape
@@ -663,11 +670,11 @@
 
     return pl.pallas_call(
         functools.partial(middle_kernel, chunks),
-        out_shape=(out((rows, width), bf), out((rows, width), jnp.float32), out((rows, width), bf),
-                   out((hidden, full), jnp.float32), out((full, hidden), jnp.float32), out((width, full), jnp.float32),
-                   out((8, full), jnp.float32)),
-        in_specs=[VMEM] * 7, out_specs=(VMEM,) * 7,
+        out_shape=(out((rows, width), bf), out((width // LANES, rows, LANES), jnp.float32), out((rows, width), bf),
+                   out((hidden + full + width, full), bf), out((8, full), jnp.float32)),
+        in_specs=[VMEM] * 7, out_specs=(VMEM,) * 5,
         scratch_shapes=[
+            buf(hidden, full, dtype=jnp.float32), buf(full, hidden, dtype=jnp.float32), buf(width, full, dtype=jnp.float32),
             buf(4, rows, width), buf(4, rows, width), buf(rows, width, dtype=jnp.float32),
             buf(3, DEEP, 4, ROWS, width), buf(3, chunks, 2, ROWS, width), buf(3, chunks, ROWS, width), buf(3, DEEP, ROWS, width),
             buf(ROWS, full), buf(ROWS, hidden), buf(ROWS, hidden),
@@ -678,6 +685,444 @@
         compiler_params=pltpu.CompilerParams(collective_id=0, has_side_effects=True, vmem_limit_bytes=60 * 2**20),
         cost_estimate=pl.CostEstimate(flops=30 * 10**9, bytes_accessed=30 * 10**6, transcendentals=4 * 10**6),
         name="middle_phase")(att, tok, cot_full, w_out, w_up, w_down, gain)
+
+
+POINTS = 14
+
+
+def ring_place(index, count):
+    side, along = index % 2, index // 2
+    return (1 - side) * along + side * (count - 1 - along)
+
+
+def ring_index(place, count):
+    side = place // (count // 2)
+    return (1 - side) * (2 * place) + side * (2 * (count - 1 - place) + 1)
+
+
+class Ring:
+    def __init__(self, count, half, data, total, held, send_sem, recv_sem):
+        self.count, self.half = count, half
+        self.data, self.total, self.held = data, total, held
+        self.send_sem, self.recv_sem = send_sem, recv_sem
+        self.place = ring_place(lax.axis_index("dp"), count)
+        self.mp = lax.axis_index("mp")
+        self.events = 2 * count - 1
+
+    def rows(self, chunk, way):
+        return pl.ds(pl.multiple_of((2 * chunk + way) * self.half, self.half), self.half)
+
+    def chunk(self, way, back):
+        return (self.place + (1 - 2 * (1 - way)) * back + 2 * self.count) % self.count
+
+    def copy(self, src, dst, way, step):
+        peer = ring_index((self.place + 1 - 2 * way + self.count) % self.count, self.count)
+        return pltpu.make_async_remote_copy(
+            src_ref=src, dst_ref=dst, send_sem=self.send_sem.at[way, step], recv_sem=self.recv_sem.at[way, step],
+            device_id=(peer, self.mp), device_id_type=MESH)
+
+    def add_copy(self, way, step):
+        return self.copy(self.held.at[way, step], self.held.at[way, step], way, step)
+
+    def give_copy(self, way, step, chunk):
+        piece = self.total.at[self.rows(chunk, way)]
+        return self.copy(piece, piece, way, self.count - 1 + step)
+
+    def event(self, e):
+        n = self.count
+
+        @pl.when(e == 0)
+        def _():
+            for way in range(2):
+                self.copy(self.data.at[self.rows(self.chunk(way, 0), way)], self.held.at[way, 0], way, 0).start()
+
+        @pl.when(jnp.logical_and(e >= 1, e < n - 1))
+        def _():
+            for way in range(2):
+                self.add_copy(way, e - 1).wait_recv()
+                own = self.data[self.rows(self.chunk(way, e), way), :].astype(jnp.float32)
+                self.held[way, e - 1] = (self.held[way, e - 1].astype(jnp.float32) + own).astype(jnp.bfloat16)
+                self.copy(self.held.at[way, e - 1], self.held.at[way, e], way, e).start()
+
+        @pl.when(e == n - 1)
+        def _():
+            for way in range(2):
+                self.add_copy(way, n - 2).wait_recv()
+                mine = self.chunk(way, n - 1)
+                own = self.data[self.rows(mine, way), :].astype(jnp.float32)
+                self.total[self.rows(mine, way), :] = (self.held[way, n - 2].astype(jnp.float32) + own).astype(jnp.bfloat16)
+                self.give_copy(way, 0, mine).start()
+
+        @pl.when(jnp.logical_and(e >= n, e < 2 * n - 2))
+        def _():
+            for way in range(2):
+                self.give_copy(way, e - n, self.chunk(way, e - n)).wait_recv()
+                self.give_copy(way, e - n + 1, self.chunk(way, e - n)).start()
+
+        @pl.when(e == 2 * n - 2)
+        def _():
+            for way in range(2):
+                self.give_copy(way, n - 2, self.chunk(way, n - 2)).wait_recv()
+
+    def point(self, k):
+        first, last = (k * (self.events - 1)) // POINTS, ((k + 1) * (self.events - 1)) // POINTS
+
+        @pl.loop(first + 1, last + 1)
+        def _(e):
+            self.event(e)
+
+    def settle(self):
+        @pl.loop(0, 2 * (self.count - 1))
+        def _(step):
+            for way in range(2):
+                self.copy(self.held.at[way, 0], self.held.at[way, 0], way, step).wait_send()
+
+
+class Spread:
+    def __init__(self, count, send_sem, recv_sem):
+        self.count, self.send_sem, self.recv_sem = count, send_sem, recv_sem
+        self.me, self.mp = lax.axis_index("dp"), lax.axis_index("mp")
+
+    def copy(self, src, dst, o):
+        return pltpu.make_async_remote_copy(
+            src_ref=src, dst_ref=dst, send_sem=self.send_sem.at[o], recv_sem=self.recv_sem.at[o],
+            device_id=((self.me + o) % self.count, self.mp), device_id_type=MESH)
+
+    def start(self, src, dst):
+        @pl.loop(1, self.count)
+        def _(o):
+            self.copy(src(o), dst(o), o).start()
+
+    def wait(self, src, dst):
+        @pl.loop(1, self.count)
+        def _(o):
+            self.copy(src(o), dst(o), o).wait()
+
+
+def greet_all(count):
+    me, mp = lax.axis_index("dp"), lax.axis_index("mp")
+    barrier = pltpu.get_barrier_semaphore()
+
+    @pl.loop(1, count)
+    def _(o):
+        pl.semaphore_signal(barrier, inc=1, device_id=((me + o) % count, mp), device_id_type=MESH)
+
+    for peer in group_of_four()[1:]:
+        pl.semaphore_signal(barrier, inc=1, device_id=(me, peer), device_id_type=MESH)
+    pl.semaphore_wait(barrier, count + 2)
+
+
+def masks_of(bounds_ref, span, group):
+    if bounds_ref is None:
+        return None
+    return [keep_mask(bounds_ref, span, group * GROUP + j) for j in range(GROUP)]
+
+
+def open_segment(bounds_ref, span, seg):
+    if bounds_ref is None:
+        return 1.0
+    return no_bound_in_seg(bounds_ref, span, seg)
+
+
+def adjoint_pass(bounds_ref, gk_ref, gv_ref, wide_ref, adj_ref, span, tiles, row0, beside):
+    adj_ref[...] = jnp.zeros_like(adj_ref)
+    groups = span // GROUP
+
+    @pl.loop(0, groups)
+    def _(step):
+        group = groups - 1 - step
+        keep = masks_of(bounds_ref, span, group)
+        for lt in range(tiles):
+            gk = [gk_ref[lt, pl.ds(row0 + group * GROUP + j, SEG, stride=span), :] for j in range(GROUP)]
+            gv = [gv_ref[lt, pl.ds(row0 + group * GROUP + j, SEG, stride=span), :] for j in range(GROUP)]
+            for n in range(STATES):
+                mine = slice(n * SEG, (n + 1) * SEG)
+                a, ck, cv = wide_ref[0, n, lt], wide_ref[1, n, lt], wide_ref[2, n, lt]
+                m = adj_ref[lt, mine, :]
+                for j in reversed(range(GROUP)):
+                    m = a * (m + (ck * gk[j] + cv * gv[j]))
+                    if keep is not None:
+                        m = m * keep[j]
+                adj_ref[lt, mine, :] = m
+        beside(step)
+
+
+def adjoint_chain(bounds_ref, adj_ref, last, far_ref, span, tiles, write):
+    ends = []
+    for lt in range(tiles):
+        lanes = slice(lt * LANES, (lt + 1) * LANES)
+        start, far = last[:, lanes], far_ref[:, lanes]
+        for seg in reversed(range(SEG)):
+            rows = pl.ds(seg, STATES, stride=SEG)
+            end = adj_ref[lt, rows, :]
+            if write:
+                adj_ref[lt, rows, :] = start
+            start = end + far * start * open_segment(bounds_ref, span, seg)
+        ends.append(start)
+    return jnp.concatenate(ends, axis=1)
+
+
+def adjoint_full(bounds_ref, u_ref, gk_ref, gv_ref, ckpt_ref, wide_ref, adj_ref, acc_ref, span, tiles, row0, group0, beside):
+    groups = span // GROUP
+
+    @pl.loop(0, groups)
+    def _(step):
+        group = groups - 1 - step
+        keep = masks_of(bounds_ref, span, group)
+        for lt in range(tiles):
+            at = [pl.ds(row0 + group * GROUP + j, SEG, stride=span) for j in range(GROUP)]
+            u = [u_ref[lt, r, :] for r in at]
+            gk = [gk_ref[lt, r, :] for r in at]
+            gv = [gv_ref[lt, r, :] for r in at]
+            gu = [jnp.zeros((SEG, LANES), jnp.float32)] * GROUP
+            for n in range(STATES):
+                mine = slice(n * SEG, (n + 1) * SEG)
+                a, ck, cv = wide_ref[0, n, lt], wide_ref[1, n, lt], wide_ref[2, n, lt]
+                states = [ckpt_ref[group0 + group, lt, mine, :]]
+                for j in range(GROUP):
+                    s = a * states[j]
+                    if keep is not None:
+                        s = s * keep[j]
+                    states.append(s + u[j])
+                m = adj_ref[lt, mine, :]
+                sum_k, sum_v, sum_a = acc_ref[0, lt, mine, :], acc_ref[1, lt, mine, :], acc_ref[2, lt, mine, :]
+                for j in reversed(range(GROUP)):
+                    lam = m + (ck * gk[j] + cv * gv[j])
+                    gu[j] = gu[j] + lam
+                    sum_k = sum_k + gk[j] * states[j + 1]
+                    sum_v = sum_v + gv[j] * states[j + 1]
+                    m = a * lam
+                    if keep is not None:
+                        m = m * keep[j]
+                    sum_a = sum_a + m * states[j]
+                acc_ref[0, lt, mine, :] = sum_k
+                acc_ref[1, lt, mine, :] = sum_v
+                acc_ref[2, lt, mine, :] = sum_a
+                adj_ref[lt, mine, :] = m
+            for j in range(GROUP):
+                u_ref[lt, at[j], :] = gu[j]
+        beside(step)
+
+
+def tail_kernel(count, half, block, bounds_ref, grads_hbm, n1_hbm, u_hbm, gk_hbm, gv_hbm, ckpt_hbm, gm_hbm,
+                gq_ref, inv_ref, w_in_ref, w_query_ref, par_ref, far_ref, rate_ref, gain_ref, gain_two_ref,
+                grad_tokens_ref, total_ref, win_ref, sums_ref, gains_ref,
+                grads_ref, n1_ref, u_ref, gk_ref, gv_ref, ckpt_ref, wide_ref, adj_ref, adj_long, acc_ref,
+                gssm_ref, up_ref, ggain_ref, held, win_data, win_held, piece_ref, piece_held, small_ref, small_held, gain_held,
+                part, near, across, joint, load_sem, ring_send, ring_recv, mp_send, mp_recv, dp_send, dp_recv):
+    rows, width = gq_ref.shape
+    tiles = width // LANES
+    full = n1_ref.shape[1]
+    me = lax.axis_index("dp")
+    mp = lax.axis_index("mp")
+    chunks = rows // ROWS
+    long_span, short_span = LONG_DEV // SEG, (rows - LONG_DEV) // SEG
+    long_groups, short_groups = long_span // GROUP, short_span // GROUP
+    known = grads_hbm.shape[0]
+    loads = [pltpu.make_async_copy(src, dst, load_sem.at[i]) for i, (src, dst) in enumerate(
+        [(gk_hbm, gk_ref), (gv_hbm, gv_ref), (n1_hbm, n1_ref), (grads_hbm, grads_ref.at[pl.ds(0, known)]),
+         (u_hbm, u_ref), (ckpt_hbm, ckpt_ref), (gm_hbm, gk_ref)])]
+    for load in loads[:6]:
+        load.start()
+    seg_scan_params(par_ref, wide_ref)
+    acc_ref[...] = jnp.zeros_like(acc_ref)
+    ggain_ref[...] = jnp.zeros_like(ggain_ref)
+    ring = Ring(count, half, grads_ref, total_ref, held, ring_send, ring_recv)
+    mover = Mover(mp_send, mp_recv)
+    token_sum = Scatter(mover, 0, part, near, across, joint)
+    first_spread = Spread(count, dp_send.at[0], dp_recv.at[0])
+    scatter_spread = Spread(count, dp_send.at[1], dp_recv.at[1])
+    gather_spread = Spread(count, dp_send.at[2], dp_recv.at[2])
+    small_spread = Spread(count, dp_send.at[3], dp_recv.at[3])
+    greet_all(count)
+
+    def nothing(step):
+        del step
+
+    loads[0].wait()
+    loads[1].wait()
+    adjoint_pass(None, gk_ref, gv_ref, wide_ref, adj_long, long_span, tiles, 0, nothing)
+    zero = jnp.zeros((STATES, width), jnp.float32)
+    piece_ref[...] = adjoint_chain(None, adj_long, zero, far_ref.at[0], long_span, tiles, False)
+    first_spread.start(lambda o: piece_ref, lambda o: piece_held.at[me])
+
+    loads[2].wait()
+    loads[3].wait()
+    for d in range(full // width):
+        grads_ref[known : known + width, cut(d, width)] = mm(gq_ref[...], n1_ref[:, cut(d, width)], 0, 0).astype(jnp.bfloat16)
+    if grads_ref.shape[0] > known + width:
+        grads_ref[known + width :, :] = jnp.zeros((grads_ref.shape[0] - known - width, full), jnp.bfloat16)
+    ring.event(0)
+
+    loads[4].wait()
+    loads[5].wait()
+
+    def beside_first(step):
+        @pl.when(step == short_groups - 1)
+        def _():
+            ring.point(0)
+
+    adjoint_pass(bounds_ref, gk_ref, gv_ref, wide_ref, adj_ref, short_span, tiles, LONG_DEV, beside_first)
+    adjoint_chain(bounds_ref, adj_ref, zero, far_ref.at[1], short_span, tiles, True)
+
+    def beside_second(step):
+        @pl.when(step % 6 == 5)
+        def _():
+            ring.point(1 + step // 6)
+
+    adjoint_full(bounds_ref, u_ref, gk_ref, gv_ref, ckpt_ref, wide_ref, adj_ref, acc_ref,
+                 short_span, tiles, LONG_DEV, long_groups, beside_second)
+
+    first_spread.wait(lambda o: piece_ref, lambda o: piece_held.at[me])
+
+    def fold(d, total):
+        gap = d - me - 1
+        weight = jnp.exp(rate_ref[...] * (-LONG_DEV * jnp.maximum(gap, 0)).astype(jnp.float32))
+        return total + jnp.where(gap >= 0, weight * piece_held[d], 0.0)
+
+    piece_held[me] = zero
+    last = lax.fori_loop(0, count, fold, zero)
+    adjoint_chain(None, adj_long, last, far_ref.at[0], long_span, tiles, True)
+    adjoint_full(None, u_ref, gk_ref, gv_ref, ckpt_ref, wide_ref, adj_long, acc_ref,
+                 long_span, tiles, 0, 0, nothing)
+    loads[6].start()
+    ring.point(5)
+
+    for lt in range(tiles):
+        gssm_ref[:, lt * LANES : (lt + 1) * LANES] = u_ref[lt].astype(jnp.bfloat16)
+        for p in range(3):
+            total = acc_ref[p, lt, pl.ds(0, STATES, stride=SEG), :]
+            for seg in range(1, SEG):
+                total = total + acc_ref[p, lt, pl.ds(seg, STATES, stride=SEG), :]
+            small_ref[p * STATES : (p + 1) * STATES, lt * LANES : (lt + 1) * LANES] = total
+
+    for d in range(full // width):
+        win_data[:width, cut(d, width)] = mm(gssm_ref[...], n1_ref[:, cut(d, width)], 0, 0).astype(jnp.bfloat16)
+    if win_data.shape[0] > width:
+        win_data[width:, :] = jnp.zeros((win_data.shape[0] - width, full), jnp.bfloat16)
+
+    def win_rows(device):
+        return pl.ds(pl.multiple_of(device * block, block), block)
+
+    scatter_spread.start(lambda o: win_data.at[win_rows((me + o) % count)], lambda o: win_held.at[o])
+    loads[6].wait()
+
+    def span_of(c):
+        return pl.ds(pl.multiple_of(c * ROWS, ROWS), ROWS)
+
+    def project(c):
+        up_ref[...] = mm(gssm_ref[span_of(c), :], w_in_ref[...], 1, 1) + mm(gq_ref[span_of(c), :], w_query_ref[...], 1, 1)
+
+        @pl.loop(0, ROWS // SUB)
+        def _(sub):
+            mine = pl.ds(pl.multiple_of(sub * SUB, SUB), SUB)
+            here = pl.ds(pl.multiple_of(c * ROWS + sub * SUB, SUB), SUB)
+            xhat = n1_ref[here, :].astype(jnp.float32) * (1.0 / gain_ref[...])
+            up = up_ref[mine, :]
+            both = up * xhat
+            ggain_ref[...] += jnp.sum(both.reshape(SUB // 8, 8, full), axis=0)
+            scaled = up * gain_ref[...]
+            plain = jnp.mean(scaled, axis=1, keepdims=True)
+            cross = jnp.mean(scaled * xhat, axis=1, keepdims=True)
+            up_ref[mine, :] = inv_ref[here, :] * (scaled - plain - xhat * cross)
+
+        token_sum.start(c, lambda d: up_ref[:, cut(d, width)])
+
+    def finish(c):
+        gm = jnp.concatenate([gk_ref[lt, span_of(c), :] for lt in range(tiles)], axis=1)
+        grad_tokens_ref[span_of(c), :] = (gm + token_sum.finish(c)).astype(grad_tokens_ref.dtype)
+
+    stages = [(finish, 2), (token_sum.combine, 1), (project, 0)]
+
+    @pl.loop(0, chunks + 2)
+    def _(i):
+        for stage, lag in stages:
+            @pl.when(jnp.logical_and(i >= lag, i < chunks + lag))
+            def _(stage=stage, lag=lag):
+                stage(i - lag)
+
+        @pl.when(i % 2 == 1)
+        def _():
+            ring.point(6 + i // 2)
+
+    ggain = jnp.sum(ggain_ref[...], axis=0, keepdims=True)
+    gtwo = jnp.sum(gain_two_ref[...], axis=0, keepdims=True)
+    for d in range(full // width):
+        small_ref[3 * STATES + d : 3 * STATES + d + 1, :] = ggain[:, cut(d, width)]
+        small_ref[3 * STATES + 4 + d : 3 * STATES + 5 + d, :] = gtwo[:, cut(d, width)]
+    small_spread.start(lambda o: small_ref, lambda o: small_held.at[me])
+    small_held[me] = small_ref[...]
+
+    scatter_spread.wait(lambda o: win_data.at[win_rows((me + o) % count)], lambda o: win_held.at[o])
+    win_held[0] = win_data[win_rows(me), :]
+    total = win_held[0].astype(jnp.float32)
+    total = lax.fori_loop(1, count, lambda o, t: t + win_held[o].astype(jnp.float32), total)
+    win_ref[win_rows(me), :] = total.astype(jnp.bfloat16)
+    gather_spread.start(lambda o: win_ref.at[win_rows(me)], lambda o: win_ref.at[win_rows(me)])
+    ring.point(11)
+    small_spread.wait(lambda o: small_ref, lambda o: small_held.at[me])
+    small = lax.fori_loop(1, count, lambda d, t: t + small_held[d], small_held[0])
+    sums_ref[...] = small[: 3 * STATES]
+    gain_held[mp] = small[3 * STATES :]
+    group = group_of_four()
+    sends = [mover.copy(gain_held.at[mp], gain_held.at[mp], 3, i, group[1 + i]) for i in range(3)]
+    for send in sends:
+        send.start()
+    ring.point(12)
+    for send in sends:
+        send.wait()
+    gains_ref[...] = ((gain_held[0] + gain_held[1]) + gain_held[2]) + gain_held[3]
+    gather_spread.wait(lambda o: win_ref.at[win_rows(me)], lambda o: win_ref.at[win_rows(me)])
+    ring.point(13)
+    ring.settle()
+
+
+def round_up(value, unit):
+    return -(-value // unit) * unit
+
+
+def tail_phase(bounds, grads, n1, u, gk, gv, ckpt, gm, gq, inv, w_in_t, w_query_t, par, far, rate, gain, gain_two_parts, count):
+    rows, width = gq.shape
+    tiles = width // LANES
+    full = n1.shape[1]
+    bf = jnp.bfloat16
+    used = grads.shape[0] + width
+    half = round_up(-(-used // (2 * count)), 16)
+    block = round_up(-(-width // count), 16)
+
+    def out(shape, dtype):
+        return jax.ShapeDtypeStruct(shape, dtype)
+
+    def buf(*shape, dtype=bf):
+        return pltpu.VMEM(shape, dtype)
+
+    def wide(*shape):
+        return pltpu.VMEM(shape, jnp.float32)
+
+    ANY = pl.BlockSpec(memory_space=pl.ANY)
+    chunks = rows // ROWS
+    dma = pltpu.SemaphoreType.DMA
+    small_rows = 3 * STATES + 8
+    return pl.pallas_call(
+        functools.partial(tail_kernel, count, half, block),
+        out_shape=(out((rows, width), bf), out((2 * count * half, full), bf), out((count * block, full), bf),
+                   out((3 * STATES, width), jnp.float32), out((8, width), jnp.float32)),
+        in_specs=[SMEM] + [ANY] * 7 + [VMEM] * 9, out_specs=(VMEM,) * 5,
+        scratch_shapes=[
+            buf(2 * count * half, full), buf(rows, full),
+            wide(tiles, rows, LANES), wide(tiles, rows, LANES), wide(tiles, rows, LANES),
+            wide(*ckpt.shape), wide(3, STATES, tiles, SEG, LANES), wide(tiles, STATES * SEG, LANES), wide(tiles, STATES * SEG, LANES),
+            wide(3, tiles, STATES * SEG, LANES),
+            buf(rows, width), wide(ROWS, full), wide(8, full), buf(2, count - 1, half, full),
+            buf(count * block, full), buf(count, block, full), wide(STATES, width), wide(count, STATES, width),
+            wide(small_rows, width), wide(count, small_rows, width), wide(4, 8, width),
+            buf(DEEP, 4, ROWS, width), buf(chunks, 2, ROWS, width), buf(chunks, ROWS, width), buf(DEEP, ROWS, width),
+            dma((7,)), dma((2, 2 * (count - 1))), dma((2, 2 * (count - 1))),
+            dma((4, chunks)), dma((4, chunks)), dma((4, count)), dma((4, count)),
+        ],
+        compiler_params=pltpu.CompilerParams(collective_id=1, has_side_effects=True, vmem_limit_bytes=62 * 2**20),
+        cost_estimate=pl.CostEstimate(flops=6 * 10**9, bytes_accessed=40 * 10**6, transcendentals=0),
+        name="tail_phase")(bounds, grads, n1, u, gk, gv, ckpt, gm, gq, inv, w_in_t, w_query_t, par, far, rate, gain, gain_two_parts)
 
 
 def gather_features(values_in):
@@ -748,6 +1193,7 @@
 ):
     low = jnp.bfloat16
     device = lax.axis_index("dp")
+    local_width = w_in.shape[1]
     lengths = short_lengths[0]
     ends = jnp.cumsum(lengths).astype(jnp.int32)
     short_starts = jnp.concatenate([jnp.zeros((1,), jnp.int32), ends[:-1]])
@@ -784,51 +1230,40 @@
     att_short, lse_short = attend(short_starts, q_short, k_short, v_short, 0, "attend_short")
     att_long, lse_long = attend(long_low, q_long, k_long, v_long, CTX, "attend_long")
     attended = jnp.concatenate([att_long, att_short])
-    result, grad_middle, grad_attended, grad_w_down, grad_w_up, grad_w_out, gain_parts = middle_phase(
+    result, grad_middle, grad_attended, grads, gain_two_parts = middle_phase(
         attended, tokens, cotangent_full, w_out, w_up, w_down, gain_two[None]
     )
-    grad_gain_two = jnp.sum(gain_parts, axis=0)
 
     gq_long, gk_long, gv_long = attend_back(
         long_low, q_long, k_long, v_long, grad_attended[:LONG_DEV], lse_long, CTX, "attend_back_long"
     )
-    back_k, back_v = from_behind((gk_long[:CTX].astype(low), gv_long[:CTX].astype(low)), "dp", -1)
+    back = from_behind(jnp.stack([gk_long[:, :CTX], gv_long[:, :CTX]]).astype(low), "dp", -1).astype(jnp.float32)
     gq_short, gk_short, gv_short = attend_back(
         short_starts, q_short, k_short, v_short, grad_attended[LONG_DEV:], lse_short, 0, "attend_back_short"
     )
-    gk_long = gk_long[CTX:].at[LONG_DEV - CTX :].add(back_k.astype(jnp.float32))
-    gv_long = gv_long[CTX:].at[LONG_DEV - CTX :].add(back_v.astype(jnp.float32))
-    local_in = ssm_adjoint_ends(no_bound, gk_long, gv_long, par, far_long)
-    grad_pieces = lax.all_gather(local_in[None], "dp", axis=0, tiled=True)
-    grad_end = fold_pieces(grad_pieces, rate_t, others - device - 1)
-    gu_short, sums_short = ssm_backward(
-        short_starts, u_short, gk_short, gv_short, par, far_short, zero_state, ckpt_short, "ssm_back_short"
+    gk_long = gk_long[:, CTX:].at[:, LONG_DEV - CTX :].add(back[0])
+    gv_long = gv_long[:, CTX:].at[:, LONG_DEV - CTX :].add(back[1])
+    gk = jnp.concatenate([gk_long, gk_short], axis=1)
+    gv = jnp.concatenate([gv_long, gv_short], axis=1)
+    u_tiles = ssm_input.reshape(-1, local_width // LANES, LANES).transpose(1, 0, 2)
+    ckpt = jnp.concatenate([ckpt_long, ckpt_short])
+    grad_queries = jnp.concatenate([gq_long, gq_short])
+    grad_tokens, total, win_t, sums, gains = tail_phase(
+        short_starts, grads, normed_one_low, u_tiles, gk, gv, ckpt, grad_middle, grad_queries, inverse_one,
+        w_in, w_query, par, jnp.stack([far_long, far_short]), rate_t, gain_one[None], gain_two_parts, lax.axis_size("dp"),
     )
-    gu_long, sums_long = ssm_backward(
-        no_bound, u_long, gk_long, gv_long, par, far_long, grad_end, ckpt_long, "ssm_back_long"
-    )
-    sums = sums_short + sums_long
-    grad_ssm = jnp.concatenate([gu_long, gu_short])
-    grad_queries = jnp.concatenate([gq_long, gq_short])
-    grad_w_in = dot(normed_one_low, grad_ssm, ((0,), (0,)))
-    grad_w_query = dot(normed_one_low, grad_queries, ((0,), (0,)))
-    grad_hidden_one = dot(grad_ssm, w_in, ((1,), (1,))) + dot(grad_queries, w_query, ((1,), (1,)))
-    token_part, grad_gain_one = norm_backward(grad_hidden_one, normed_one, inverse_one, gain_one)
-    grad_tokens = (grad_middle + reduce_features(token_part)).astype(low)
-
-    grad_w_in, grad_w_query, grad_w_out, grad_w_up, grad_w_down = (
-        g.astype(jnp.float32)
-        for g in lax.psum(
-            tuple(g.astype(low) for g in (grad_w_in, grad_w_query, grad_w_out, grad_w_up, grad_w_down)), "dp"
-        )
-    )
-    sums = lax.psum(sums, "dp")
+    hidden, full = w_down.shape
+    rows_of = [total[:hidden], total[hidden : hidden + full], total[hidden + full : hidden + full + local_width],
+               total[hidden + full + local_width : hidden + full + 2 * local_width].T, win_t[:local_width].T]
+    grad_w_down, grad_w_up, grad_w_out, grad_w_query, grad_w_in = (r.astype(jnp.float32) for r in rows_of)
+    grad_gain_one, grad_gain_two = gains.reshape(2, full)
+    sums = sums.reshape(3, STATES, local_width)
+
     grad_ck = (drive * sums[0]).T
     grad_cv = (drive * sums[1]).T
     grad_drive = ck_t * sums[0] + cv_t * sums[1]
     grad_b = (root * grad_drive).T
     grad_rate = (grad_drive * b_in.T * jnp.exp(-2.0 * rate_t) / root - sums[2]).T
-    grad_gain_one, grad_gain_two = lax.psum((grad_gain_one, grad_gain_two), ("dp", "mp"))
     return (
         result,
         grad_tokens,

time: 632 us -> 484 us (0.77)
  waiting for transfers between devices: 178 us -> 36.9 us
  Pallas kernels: 218 us -> 339 us
  blocking collectives: 149 us -> 30.6 us
  local copies, waits for them, and re-layouts: 11 us -> 23.9 us
  matrix products: 13.8 us -> 5 us
  other arithmetic: 33.4 us -> 26.3 us
    pallas_call x3 -> x1, Pallas kernels: 36 us -> 157 us  [tail_phase(): pl.pallas_call(functools.partial(tail_kernel, count, half, block), out_sh...]
    psum x1 -> x0, waiting for transfers between devices: 106 us -> none  [on_device(): lax.psum(tuple((g.astype(low) for g in (grad_w_in, grad_w_query, grad_w_o...]
    psum x2 -> x0, blocking collectives: 83.3 us -> none  [the longest x1 45.1 us: on_device(): lax.psum((grad_gain_one, grad_gain_two), ('dp', 'mp'))]
    reduce_scatter x1 -> x0, waiting for transfers between devices: 35.7 us -> none  [reduce_features(): lax.psum_scatter(values_in.astype(jnp.bfloat16), 'mp', scatter_dimension=...]
    all_gather x1 -> x0, blocking collectives: 34.7 us -> none  [on_device(): grad_pieces = lax.all_gather(local_in[None], 'dp', axis=0, tiled=True)]
    convert_element_type x10 -> x4, other arithmetic: 20.9 us -> 9.27 us  [the longest x3 9.25 us: on_device(): r.astype(jnp.float32)]
    dot_general x4 -> x0, matrix products: 11.3 us -> none  [dot(): lax.dot_general(left, right, ((dims[0], dims[1]), ((), ())), preferred_el...]
    unnamed x89 -> x61, local copies, waits for them, and re-layouts: 8.28 us -> 13.5 us
  transfers between devices with their start and end apart: 8 -> 5, of which waited for: 3 -> 1; matrix products, arithmetic and copies ran while one was open for 7% -> 6% of each run, Pallas kernels for 10% -> 8%
where the time goes in v3:
time: 484 us; the launch traced here: 483 us
  Pallas kernels  339 us (70%)
  waiting for transfers between devices  36.9 us (8%)
  blocking collectives  30.6 us (6%)
  other arithmetic  26.3 us (5%)
  local copies, waits for them, and re-layouts  23.9 us (5%)
  between operations  14.5 us (3%)
  starting transfers between devices  7.27 us (2%)
  matrix products  5 us (1%)
    pallas_call x1, Pallas kernels, tail_phase(): pl.pallas_call(functools.partial(tail_kernel, count, half, block), out_sh...  157 us
    pallas_call x1, Pallas kernels, middle_phase(): pl.pallas_call(functools.partial(middle_kernel, chunks), out_shape=(out((...  138 us
    all_gather x2, waiting for transfers between devices, gather_features(): return lax.all_gather(values_in, 'mp', axis=1, tiled=True)  35.5 us
    all_gather x1, blocking collectives, on_device(): pieces = lax.all_gather(local_end[None], 'dp', axis=0, tiled=True)  30.6 us
    pallas_call x2, Pallas kernels, ssm_forward(): pl.pallas_call(functools.partial(forward_kernel, span, tiles), out_shape=...  18.3 us
    unnamed x61, local copies, waits for them, and re-layouts  13.5 us
    pallas_call x2, Pallas kernels, attend_back(): pl.pallas_call(functools.partial(attend_back_kernel, tiles_of(rows, shift...  12 us
    pallas_call x2, Pallas kernels, attend(): pl.pallas_call(functools.partial(attend_kernel, tiles_of(rows, shift), sh...  11.6 us
  transfers between devices with their start and end apart: 5, of which 1 were waited for; matrix products, arithmetic and copies ran while one was open for 6% of the time, Pallas kernels for 8%

profile of v3, /device:TPU:0, one launch (start us, length us, event | category | flops | bytes accessed | tf_op | source)
XLA Modules:
  0.0 483.2 jit_solution(5530256924322779720)
XLA Ops:
  7.2 0.7 all-gather.4.cloned.1.call-update
  8.0 0.7 all-gather.6.cloned.1.call-update
  8.7 0.8 reduce-window.4
  9.6 0.8 fusion.19
  11.0 0.7 fusion.11
  11.8 35.5 %all-gather.4.cloned.1.call-done = bf16[2048,1024]{1,0:T(8,128)(2,1)} async-done(((bf16[2048,256]{1,0:T(8,128)(2,1)}), bf16[2048,1024]{1,0:T(8,128)(2,1)}) %all-gather.4.cloned.1.call-update) | async-done | bytes 4194320 | tf_op jit(solution)/shard_map/all_gather | solution.py:1129
  47.3 3.0 convert_reduce_fusion
  50.8 1.4 fusion.2
  52.2 1.4 fusion.4.n1_hbm
  53.6 1.3 fusion.22
  55.0 0.6 copy-done.9
  55.6 0.7 copy-done.10
  56.4 1.3 slice.156
  57.9 1.0 ssm_ends.1
  58.9 30.6 %all-gather = f32[128,256]{1,0:T(8,128)S(1)} all-gather(f32[16,256]{1,0:T(8,128)S(1)} %ssm_ends.1), channel_id=2, replica_groups=mesh['dp'=8,'mp'=4] {'dp'}, dimensions={0}, use_global_device_ids=true | all-gather | bytes 147456 | tf_op jit(solution)/shard_map/all_gather | solution.py:1220
  89.6 4.4 ssm_long.1
  94.0 1.0 copy-done.5
  95.0 1.5 slice.130
  96.5 3.4 collective-permute-start
  99.8 1.9 copy.38.u_in
  101.7 13.9 %ssm_short.1 = (bf16[1536,256]{1,0:T(8,128)(2,1)S(1)}, bf16[1536,256]{1,0:T(8,128)(2,1)S(1)}, f32[24,2,128,128]{3,2,1,0:T(8,128)}) custom-call(s32[2]{0:T(128)S(1)} %pad_add_fusion.bounds_ref.starts_ref, f32[1536,256]{1,0:T(8,128)S(1)} %copy.38.u_in, f32[3,16,256]{2,1,0:T(8,128)S(1)} %pad_maximum_fusion.6.par_ref, f32[16,256]{1,0:T(8,128)S(1)} %get-tuple-element.131.far_ref, ...), custom_call_target="tpu_custom_call" | custom-call | tf_op jit(solution)/shard_map/ssm_short/pallas_call | solution.py:295
  115.7 3.7 convolution_convert_fusion
  119.4 2.5 pad_maximum_fusion.ckpt_hbm
  122.0 1.3 copy.34.inv_ref
  123.3 2.5 collective-permute-start.1
  125.9 2.9 copy.33
  128.8 8.9 %attend_short.1 = (bf16[1536,256]{1,0:T(8,128)(2,1)S(1)}, f32[2,1,1536]{2,1,0:T(1,128)S(1)}) custom-call(s32[2]{0:T(128)S(1)} %pad_add_fusion.bounds_ref.starts_ref, bf16[1536,256]{1,0:T(8,128)(2,1)S(1)} %slice.155.q_ref, bf16[1536,256]{1,0:T(8,128)(2,1)S(1)} %get-tuple-element.66.k_ref, bf16[1536,256]{1,0:T(8,128)(2,1)S(1)} %get-tuple-element.67.v_ref), custom_call_target="tpu_custom_call" | custom-call | tf_op jit(solution)/shard_map/attend_short/pallas_call | solution.py:384
  137.7 0.8 constant_dynamic-update-slice_fusion.3
  138.6 1.0 constant_dynamic-update-slice_fusion.k_ref
  139.6 2.7 attend_long.1
  142.3 1.0 pad_maximum_fusion.3.att_ref
  143.4 138.3 %middle_phase.1 = (bf16[2048,256]{1,0:T(8,128)(2,1)}, f32[2,2048,128]{2,1,0:T(8,128)}, bf16[2048,256]{1,0:T(8,128)(2,1)}, bf16[2304,1024]{1,0:T(8,128)(2,1)}, f32[8,1024]{1,0:T(8,128)}) custom-call(bf16[2048,256]{1,0:T(8,128)(2,1)} %pad_maximum_fusion.3.att_ref, bf16[2048,256]{1,0:T(8,128)(2,1)} %tok_ref.1, ...), custom_call_target="tpu_custom_call" | custom-call | flops 30000001024 | bytes 30000000 | tf_op jit(solution)/shard_map/middle_phase/pallas_call | solution.py:671
  281.6 1.0 slice.136.g_ref
  282.6 1.2 slice.142.g_ref
  283.8 1.0 copy-done.1
  284.8 1.0 copy-done.3
  285.8 2.8 attend_back_long.1
  288.7 1.3 collective-permute-start.2
  290.0 9.2 %attend_back_short.1 = (bf16[1536,256]{1,0:T(8,128)(2,1)S(1)}, f32[2,1536,128]{2,1,0:T(8,128)S(1)}, f32[2,1536,128]{2,1,0:T(8,128)S(1)}) custom-call(s32[2]{0:T(128)S(1)} %pad_add_fusion.bounds_ref.starts_ref, bf16[1536,256]{1,0:T(8,128)(2,1)S(1)} %slice.155.q_ref, bf16[1536,256]{1,0:T(8,128)(2,1)S(1)} %get-tuple-element.66.k_ref, ...), custom_call_target="tpu_custom_call" | custom-call | tf_op jit(solution)/shard_map/attend_back_short/pallas_call | solution.py:420
  299.2 1.0 pad_maximum_fusion.4.gq_ref
  300.3 2.3 pad_maximum_fusion.1
  302.6 157.4 %tail_phase.1 = (bf16[2048,256]{1,0:T(8,128)(2,1)}, bf16[2560,1024]{1,0:T(8,128)(2,1)}, bf16[256,1024]{1,0:T(8,128)(2,1)}, f32[48,256]{1,0:T(8,128)}, f32[8,256]{1,0:T(8,128)}) custom-call(s32[2]{0:T(128)} %copy-done.7, bf16[2304,1024]{1,0:T(8,128)(2,1)} %get-tuple-element.70.grads_hbm, bf16[2048,1024]{1,0:T(8,128)(2,1)} %copy-done.9, ...), custom_call_target="tpu_custom_call" | custom-call | flops 6000000000 | bytes 40000000 | tf_op jit(solution)/shard_map/tail_phase/pallas_call | solution.py:1106
  460.0 2.4 slice_convert_fusion.2
  462.4 6.7 %slice_convert_fusion = (f32[1024,1024]{1,0:T(8,128)}, f32[1024,1024]{1,0:T(8,128)}) fusion(bf16[2560,1024]{1,0:T(8,128)(2,1)} %get-tuple-element.87), kind=kLoop, calls=%fused_computation.11 | loop fusion | flops 2097152 | bytes 12582912 | tf_op jit(solution)/shard_map/convert_element_type | solution.py:1258
  471.8 1.3 copy.35
  473.1 1.3 copy.36
  474.4 1.0 copy.47
  475.4 1.0 copy.48
  (80 shorter events, 4.6 us)
Async XLA Ops:
  7.2 40.1 %all-gather.4.cloned.1.call-start = ((), (), s32[]{:S(2)}) async-start(), calls=%async_computation | async-start | bytes 5242880 | tf_op jit(solution)/shard_map/all_gather | solution.py:1129
  7.9 135.5 %all-gather.6.cloned.1.call-start = ((), (), s32[]{:S(2)}) async-start(), calls=%async_computation.1 | async-start | bytes 5242880 | tf_op jit(solution)/shard_map/all_gather | solution.py:1129
  9.6 280.4 %copy-start.7 = (s32[2]{0:T(128)}, s32[2]{0:T(128)S(1)}, u32[]{:S(2)}) copy-start(s32[2]{0:T(128)S(1)} %pad_add_fusion.bounds_ref.starts_ref) | copy-start | bytes 28
  10.4 41.7 %copy-start.17 = (f32[16,256]{1,0:T(8,128)}, f32[16,256]{1,0:T(8,128)S(1)}, u32[]{:S(2)}) copy-start(f32[16,256]{1,0:T(8,128)S(1)} %get-tuple-element.135) | copy-start | bytes 49156
  11.8 90.0 %copy-start.4 = (f32[3,16,256]{2,1,0:T(8,128)}, f32[3,16,256]{2,1,0:T(8,128)S(1)}, u32[]{:S(2)}) copy-start(f32[3,16,256]{2,1,0:T(8,128)S(1)} %pad_maximum_fusion.6.par_ref) | copy-start | bytes 147460
  11.8 40.4 %copy-start.23 = (f32[1024]{0:T(1024)S(1)}, f32[1024]{0:T(1024)}, u32[]{:S(2)}) copy-start(f32[1024]{0:T(1024)} %param.19) | copy-start | bytes 12292
  47.3 3.4 copy-start.8
  52.2 1.4 copy-start.14
  53.6 2.0 copy-start.9
  54.9 1.4 copy-start.10
  94.0 1.0 copy-start.5
  96.5 41.2 %collective-permute-start = (bf16[128,256]{1,0:T(8,128)(2,1)}, bf16[128,256]{1,0:T(8,128)(2,1)S(1)}, u32[]{:S(2)}, u32[]{:S(2)}) collective-permute-start(bf16[128,256]{1,0:T(8,128)(2,1)} %slice.130), channel_id=1, source_target_pairs={{0,4},{4,8},{8,12},{12,16},{16,20},{20,24},{24,28},{1,5},{5,9},{9,... | collective-permute-start | bytes 196616 | tf_op jit(solution)/shard_map/ppermute | solution.py:1141
  115.7 3.7 copy-start.6
  115.7 3.7 copy-start.11
  123.3 14.4 %collective-permute-start.1 = (bf16[128,256]{1,0:T(8,128)(2,1)S(1)}, bf16[128,256]{1,0:T(8,128)(2,1)}, u32[]{:S(2)}, u32[]{:S(2)}) collective-permute-start(bf16[128,256]{1,0:T(8,128)(2,1)S(1)} %slice.131), channel_id=1, source_target_pairs={{0,4},{4,8},{8,12},{12,16},{16,20},{20,24},{24,28},{1,5},{5,9},{9,... | collective-permute-start | bytes 196616 | tf_op jit(solution)/shard_map/ppermute | solution.py:1141
  139.6 142.1 %copy-start = (bf16[640,256]{1,0:T(8,128)(2,1)}, bf16[640,256]{1,0:T(8,128)(2,1)S(1)}, u32[]{:S(2)}) copy-start(bf16[640,256]{1,0:T(8,128)(2,1)S(1)} %constant_dynamic-update-slice_fusion.k_ref) | copy-start | bytes 983044
  139.6 142.0 %copy-start.2 = (bf16[640,256]{1,0:T(8,128)(2,1)}, bf16[640,256]{1,0:T(8,128)(2,1)S(1)}, u32[]{:S(2)}) copy-start(bf16[640,256]{1,0:T(8,128)(2,1)S(1)} %constant_dynamic-update-slice_fusion.2.v_ref) | copy-start | bytes 983044
  283.8 1.0 copy-start.1
  284.8 1.0 copy-start.3
  288.7 11.5 %collective-permute-start.2 = (bf16[2,2,128,128]{3,2,1,0:T(8,128)(2,1)S(1)}, bf16[2,2,128,128]{3,2,1,0:T(8,128)(2,1)S(1)}, u32[]{:S(2)}, u32[]{:S(2)}) collective-permute-start(bf16[2,2,128,128]{3,2,1,0:T(8,128)(2,1)S(1)} %pad_maximum_fusion.5), channel_id=1, source_target_pairs={{4,0},{8,4},{12,8},{16,12},{20,16},{24,20},{28,24},{5,1},{9,5},{13... | collective-permute-start | bytes 393224 | tf_op jit(solution)/shard_map/ppermute | solution.py:1141
  462.4 6.8 %copy-start.24 = (f32[8,256]{1,0:T(8,128)S(1)}, f32[8,256]{1,0:T(8,128)}, u32[]{:S(2)}) copy-start(f32[8,256]{1,0:T(8,128)} %get-tuple-element.85) | copy-start | bytes 24580
  462.4 8.0 %copy-start.16 = (f32[256,16]{0,1:T(8,128)S(1)}, f32[256,16]{0,1:T(8,128)}, u32[]{:S(2)}) copy-start(f32[256,16]{0,1:T(8,128)} %param.26) | copy-start | bytes 49156
  462.4 8.0 %copy-start.19 = (f32[48,256]{1,0:T(8,128)S(1)}, f32[48,256]{1,0:T(8,128)}, u32[]{:S(2)}) copy-start(f32[48,256]{1,0:T(8,128)} %get-tuple-element.88) | copy-start | bytes 147460
  462.4 8.0 %copy-start.20 = (f32[256,16]{0,1:T(8,128)S(1)}, f32[256,16]{0,1:T(8,128)}, u32[]{:S(2)}) copy-start(f32[256,16]{0,1:T(8,128)} %param.29) | copy-start | bytes 49156
  462.4 8.0 %copy-start.21 = (f32[256,16]{0,1:T(8,128)S(1)}, f32[256,16]{0,1:T(8,128)}, u32[]{:S(2)}) copy-start(f32[256,16]{0,1:T(8,128)} %param.28) | copy-start | bytes 49156
  462.4 8.6 %copy-start.18 = (f32[16,256]{1,0:T(8,128)S(1)}, f32[16,256]{1,0:T(8,128)}, u32[]{:S(2)}) copy-start(f32[16,256]{1,0:T(8,128)} %copy-done.17) | copy-start | bytes 49156
  462.4 8.6 %copy-start.22 = (f32[256,16]{0,1:T(8,128)S(1)}, f32[256,16]{0,1:T(8,128)}, u32[]{:S(2)}) copy-start(f32[256,16]{0,1:T(8,128)} %param.27) | copy-start | bytes 49156
  462.4 9.2 %copy-start.15 = (bf16[256,1024]{1,0:T(8,128)(2,1)S(1)}, bf16[256,1024]{1,0:T(8,128)(2,1)}, u32[]{:S(2)}) copy-start(bf16[256,1024]{1,0:T(8,128)(2,1)} %get-tuple-element.86) | copy-start | bytes 1572868
  469.2 5.2 %copy-start.12 = (bf16[2048,256]{1,0:T(8,128)(2,1)S(1)}, bf16[2048,256]{1,0:T(8,128)(2,1)}, u32[]{:S(2)}) copy-start(bf16[2048,256]{1,0:T(8,128)(2,1)} %get-tuple-element.153) | copy-start | bytes 3145732
  473.1 2.3 copy-start.13
Sparse Core Ops, SparseCore 0:
  9.6 37.7 all-gather.3
  48.9 35.0 all-gather.5

commit v4 on v3

--- a/solution.py
+++ b/solution.py
@@ -461,18 +461,23 @@
 
 
 class Gather:
-    def __init__(self, mover, base, full, rows):
-        self.mover, self.base, self.full, self.rows = mover, base, full, rows
+    def __init__(self, mover, base, full, rows, own=None):
+        self.mover, self.base, self.full, self.rows, self.own = mover, base, full, rows, own
         self.me, self.mate, self.over, self.far = group_of_four()
 
     def at(self, owner, c):
         return self.full.at[owner, pl.ds(pl.multiple_of(c * self.rows, self.rows), self.rows)]
 
+    def mine(self, c):
+        if self.own is None:
+            return self.at(self.me, c)
+        return self.own.at[pl.ds(pl.multiple_of(c * self.rows, self.rows), self.rows)]
+
     def near(self, c):
-        return self.mover.copy(self.at(self.me, c), self.at(self.me, c), self.base, c, self.mate)
+        return self.mover.copy(self.mine(c), self.at(self.me, c), self.base, c, self.mate)
 
     def across(self, c):
-        return self.mover.copy(self.at(self.me, c), self.at(self.me, c), self.base + 1, c, self.over)
+        return self.mover.copy(self.mine(c), self.at(self.me, c), self.base + 1, c, self.over)
 
     def onward(self, c):
         return self.mover.copy(self.at(self.over, c), self.at(self.over, c), self.base + 2, c, self.mate)
@@ -583,7 +588,7 @@
             inv_ref[mine, :] = inv
             n2_ref[mine, :] = (centred * inv * gain_ref[...]).astype(jnp.bfloat16)
 
-        cot = cot_ref[span(c), :]
+        cot = jnp.concatenate([cot_ref[d, span(c), :] for d in range(4)], axis=1)
         pre_ref[...] = mm(n2_ref[...], w_up_ref[...], 1, 0)
         gact_ref[...] = mm(cot, w_down_ref[...], 1, 1)
 
@@ -616,8 +621,7 @@
         gup_ref[...] += mm(n2_ref[...], gpre_ref[...], 0, 0)
 
     def finish_sums(c):
-        own = pl.ds(pl.multiple_of(me * width, width), width)
-        gm = cot_ref[span(c), own].astype(jnp.float32) + sums[2].finish(c)
+        gm = cot_ref[me, span(c), :].astype(jnp.float32) + sums[2].finish(c)
         for lt in range(width // LANES):
             gm_ref[lt, span(c), :] = gm[:, cut(lt, LANES)]
         gm_full[me, span(c), :] = gm.astype(jnp.bfloat16)
@@ -657,7 +661,7 @@
 
 def middle_phase(att, tok, cot_full, w_out, w_up, w_down, gain):
     rows, width = att.shape
-    full = cot_full.shape[1]
+    full = w_out.shape[1]
     hidden = w_up.shape[1]
     chunks = rows // ROWS
     bf = jnp.bfloat16
@@ -1125,6 +1129,240 @@
         name="tail_phase")(bounds, grads, n1, u, gk, gv, ckpt, gm, gq, inv, w_in_t, w_query_t, par, far, rate, gain, gain_two_parts)
 
 
+def forward_pass(bounds_ref, u_ref, wide_ref, state_ref, span, tiles, row0, beside):
+    state_ref[...] = jnp.zeros_like(state_ref)
+
+    @pl.loop(0, span // GROUP)
+    def _(group):
+        keep = masks_of(bounds_ref, span, group)
+        for lt in range(tiles):
+            u = [u_ref[lt, pl.ds(row0 + group * GROUP + j, SEG, stride=span), :] for j in range(GROUP)]
+            for n in range(STATES):
+                mine = slice(n * SEG, (n + 1) * SEG)
+                a = wide_ref[0, n, lt]
+                s = state_ref[lt, mine, :]
+                for j in range(GROUP):
+                    s = a * s
+                    if keep is not None:
+                        s = s * keep[j]
+                    s = s + u[j]
+                state_ref[lt, mine, :] = s
+        beside(group)
+
+
+def forward_chain(bounds_ref, state_ref, first, far_ref, span, tiles, write):
+    ends = []
+    for lt in range(tiles):
+        lanes = slice(lt * LANES, (lt + 1) * LANES)
+        start, far = first[:, lanes], far_ref[:, lanes]
+        for seg in range(SEG):
+            rows = pl.ds(seg, STATES, stride=SEG)
+            end = state_ref[lt, rows, :]
+            if write:
+                state_ref[lt, rows, :] = start
+            start = end + far * start * open_segment(bounds_ref, span, seg)
+        ends.append(start)
+    return jnp.concatenate(ends, axis=1)
+
+
+def forward_full(bounds_ref, u_ref, k_ref, v_ref, ckpt_ref, wide_ref, state_ref, span, tiles, row0, group0, beside):
+    @pl.loop(0, span // GROUP)
+    def _(group):
+        keep = masks_of(bounds_ref, span, group)
+        for lt in range(tiles):
+            at = [pl.ds(row0 + group * GROUP + j, SEG, stride=span) for j in range(GROUP)]
+            u = [u_ref[lt, r, :] for r in at]
+            ks = [jnp.zeros((SEG, LANES), jnp.float32)] * GROUP
+            vs = [jnp.zeros((SEG, LANES), jnp.float32)] * GROUP
+            for n in range(STATES):
+                mine = slice(n * SEG, (n + 1) * SEG)
+                a, ck, cv = wide_ref[0, n, lt], wide_ref[1, n, lt], wide_ref[2, n, lt]
+                s = state_ref[lt, mine, :]
+                ckpt_ref[group0 + group, lt, mine, :] = s
+                for j in range(GROUP):
+                    s = a * s
+                    if keep is not None:
+                        s = s * keep[j]
+                    s = s + u[j]
+                    ks[j] = ks[j] + ck * s
+                    vs[j] = vs[j] + cv * s
+                state_ref[lt, mine, :] = s
+            for j in range(GROUP):
+                k_ref[lt, at[j], :] = ks[j]
+                v_ref[lt, at[j], :] = vs[j]
+        beside(group)
+
+
+COT_ROWS = 512
+
+
+def head_kernel(count, bounds_ref, cot_in, tok_ref, w_in_ref, w_query_ref, par_ref, far_ref, rate_ref, gain_ref,
+                inv_ref, n1_hbm, u_hbm, q_hbm, k_hbm, v_hbm, ckpt_hbm, cot_hbm,
+                tok_full, n1_ref, u_ref, q_ref, k_ref, v_ref, k_wide, v_wide, ckpt_ref, wide_ref, state_long, state_short,
+                piece_ref, piece_held, save_sem, mp_send, mp_recv, cot_send, cot_recv, dp_send, dp_recv, ctx_send, ctx_recv):
+    rows, width = tok_ref.shape
+    tiles = width // LANES
+    full = n1_ref.shape[1]
+    me = lax.axis_index("dp")
+    mp = lax.axis_index("mp")
+    chunks = rows // ROWS
+    cot_chunks = rows // COT_ROWS
+    long_span, short_span = LONG_DEV // SEG, (rows - LONG_DEV) // SEG
+    long_groups, short_groups = long_span // GROUP, short_span // GROUP
+    tokens = Gather(Mover(mp_send, mp_recv), 0, tok_full, ROWS, tok_ref)
+    cots = Gather(Mover(cot_send, cot_recv), 0, cot_hbm, COT_ROWS, cot_in)
+    pieces = Spread(count, dp_send, dp_recv)
+    greet_all(count)
+    for c in range(chunks):
+        tokens.start(c)
+    for c in range(cot_chunks):
+        cots.start(c)
+
+    def save(src, dst, i):
+        return pltpu.make_async_copy(src, dst, save_sem.at[i])
+
+    own_cot = save(cot_in, cot_hbm.at[mp], 0)
+    own_cot.start()
+    seg_scan_params(par_ref, wide_ref)
+    tok_full[mp] = tok_ref[...]
+    zero = jnp.zeros((STATES, width), jnp.float32)
+
+    def nothing(step):
+        del step
+
+    def span_of(c):
+        return pl.ds(pl.multiple_of(c * ROWS, ROWS), ROWS)
+
+    def project(c):
+        tokens.finish(c)
+
+        @pl.loop(0, ROWS // SUB)
+        def _(sub):
+            here = pl.ds(pl.multiple_of(c * ROWS + sub * SUB, SUB), SUB)
+            v = normed(tok_full, c, sub, ROWS)
+            mean = jnp.mean(v, axis=1, keepdims=True)
+            centred = v - mean
+            inv = lax.rsqrt(jnp.mean(centred * centred, axis=1, keepdims=True) + EPS)
+            inv_ref[here, :] = inv
+            n1_ref[here, :] = (centred * inv * gain_ref[...]).astype(jnp.bfloat16)
+
+        n1 = n1_ref[span_of(c), :]
+        u = mm(n1, w_in_ref[...], 1, 0)
+        for lt in range(tiles):
+            u_ref[lt, span_of(c), :] = u[:, lt * LANES : (lt + 1) * LANES]
+        q_ref[span_of(c), :] = mm(n1, w_query_ref[...], 1, 0).astype(jnp.bfloat16)
+
+    def context(src, i):
+        rows_out = src.at[pl.ds(LONG_DEV, CTX)]
+        return pltpu.make_async_remote_copy(
+            src_ref=rows_out, dst_ref=src.at[pl.ds(0, CTX)], send_sem=ctx_send.at[i], recv_sem=ctx_recv.at[i],
+            device_id=((me + 1) % count, mp), device_id_type=MESH)
+
+    def narrow(first, size):
+        for lt in range(tiles):
+            lanes = slice(lt * LANES, (lt + 1) * LANES)
+            k_ref[CTX + first : CTX + first + size, lanes] = k_wide[lt, first : first + size, :].astype(jnp.bfloat16)
+            v_ref[CTX + first : CTX + first + size, lanes] = v_wide[lt, first : first + size, :].astype(jnp.bfloat16)
+
+    @pl.loop(0, chunks + 1)
+    def _(i):
+        @pl.when(i < chunks)
+        def _():
+            tokens.forward(i)
+
+        @pl.when(i >= 1)
+        def _():
+            project(i - 1)
+
+        @pl.when(i == LONG_DEV // ROWS)
+        def _():
+            forward_pass(None, u_ref, wide_ref, state_long, long_span, tiles, 0, nothing)
+            piece_ref[...] = forward_chain(None, state_long, zero, far_ref.at[0], long_span, tiles, False)
+            pieces.start(lambda o: piece_ref, lambda o: piece_held.at[me])
+
+    pieces.wait(lambda o: piece_ref, lambda o: piece_held.at[me])
+    piece_held[me] = zero
+
+    def fold(d, total):
+        gap = me - 1 - d
+        weight = jnp.exp(rate_ref[...] * (-LONG_DEV * jnp.maximum(gap, 0)).astype(jnp.float32))
+        return total + jnp.where(gap >= 0, weight * piece_held[d], 0.0)
+
+    first = lax.fori_loop(0, count, fold, zero)
+    saves = [save(n1_ref, n1_hbm, 1), save(u_ref, u_hbm, 2), save(q_ref, q_hbm, 3)]
+    for s in saves:
+        s.start()
+    forward_chain(None, state_long, first, far_ref.at[0], long_span, tiles, True)
+    forward_full(None, u_ref, k_wide, v_wide, ckpt_ref, wide_ref, state_long, long_span, tiles, 0, 0, nothing)
+    narrow(0, LONG_DEV)
+    contexts = [context(k_ref, 0), context(v_ref, 1)]
+    for copy in contexts:
+        copy.start()
+
+    cots.forward(0)
+    forward_pass(bounds_ref, u_ref, wide_ref, state_short, short_span, tiles, LONG_DEV, nothing)
+    cots.forward(1)
+    forward_chain(bounds_ref, state_short, zero, far_ref.at[1], short_span, tiles, True)
+
+    def beside(group):
+        @pl.when(group == short_groups // 2)
+        def _():
+            cots.forward(2)
+
+    forward_full(bounds_ref, u_ref, k_wide, v_wide, ckpt_ref, wide_ref, state_short, short_span, tiles, LONG_DEV, long_groups, beside)
+    cots.forward(3)
+    last = [save(ckpt_ref, ckpt_hbm, 4)]
+    last[0].start()
+    narrow(LONG_DEV, rows - LONG_DEV)
+    for copy in contexts:
+        copy.wait()
+    for s in (save(k_ref, k_hbm, 5), save(v_ref, v_hbm, 6)):
+        s.start()
+        last.append(s)
+    for c in range(cot_chunks):
+        cots.finish(c)
+    for s in saves + last + [own_cot]:
+        s.wait()
+
+
+def head_phase(bounds, cot, tok, w_in, w_query, par, far, rate, gain, count):
+    rows, width = tok.shape
+    full = w_in.shape[0]
+    tiles = width // LANES
+    bf = jnp.bfloat16
+    groups = rows // SEG // GROUP
+
+    def out(shape, dtype):
+        return jax.ShapeDtypeStruct(shape, dtype)
+
+    def buf(*shape):
+        return pltpu.VMEM(shape, bf)
+
+    def wide(*shape):
+        return pltpu.VMEM(shape, jnp.float32)
+
+    ANY = pl.BlockSpec(memory_space=pl.ANY)
+    dma = pltpu.SemaphoreType.DMA
+    chunks, cot_chunks = rows // ROWS, rows // COT_ROWS
+    return pl.pallas_call(
+        functools.partial(head_kernel, count),
+        out_shape=(out((rows, 1), jnp.float32), out((rows, full), bf), out((tiles, rows, LANES), jnp.float32), out((rows, width), bf),
+                   out((CTX + rows, width), bf), out((CTX + rows, width), bf),
+                   out((groups, tiles, STATES * SEG, LANES), jnp.float32), out((4, rows, width), bf)),
+        in_specs=[SMEM, ANY] + [VMEM] * 7, out_specs=(VMEM,) + (ANY,) * 7,
+        scratch_shapes=[
+            buf(4, rows, width), buf(rows, full), wide(tiles, rows, LANES), buf(rows, width), buf(CTX + rows, width), buf(CTX + rows, width),
+            wide(tiles, rows, LANES), wide(tiles, rows, LANES), wide(groups, tiles, STATES * SEG, LANES),
+            wide(3, STATES, tiles, SEG, LANES), wide(tiles, STATES * SEG, LANES), wide(tiles, STATES * SEG, LANES),
+            wide(STATES, width), wide(count, STATES, width),
+            dma((7,)), dma((3, chunks)), dma((3, chunks)), dma((3, cot_chunks)), dma((3, cot_chunks)), dma((count,)), dma((count,)),
+            dma((2,)), dma((2,)),
+        ],
+        compiler_params=pltpu.CompilerParams(collective_id=2, has_side_effects=True, vmem_limit_bytes=56 * 2**20),
+        cost_estimate=pl.CostEstimate(flops=3 * 10**9, bytes_accessed=40 * 10**6, transcendentals=0),
+        name="head_phase")(bounds, cot, tok, w_in, w_query, par, far, rate, gain)
+
+
 def gather_features(values_in):
     return lax.all_gather(values_in, "mp", axis=1, tiled=True)
 
@@ -1209,23 +1447,13 @@
     far_long = jnp.exp(-rate_t * (LONG_DEV // SEG))
     far_short = jnp.exp(-rate_t * (short_rows // SEG))
 
-    tokens_full = gather_features(tokens).astype(jnp.float32)
-    cotangent_full = gather_features(cotangent)
-    normed_one, inverse_one, hidden_one = norm_forward(tokens_full, gain_one)
-    normed_one_low = hidden_one.astype(low)
-    ssm_input = jnp.dot(normed_one_low, w_in, preferred_element_type=jnp.float32)
-    queries = jnp.dot(normed_one_low, w_query, preferred_element_type=jnp.float32).astype(low)
-    u_long, u_short = ssm_input[:LONG_DEV], ssm_input[LONG_DEV:]
-    local_end = ssm_ends(no_bound, u_long, par, far_long)
-    pieces = lax.all_gather(local_end[None], "dp", axis=0, tiled=True)
-    others = jnp.arange(pieces.shape[0], dtype=jnp.int32)
-    state_in = fold_pieces(pieces, rate_t, device - 1 - others)
-    zero_state = jnp.zeros_like(state_in)
-    k_short, v_short, ckpt_short = ssm_forward(short_starts, u_short, par, far_short, zero_state, "ssm_short")
-    k_long, v_long, ckpt_long = ssm_forward(no_bound, u_long, par, far_long, state_in, "ssm_long")
-    ctx_k, ctx_v = from_behind((k_long[LONG_DEV - CTX :], v_long[LONG_DEV - CTX :]), "dp", 1)
-    k_long = jnp.concatenate([ctx_k, k_long])
-    v_long = jnp.concatenate([ctx_v, v_long])
+    count = lax.axis_size("dp")
+    far = jnp.stack([far_long, far_short])
+    inverse_one, normed_one_low, u_tiles, queries, k_ext, v_ext, ckpt, cotangent_full = head_phase(
+        short_starts, cotangent, tokens, w_in, w_query, par, far, rate_t, gain_one[None], count
+    )
+    k_long, v_long = k_ext[: CTX + LONG_DEV], v_ext[: CTX + LONG_DEV]
+    k_short, v_short = k_ext[CTX + LONG_DEV :], v_ext[CTX + LONG_DEV :]
     q_long, q_short = queries[:LONG_DEV], queries[LONG_DEV:]
     att_short, lse_short = attend(short_starts, q_short, k_short, v_short, 0, "attend_short")
     att_long, lse_long = attend(long_low, q_long, k_long, v_long, CTX, "attend_long")
@@ -1245,12 +1473,10 @@
     gv_long = gv_long[:, CTX:].at[:, LONG_DEV - CTX :].add(back[1])
     gk = jnp.concatenate([gk_long, gk_short], axis=1)
     gv = jnp.concatenate([gv_long, gv_short], axis=1)
-    u_tiles = ssm_input.reshape(-1, local_width // LANES, LANES).transpose(1, 0, 2)
-    ckpt = jnp.concatenate([ckpt_long, ckpt_short])
     grad_queries = jnp.concatenate([gq_long, gq_short])
     grad_tokens, total, win_t, sums, gains = tail_phase(
         short_starts, grads, normed_one_low, u_tiles, gk, gv, ckpt, grad_middle, grad_queries, inverse_one,
-        w_in, w_query, par, jnp.stack([far_long, far_short]), rate_t, gain_one[None], gain_two_parts, lax.axis_size("dp"),
+        w_in, w_query, par, far, rate_t, gain_one[None], gain_two_parts, count,
     )
     hidden, full = w_down.shape
     rows_of = [total[:hidden], total[hidden : hidden + full], total[hidden + full : hidden + full + local_width],

time: 484 us -> 409 us (0.85)
  Pallas kernels: 339 us -> 377 us
  waiting for transfers between devices: 36.9 us -> 0.01 us
  blocking collectives: 30.6 us -> 0 us
  between operations: 14.5 us -> 0.94 us
  local copies, waits for them, and re-layouts: 23.9 us -> 10.5 us
  other arithmetic: 26.3 us -> 19.1 us
  starting transfers between devices: 7.27 us -> 1.29 us
  matrix products: 5 us -> 0 us
    pallas_call x3 -> x1, Pallas kernels: 19.4 us -> 59.1 us  [head_phase(): pl.pallas_call(functools.partial(head_kernel, count), out_shape=(out((row...]
    all_gather x2 -> x0, waiting for transfers between devices: 35.5 us -> none  [gather_features(): return lax.all_gather(values_in, 'mp', axis=1, tiled=True)]
    all_gather x1 -> x0, blocking collectives: 30.6 us -> none  [on_device(): pieces = lax.all_gather(local_end[None], 'dp', axis=0, tiled=True)]
    unnamed x61 -> x33, local copies, waits for them, and re-layouts: 13.5 us -> 6.88 us
    ppermute x3 -> x1, starting transfers between devices: 7.2 us -> 1.29 us  [from_behind(): lax.ppermute(value, axis, [(source, source + steps) for source in range(i...]
    dot_general x2 -> x0, matrix products: 5 us -> none  [the longest x1 3.7 us: on_device(): jnp.dot(normed_one_low, w_query, preferred_element_type=jnp.float32)]
  transfers between devices with their start and end apart: 5 -> 1, of which waited for: 1 -> 0; matrix products, arithmetic and copies ran while one was open for 6% -> 0% of each run, Pallas kernels for 8% -> 2%
where the time goes in v4:
time: 409 us
  Pallas kernels  377 us (92%)
  other arithmetic  19.1 us (5%)
  local copies, waits for them, and re-layouts  10.5 us (3%)
    pallas_call x1, Pallas kernels, tail_phase(): pl.pallas_call(functools.partial(tail_kernel, count, half, block), out_sh...  155 us
    pallas_call x1, Pallas kernels, middle_phase(): pl.pallas_call(functools.partial(middle_kernel, chunks), out_shape=(out((...  139 us
    pallas_call x1, Pallas kernels, head_phase(): pl.pallas_call(functools.partial(head_kernel, count), out_shape=(out((row...  59.1 us
    pallas_call x2, Pallas kernels, attend_back(): pl.pallas_call(functools.partial(attend_back_kernel, tiles_of(rows, shift...  12 us
    pallas_call x2, Pallas kernels, attend(): pl.pallas_call(functools.partial(attend_kernel, tiles_of(rows, shift), sh...  11.6 us
    convert_element_type x3, other arithmetic, on_device(): r.astype(jnp.float32)  9.17 us
  transfers between devices with their start and end apart: 1, of which 0 were waited for; matrix products, arithmetic and copies ran while one was open for 0% of the time, Pallas kernels for 2%

profile of v4, /device:TPU:0, one launch (start us, length us, event | category | flops | bytes accessed | tf_op | source)
XLA Modules:
  0.0 408.6 jit_solution(7657837677669690377)
XLA Ops:
  0.6 0.8 reduce-window.4
  1.5 0.6 pad_add_fusion.bounds_ref.starts_ref
  2.1 0.8 exponential_bitcast_fusion.1
  2.9 0.6 pad_maximum_fusion.6.far_ref
  3.5 0.7 fusion.6
  4.2 0.6 pad_maximum_fusion.5.par_ref
  4.8 59.1 %head_phase.1 = (f32[2048,1]{1,0:T(8,128)}, bf16[2048,1024]{1,0:T(8,128)(2,1)}, f32[2,2048,128]{2,1,0:T(8,128)}, bf16[2048,256]{1,0:T(8,128)(2,1)}, bf16[2176,25...) custom-call(s32[2]{0:T(128)} %pad_add_fusion.bounds_ref.starts_ref, ...), custom_call_target="tpu_custom_call" | custom-call | flops 3000000000 | bytes 40000000 | tf_op jit(solution)/shard_map/head_phase/pallas_call | solution.py:1347
  64.0 0.0 copy-start.2
  64.0 0.0 copy-start.1
  64.0 1.1 slice.130.q_ref
  65.1 1.2 slice.133.q_ref
  66.3 0.0 copy-done.2
  66.3 0.0 copy-start
  66.4 0.1 slice.134.k_ref
  66.4 0.0 copy-done.1
  66.5 0.1 slice.135.v_ref
  66.5 0.4 copy-done
  67.0 8.9 %attend_short.1 = (bf16[1536,256]{1,0:T(8,128)(2,1)S(1)}, f32[2,1,1536]{2,1,0:T(1,128)S(1)}) custom-call(s32[2]{0:T(128)S(1)} %copy-done, bf16[1536,256]{1,0:T(8,128)(2,1)S(1)} %slice.133.q_ref, bf16[1536,256]{1,0:T(8,128)(2,1)S(1)} %slice.134.k_ref, bf16[1536,256]{1,0:T(8,128)(2,1)S(1)} %slice.135.v_ref), custom_call_target="tpu_custom_call" | custom-call | tf_op jit(solution)/shard_map/attend_short/pallas_call | solution.py:384
  75.9 2.7 attend_long.1
  78.6 1.0 pad_maximum_fusion.2.att_ref
  79.7 138.5 %middle_phase.1 = (bf16[2048,256]{1,0:T(8,128)(2,1)}, f32[2,2048,128]{2,1,0:T(8,128)}, bf16[2048,256]{1,0:T(8,128)(2,1)}, bf16[2304,1024]{1,0:T(8,128)(2,1)}, f32[8,1024]{1,0:T(8,128)}) custom-call(bf16[2048,256]{1,0:T(8,128)(2,1)} %pad_maximum_fusion.2.att_ref, bf16[2048,256]{1,0:T(8,128)(2,1)} %tok_ref.3, bf16[4,2048,256]{2,1,0:T(8,128)(2,1)} %get-tuple-element.70.cot_ref, ...), custom_call_target="tpu_custom_call" | custom-call | flops 30000001024 | bytes 30000000 | tf_op jit(solution)/shard_map/middle_phase/pallas_call | solution.py:675
  218.2 0.0 copy-start.3
  218.2 1.1 slice.136.g_ref
  219.3 2.8 attend_back_long.1
  222.1 1.3 collective-permute-start
  223.4 0.0 copy-done.3
  223.4 0.1 slice.142.g_ref
  223.6 9.2 %attend_back_short.1 = (bf16[1536,256]{1,0:T(8,128)(2,1)S(1)}, f32[2,1536,128]{2,1,0:T(8,128)S(1)}, f32[2,1536,128]{2,1,0:T(8,128)S(1)}) custom-call(s32[2]{0:T(128)S(1)} %copy-done, bf16[1536,256]{1,0:T(8,128)(2,1)S(1)} %slice.133.q_ref, bf16[1536,256]{1,0:T(8,128)(2,1)S(1)} %slice.134.k_ref, bf16[1536,256]{1,0:T(8,128)(2,1)S(1)} %slice.135.v_ref, ...), custom_call_target="tpu_custom_call" | custom-call | tf_op jit(solution)/shard_map/attend_back_short/pallas_call | solution.py:420
  232.8 1.0 pad_maximum_fusion.3.gq_ref
  233.9 0.0 collective-permute-done
  233.9 2.3 pad_maximum_fusion
  236.3 155.5 %tail_phase.1 = (bf16[2048,256]{1,0:T(8,128)(2,1)}, bf16[2560,1024]{1,0:T(8,128)(2,1)}, bf16[256,1024]{1,0:T(8,128)(2,1)}, f32[48,256]{1,0:T(8,128)}, f32[8,256]{1,0:T(8,128)}) custom-call(s32[2]{0:T(128)} %pad_add_fusion.bounds_ref.starts_ref, bf16[2304,1024]{1,0:T(8,128)(2,1)} %get-tuple-element.72.grads_hbm, bf16[2048,1024]{1,0:T(8,128)(2,1)} %get-tuple-element.73.n1_hbm, ...), custom_call_target="tpu_custom_call" | custom-call | flops 6000000000 | bytes 40000000 | tf_op jit(solution)/shard_map/tail_phase/pallas_call | solution.py:1110
  391.7 2.3 slice_convert_fusion.2
  394.1 0.0 copy-start.10
  394.1 0.0 copy-start.11
  394.1 0.0 copy-start.6
  394.1 6.7 %slice_convert_fusion = (f32[1024,1024]{1,0:T(8,128)}, f32[1024,1024]{1,0:T(8,128)}) fusion(bf16[2560,1024]{1,0:T(8,128)(2,1)} %get-tuple-element.91), kind=kLoop, calls=%fused_computation.2 | loop fusion | flops 2097152 | bytes 12582912 | tf_op jit(solution)/shard_map/convert_element_type | solution.py:1484
  400.8 0.6 copy.30
  401.4 0.6 copy.29
  402.0 0.0 copy-done.7
  402.1 0.6 multiply_bitcast_fusion.2
  402.7 0.6 multiply_bitcast_fusion
  403.3 0.1 convert_bitcast_fusion.1
  403.4 1.3 copy.27
  404.8 1.3 copy.28
  406.1 1.0 copy.35
  407.0 0.6 copy-done.5
  407.7 1.0 copy.36
  (23 shorter events, 0.2 us)
Async XLA Ops:
  64.0 2.3 copy-start.2
  64.0 2.4 copy-start.1
  66.3 0.7 copy-start
  218.2 5.2 %copy-start.3 = (bf16[2048,256]{1,0:T(8,128)(2,1)S(1)}, bf16[2048,256]{1,0:T(8,128)(2,1)}, u32[]{:S(2)}) copy-start(bf16[2048,256]{1,0:T(8,128)(2,1)} %get-tuple-element.75) | copy-start | bytes 3145732
  222.1 11.7 %collective-permute-start = (bf16[2,2,128,128]{3,2,1,0:T(8,128)(2,1)S(1)}, bf16[2,2,128,128]{3,2,1,0:T(8,128)(2,1)S(1)}, u32[]{:S(2)}, u32[]{:S(2)}) collective-permute-start(bf16[2,2,128,128]{3,2,1,0:T(8,128)(2,1)S(1)} %pad_maximum_fusion.4), channel_id=1, source_target_pairs={{4,0},{8,4},{12,8},{16,12},{20,16},{24,20},{28,24},{5,1},{9,5},{13... | collective-permute-start | bytes 393224 | tf_op jit(solution)/shard_map/ppermute | solution.py:1379
  394.1 6.8 %copy-start.12 = (f32[8,256]{1,0:T(8,128)S(1)}, f32[8,256]{1,0:T(8,128)}, u32[]{:S(2)}) copy-start(f32[8,256]{1,0:T(8,128)} %get-tuple-element.89) | copy-start | bytes 24580
  394.1 8.0 %copy-start.7 = (f32[256,16]{0,1:T(8,128)S(1)}, f32[256,16]{0,1:T(8,128)}, u32[]{:S(2)}) copy-start(f32[256,16]{0,1:T(8,128)} %param.26) | copy-start | bytes 49156
  394.1 8.0 %copy-start.8 = (f32[48,256]{1,0:T(8,128)S(1)}, f32[48,256]{1,0:T(8,128)}, u32[]{:S(2)}) copy-start(f32[48,256]{1,0:T(8,128)} %get-tuple-element.92) | copy-start | bytes 147460
  394.1 8.0 %copy-start.9 = (f32[256,16]{0,1:T(8,128)S(1)}, f32[256,16]{0,1:T(8,128)}, u32[]{:S(2)}) copy-start(f32[256,16]{0,1:T(8,128)} %param.29) | copy-start | bytes 49156
  394.1 8.0 %copy-start.10 = (f32[256,16]{0,1:T(8,128)S(1)}, f32[256,16]{0,1:T(8,128)}, u32[]{:S(2)}) copy-start(f32[256,16]{0,1:T(8,128)} %param.28) | copy-start | bytes 49156
  394.1 8.6 %copy-start.11 = (f32[256,16]{0,1:T(8,128)S(1)}, f32[256,16]{0,1:T(8,128)}, u32[]{:S(2)}) copy-start(f32[256,16]{0,1:T(8,128)} %param.27) | copy-start | bytes 49156
  394.1 9.2 %copy-start.6 = (bf16[256,1024]{1,0:T(8,128)(2,1)S(1)}, bf16[256,1024]{1,0:T(8,128)(2,1)}, u32[]{:S(2)}) copy-start(bf16[256,1024]{1,0:T(8,128)(2,1)} %get-tuple-element.90) | copy-start | bytes 1572868
  404.8 1.3 copy-start.4
  406.1 1.6 copy-start.5
